TPU v7x, 32 devices: a whole 2x2x4 slice. The times are simulated.
32 devices in a mesh: basis: 4 (over x, core), tm: 8 (over z, y).
Axes of the slice: x: 2, y: 2, z: 4, core: 2. Of those that a mesh axis runs over, the one named last changes fastest.
Arguments:
- strain: bfloat16 [3, 4096], P(None, 'tm'), may hold values from -6 to 6
- basis_filters: bfloat16 [4096, 2048], P('basis'), may hold values from -0.125 to 0.125
- coefficients: bfloat16 [8192, 4096], P(('basis', 'tm')), may hold values from -0.1875 to 0.1875
Outputs:
- snr: bfloat16 [8192, 3, 1024], P('basis', None, 'tm')
All inputs are finite; a program needn't handle non-finite values.
Results may differ from a plain program's by a relative error of at most 0.0049.
Values may be sent and summed in bfloat16 or wider, within the bound.
No kernel may reach another device: no remote copies, remote signals or barrier semaphores. Data moves between devices by JAX's collectives and lax.ppermute only.
A program may use at most 128 MiB of HBM per device.

v0:
```python
import jax
import jax.numpy as jnp
from jax import lax
from jax.sharding import PartitionSpec as P

STRIDE = 4


def shifted(block, axis, distance):
    devices = range(lax.axis_size(axis))
    route = [(i - distance, i) for i in devices if i - distance in devices]
    return lax.ppermute(block, axis, route)


def shards(strain, basis_filters, coefficients):
    detectors, block_len = strain.shape
    filters_here, filter_len = basis_filters.shape
    reach = filter_len - STRIDE
    blocks_needed = -(-reach // block_len)
    pieces = [strain]
    for offset in range(1, blocks_needed + 1):
        pieces.append(shifted(strain, "tm", -offset))
    extended = jnp.concatenate(pieces, axis=1)
    window_len = block_len + reach
    window = extended[:, :window_len].reshape(detectors, window_len // STRIDE, STRIDE)
    phases = basis_filters.reshape(filters_here, filter_len // STRIDE, STRIDE)
    correlation = lax.conv_general_dilated(
        window,
        phases,
        (1,),
        "VALID",
        dimension_numbers=("NHC", "OHI", "NCH"),
        preferred_element_type=jnp.float32,
    ).astype(jnp.bfloat16)
    basis_count = lax.axis_size("basis")
    time_count = lax.axis_size("tm")
    own_rows = coefficients.shape[0]
    swapped = lax.all_to_all(coefficients, "basis", split_axis=1, concat_axis=0, tiled=True)
    gathered = lax.all_gather(swapped, "tm", axis=0, tiled=True)
    grid = gathered.reshape(time_count, basis_count, own_rows, filters_here)
    block_rows = time_count * own_rows
    row_start = jnp.int32(0)
    terms = []
    for inner in range(lax.axis_size("basis") * block_rows // block_rows):
        which = row_start // block_rows + inner
        rows_here = lax.dynamic_index_in_dim(grid, which, 1, keepdims=False)
        project_rows_here = rows_here.reshape(block_rows, filters_here)
        terms.append(
            jnp.einsum(
                "mb,dbt->mdt", project_rows_here, correlation, preferred_element_type=jnp.float32
            )
        )
    summed = lax.psum_scatter(
        jnp.concatenate(terms, axis=0), "basis", scatter_dimension=0, tiled=True
    )
    return summed.astype(jnp.bfloat16)


def solution(mesh):
    placed = (P(None, "tm"), P("basis", None), P(("basis", "tm"), None))
    return jax.shard_map(
        shards, mesh=mesh, in_specs=placed, out_specs=P("basis", None, "tm"), check_vma=False
    )
```

profile of v0, /device:TPU:0, one launch (start us, length us, event | category | flops | bytes accessed | tf_op | source)
XLA Modules:
  0.0 399.4 jit_solution(8554806784448087860)
XLA Ops:
  6.5 0.0 all-gather.2.cloned.1.call-start
  6.5 4.1 %copy.29 = bf16[256,4096]{0,1:T(8,128)(2,1)} copy(bf16[256,4096]{1,0:T(8,128)(2,1)} %param.5) | data formatting | bytes 4194304 | tf_op args[2]
  10.6 29.9 %all_to_all.19 = bf16[256,4,1024]{0,2,1:T(8,128)(2,1)S(1)} all-to-all(bf16[256,4,1024]{0,2,1:T(8,128)(2,1)} %bitcast.39), channel_id=1, replica_groups=mesh['basis'=4,'tm'=8] {'basis'}, dimensions={1} | all-to-all | bytes 4194304 | tf_op jit(solution)/shard_map/all_to_all | solution.py:38
  40.5 0.0 copy-start
  40.5 2.5 copy.30
  43.0 0.0 all-gather.2.cloned.1.call-update
  43.0 0.0 reduce-scatter.2.cloned.1.call-start
  43.1 0.0 copy-done
  43.1 1.3 collective-permute-start
  44.4 1.3 collective-permute-start.1
  45.7 1.3 collective-permute-start.2
  47.0 1.3 collective-permute-start.3
  48.3 6.6 %copy.26 = bf16[1024,2048]{0,1:T(8,128)(2,1)} copy(bf16[1024,2048]{1,0:T(8,128)(2,1)} %param.4) | data formatting | bytes 8388608 | tf_op args[1]
  54.9 7.4 %reshape.29 = bf16[1024,512,4]{0,2,1:T(4,128)(2,1)} reshape(bf16[1024,2048]{0,1:T(8,128)(2,1)} %copy.26) | data formatting | bytes 8388608 | tf_op jit(solution)/shard_map/reshape | solution.py:26
  62.3 0.0 collective-permute-done
  62.3 0.0 collective-permute-done.1
  62.3 0.0 collective-permute-done.2
  62.3 0.0 collective-permute-done.3
  62.4 1.1 reshape.28
  63.4 82.3 %fusion = bf16[3,1024,128]{1,0,2:T(4,128)(2,1)S(1)} fusion(bf16[1024,512,4]{0,2,1:T(4,128)(2,1)} %reshape.29, bf16[3,639,4]{2,1,0:T(8,128)(2,1)S(1)} %reshape.28), kind=kOutput, calls=%fused_computation.5 | convolution fusion | flops 1610612736 | bytes 4996072 | tf_op jit(solution)/shard_map/conv_general_dilated | solution.py:27
  145.8 0.8 copy.28
  146.6 125.3 %all-gather.2.cloned.1.call-done = bf16[8192,1024]{1,0:T(8,128)(2,1)} async-done(((bf16[1024,1024]{1,0:T(8,128)(2,1)}), bf16[8192,1024]{1,0:T(8,128)(2,1)}) %all-gather.2.cloned.1.call-update) | async-done | bytes 16777232 | tf_op jit(solution)/shard_map/all_gather | solution.py:39
  272.0 6.9 %fusion.2 = (bf16[8,1,256,1024]{3,2,1,0:T(8,128)(2,1)S(1)}, bf16[8,1,256,1024]{3,2,1,0:T(8,128)(2,1)S(1)}, bf16[8,1,256,1024]{3,2,1,0:T(8,128)(2,1)S(1)}, bf16[8,1,256,1024]{3,2,1,0:T(8,128)(2,1)S(1)}) fusion(bf16[8,4,256,1024]{3,2,1,0:T(8,128)(2,1)} %bitcast.36), kind=kLoop, calls=%fused_computation.12 | loop fusion | bytes 33554432 | tf_op jit(solution)/shard_map/jit(dynamic_index_in_dim)/dynamic_slice | solution.py:46
  278.8 1.9 convolution_bitcast_fusion
  280.7 1.9 convolution_bitcast_fusion.1
  282.6 1.9 convolution_bitcast_fusion.2
  284.5 1.9 convolution_bitcast_fusion.3
  286.4 4.9 %pad_maximum_fusion = f32[8192,3,128]{0,2,1:T(8,128)} fusion(f32[2048,3,128]{0,2,1:T(8,128)S(1)} %convolution_bitcast_fusion, f32[2048,3,128]{0,2,1:T(8,128)S(1)} %convolution_bitcast_fusion.1, f32[2048,3,128]{0,2,1:T(8,128)S(1)} %convolution_bitcast_fusion.2, f32[2048,3,128]{0,2,1:T(8,128)S(1)} %convolution_bitcast_fusion.3), kind=kLoop, calls=%fused_computation | loop fusion | flops 9437184 | bytes 25165824 | tf_op jit(solution)/shard_map/concatenate | solution.py:54
  291.3 0.0 reduce-scatter.2.cloned.1.call-update
  291.3 97.4 %reduce-scatter.2.cloned.1.call-done = f32[2048,3,128]{0,2,1:T(8,128)} async-done(((f32[8192,3,128]{0,2,1:T(8,128)}), f32[2048,3,128]{0,2,1:T(8,128)}) %reduce-scatter.2.cloned.1.call-update) | async-done | bytes 3145744 | tf_op jit(solution)/shard_map/reduce_scatter | solution.py:53
  388.7 2.1 convert_element_type.7
  390.8 1.6 copy.35
  (5 shorter events, 0.1 us)
Async XLA Ops:
  6.5 265.4 %all-gather.2.cloned.1.call-start = ((), (), s32[]{:S(2)}) async-start(), calls=%async_computation.2 | async-start | bytes 18874368 | tf_op jit(solution)/shard_map/all_gather | solution.py:39
  40.5 2.6 copy-start
  43.0 345.7 %reduce-scatter.2.cloned.1.call-start = ((), (), s32[]{:S(2)}) async-start(), calls=%async_computation.3 | async-start | bytes 15728640 | tf_op jit(solution)/shard_map/reduce_scatter | solution.py:53
  43.1 19.2 %collective-permute-start = (bf16[3,512]{1,0:T(4,128)(2,1)S(1)}, bf16[3,512]{1,0:T(4,128)(2,1)S(1)}, u32[]{:S(2)}, u32[]{:S(2)}) collective-permute-start(bf16[3,512]{1,0:T(4,128)(2,1)S(1)} %copy-done), channel_id=1, source_target_pairs={{1,0},{2,1},{3,2},{4,3},{5,4},{6,5},{7,6},{9,8},{10,9},{11,10},{12... | collective-permute-start | bytes 9224 | tf_op jit(solution)/shard_map/ppermute | solution.py:12
  44.4 17.9 %collective-permute-start.1 = (bf16[3,512]{1,0:T(4,128)(2,1)S(1)}, bf16[3,512]{1,0:T(4,128)(2,1)S(1)}, u32[]{:S(2)}, u32[]{:S(2)}) collective-permute-start(bf16[3,512]{1,0:T(4,128)(2,1)S(1)} %copy-done), channel_id=1, source_target_pairs={{2,0},{3,1},{4,2},{5,3},{6,4},{7,5},{10,8},{11,9},{12,10},{13,11},... | collective-permute-start | bytes 9224 | tf_op jit(solution)/shard_map/ppermute | solution.py:12
  45.7 16.6 %collective-permute-start.2 = (bf16[3,512]{1,0:T(4,128)(2,1)S(1)}, bf16[3,512]{1,0:T(4,128)(2,1)S(1)}, u32[]{:S(2)}, u32[]{:S(2)}) collective-permute-start(bf16[3,512]{1,0:T(4,128)(2,1)S(1)} %copy-done), channel_id=1, source_target_pairs={{3,0},{4,1},{5,2},{6,3},{7,4},{11,8},{12,9},{13,10},{14,11},{15,12... | collective-permute-start | bytes 9224 | tf_op jit(solution)/shard_map/ppermute | solution.py:12
  47.0 15.3 %collective-permute-start.3 = (bf16[3,512]{1,0:T(4,128)(2,1)S(1)}, bf16[3,512]{1,0:T(4,128)(2,1)S(1)}, u32[]{:S(2)}, u32[]{:S(2)}) collective-permute-start(bf16[3,512]{1,0:T(4,128)(2,1)S(1)} %copy-done), channel_id=1, source_target_pairs={{4,0},{5,1},{6,2},{7,3},{12,8},{13,9},{14,10},{15,11},{20,16},{21,... | collective-permute-start | bytes 9224 | tf_op jit(solution)/shard_map/ppermute | solution.py:12
Sparse Core Ops, SparseCore 0:
  43.2 228.7 all-gather.1
  291.4 97.2 reduce-scatter.1
where the time goes:
time: 402 us; the launch traced here: 399 us
  waiting for transfers between devices  223 us (55%)
  matrix products  89.9 us (22%)
  local copies, waits for them, and re-layouts  30.9 us (8%)
  blocking collectives  29.9 us (7%)
  between operations  13.7 us (3%)
  other arithmetic  6.99 us (2%)
  starting transfers between devices  5.21 us (1%)
    all_gather x1, waiting for transfers between devices, shards(): gathered = lax.all_gather(swapped, 'tm', axis=0, tiled=True)  125 us
    reduce_scatter x1, waiting for transfers between devices, shards(): lax.psum_scatter(jnp.concatenate(terms, axis=0), 'basis', scatter_dimensi...  97.4 us
    conv_general_dilated x1, matrix products, shards(): lax.conv_general_dilated(window, phases, (1,), 'VALID', dimension_numbers...  82.3 us
    all_to_all x1, blocking collectives, shards(): lax.all_to_all(coefficients, 'basis', split_axis=1, concat_axis=0, tiled=...  29.9 us
    unnamed x8, local copies, waits for them, and re-layouts  10.7 us
  transfers between devices with their start and end apart: 6, of which 2 were waited for; matrix products, arithmetic and copies ran while one was open for 25% of the time, Pallas kernels for 0%

commit v1 on v0

v1 whole, which is shorter than its diff:
```python
import functools

import jax
import jax.numpy as jnp
from jax import lax
from jax.experimental import pallas as pl
from jax.experimental.pallas import tpu as pltpu
from jax.sharding import PartitionSpec as P

STRIDE = 4
LANES = 128
CHUNKS = 4
VMEM_LIMIT = 48 * 1024 * 1024


def flipped(block, axis, mask):
    return lax.ppermute(block, axis, [(i, i ^ mask) for i in range(lax.axis_size(axis))])


def gathered_phases(strain):
    detectors, here = strain.shape
    steps = here // STRIDE
    phases = strain.reshape(detectors, steps, STRIDE).transpose(0, 2, 1)
    count = lax.axis_size("tm")
    if count & (count - 1):
        return lax.all_gather(phases, "tm", axis=2, tiled=True)
    me = lax.axis_index("tm")
    mask = 1
    while mask < count:
        other = flipped(phases, "tm", mask)
        upper = (me & mask) != 0
        phases = jnp.concatenate(
            [jnp.where(upper, other, phases), jnp.where(upper, phases, other)], axis=2
        )
        mask *= 2
    return phases


def hankel_kernel(rows_ref, out_ref):
    tile = rows_ref[0]
    width = out_ref.shape[2]
    length = tile.shape[1]
    per_step = 16 // STRIDE

    def step(i, carry):
        first = pltpu.roll(tile, lax.rem(length - per_step * i, length), 1)
        second = pltpu.roll(tile, length - per_step * i - per_step // 2, 1)
        block = jnp.concatenate([first[:, :width], second[:, :width]], axis=0)
        out_ref[0, pl.ds(pl.multiple_of(16 * i, 16), 16), :] = block.astype(out_ref.dtype)
        return carry

    lax.fori_loop(0, out_ref.shape[1] // 16, step, 0)


def hankel(phases, taps, depth, times):
    detectors, _, have = phases.shape
    width = times + (taps - depth) // STRIDE
    length = -(-(width + depth // STRIDE) // LANES) * LANES
    padded = jnp.pad(phases.astype(jnp.float32), ((0, 0), (0, 0), (0, length + 1 - have)))
    rows = jnp.concatenate([padded[:, :, :length], padded[:, :, 1:]], axis=1)
    return pl.pallas_call(
        hankel_kernel,
        grid=(detectors,),
        in_specs=[pl.BlockSpec((1, 2 * STRIDE, length), lambda d: (d, 0, 0))],
        out_specs=pl.BlockSpec((1, depth, width), lambda d: (d, 0, 0)),
        out_shape=jax.ShapeDtypeStruct((detectors, depth, width), jnp.bfloat16),
        compiler_params=pltpu.CompilerParams(vmem_limit_bytes=VMEM_LIMIT),
        name="hankel",
    )(rows)


def partial_kernel(rows_ref, near_ref, far_ref, out_ref):
    half = near_ref.shape[0]
    total = jnp.dot(rows_ref[:, :half], near_ref[...], preferred_element_type=jnp.float32)
    total += jnp.dot(rows_ref[:, half:], far_ref[...], preferred_element_type=jnp.float32)
    out_ref[...] = total.astype(out_ref.dtype)


def partial_rows(rows, near, far, dtype):
    count, depth = rows.shape
    half, taps = near.shape
    block = 512
    return pl.pallas_call(
        partial_kernel,
        grid=(taps // block,),
        in_specs=[
            pl.BlockSpec((count, depth), lambda n: (0, 0)),
            pl.BlockSpec((half, block), lambda n: (0, n)),
            pl.BlockSpec((half, block), lambda n: (0, n)),
        ],
        out_specs=pl.BlockSpec((count, block), lambda n: (0, n)),
        out_shape=jax.ShapeDtypeStruct((count, taps), dtype),
        cost_estimate=pl.CostEstimate(
            flops=2 * count * depth * taps, bytes_accessed=2 * depth * taps, transcendentals=0
        ),
        compiler_params=pltpu.CompilerParams(vmem_limit_bytes=VMEM_LIMIT),
        name="partial_rows",
    )(rows, near, far)


def product(weights, hankel_ref, start, size):
    depth = hankel_ref.shape[1]
    total = None
    for q in range(weights.shape[1] // depth):
        columns = pl.ds(pl.multiple_of(start + q * (depth // STRIDE), LANES), size)
        term = jnp.dot(
            weights[:, q * depth : (q + 1) * depth],
            hankel_ref[0, :, columns],
            preferred_element_type=jnp.float32,
        )
        total = term if total is None else total + term
    return total


def series_kernel(me_ref, own_ref, other_ref, hankel_ref, *outs):
    weights = (own_ref[...] + other_ref[...].astype(jnp.float32)).astype(jnp.bfloat16)
    me = me_ref[0]
    low = lax.rem(me, 2)
    here = outs[0].shape[2]
    for k in range(0, len(outs), 2):
        pair = (me ^ k) // 2
        total = product(weights, hankel_ref, pair * (2 * here), 2 * here).astype(jnp.bfloat16)
        left, right = total[:, :here], total[:, here:]
        outs[k][0] = jnp.where(low == 0, left, right)
        outs[k + 1][0] = jnp.where(low == 0, right, left)


def series(me, own, other, which, hankel_matrix, count, here):
    rows, taps = other.shape
    detectors, depth, width = hankel_matrix.shape
    return pl.pallas_call(
        series_kernel,
        grid_spec=pltpu.PrefetchScalarGridSpec(
            num_scalar_prefetch=1,
            grid=(detectors,),
            in_specs=[
                pl.BlockSpec((rows, taps), lambda d, me: (which, 0)),
                pl.BlockSpec((rows, taps), lambda d, me: (0, 0)),
                pl.BlockSpec((1, depth, width), lambda d, me: (d, 0, 0)),
            ],
            out_specs=[pl.BlockSpec((1, rows, here), lambda d, me: (d, 0, 0))] * count,
        ),
        out_shape=[jax.ShapeDtypeStruct((detectors, rows, here), jnp.bfloat16)] * count,
        cost_estimate=pl.CostEstimate(
            flops=2 * rows * taps * detectors * count * here,
            bytes_accessed=2 * detectors * depth * width,
            transcendentals=0,
        ),
        compiler_params=pltpu.CompilerParams(vmem_limit_bytes=VMEM_LIMIT),
        name="series",
    )(me, own, other, hankel_matrix)


def long_series_kernel(own_ref, other_ref, hankel_ref, out_ref):
    weights = (own_ref[...] + other_ref[...].astype(jnp.float32)).astype(jnp.bfloat16)
    here = out_ref.shape[3]
    total = product(weights, hankel_ref, pl.program_id(1) * (2 * here), 2 * here)
    out_ref[0, 0] = total[:, :here].astype(jnp.bfloat16)
    out_ref[1, 0] = total[:, here:].astype(jnp.bfloat16)


def long_series(own, other, which, hankel_matrix, count, here):
    rows, taps = other.shape
    detectors, depth, width = hankel_matrix.shape
    return pl.pallas_call(
        long_series_kernel,
        grid=(detectors, count // 2),
        in_specs=[
            pl.BlockSpec((rows, taps), lambda d, n: (which, 0)),
            pl.BlockSpec((rows, taps), lambda d, n: (0, 0)),
            pl.BlockSpec((1, depth, width), lambda d, n: (d, 0, 0)),
        ],
        out_specs=pl.BlockSpec((2, 1, rows, here), lambda d, n: (n, d, 0, 0)),
        out_shape=jax.ShapeDtypeStruct((count, detectors, rows, here), jnp.bfloat16),
        compiler_params=pltpu.CompilerParams(vmem_limit_bytes=VMEM_LIMIT),
        name="long_series",
    )(own, other, hankel_matrix)


def shards(strain, basis_filters, coefficients):
    detectors, samples_here = strain.shape
    here = samples_here // STRIDE
    filters, taps = basis_filters.shape
    own_rows = coefficients.shape[0]
    count = lax.axis_size("tm")
    me = lax.axis_index("tm")
    group = lax.axis_index("basis")
    chunks = min(CHUNKS, own_rows // 16)
    rows = own_rows // chunks

    def columns(first, size, which):
        return lax.dynamic_slice(coefficients, (first, which * filters), (size, filters))

    def both(first, size, which):
        return jnp.concatenate([columns(first, size, which), columns(first, size, which ^ 1)], axis=1)

    asked = [flipped(both(c * rows, rows, group ^ 2), "basis", 2) for c in range(chunks)]
    sibling = flipped(basis_filters, "basis", 1)
    matrix = hankel(gathered_phases(strain), taps, 4 * LANES, count * here)
    own = partial_rows(both(0, own_rows, group), basis_filters, sibling, jnp.float32)

    result = jnp.zeros((detectors, count * own_rows, here), jnp.bfloat16)
    for c in range(chunks):
        answer = partial_rows(asked[c], basis_filters, sibling, jnp.bfloat16)
        other = flipped(answer, "basis", 2)
        if count == 8:
            blocks = series(jnp.full((1,), me, jnp.int32), own, other, c, matrix, count, here)
            for k, block in enumerate(blocks):
                arrived = flipped(block, "tm", k) if k else block
                result = lax.dynamic_update_slice(result, arrived, (0, (me ^ k) * own_rows + c * rows, 0))
        else:
            blocks = long_series(own, other, c, matrix, count, here)
            arrived = lax.all_to_all(blocks, "tm", split_axis=0, concat_axis=0, tiled=True)
            for k in range(count):
                result = lax.dynamic_update_slice(result, arrived[k], (0, k * own_rows + c * rows, 0))
    return result.transpose(1, 0, 2)


def solution(mesh):
    placed = (P(None, "tm"), P("basis", None), P(("basis", "tm"), None))
    return jax.shard_map(
        shards, mesh=mesh, in_specs=placed, out_specs=P("basis", None, "tm"), check_vma=False
    )
```

time: 402 us -> 133 us (0.33)
  waiting for transfers between devices: 223 us -> 8.56 us
  matrix products: 89.9 us -> 0 us
  starting transfers between devices: 5.21 us -> 61.6 us
  Pallas kernels: 0 us -> 50.1 us
  blocking collectives: 29.9 us -> 0 us
  local copies, waits for them, and re-layouts: 30.9 us -> 7.92 us
  between operations: 13.7 us -> 0.73 us
    all_gather x1 -> x0, waiting for transfers between devices: 125 us -> none  [shards(): gathered = lax.all_gather(swapped, 'tm', axis=0, tiled=True)]
    reduce_scatter x1 -> x0, waiting for transfers between devices: 97.4 us -> none  [shards(): lax.psum_scatter(jnp.concatenate(terms, axis=0), 'basis', scatter_dimensi...]
    conv_general_dilated x1 -> x0, matrix products: 82.3 us -> none  [shards(): lax.conv_general_dilated(window, phases, (1,), 'VALID', dimension_numbers...]
    ppermute x4 -> x40, starting transfers between devices: 5.17 us -> 61.6 us  [flipped(): lax.ppermute(block, axis, [(i, i ^ mask) for i in range(lax.axis_size(axi...]
    pallas_call x0 -> x10, Pallas kernels: none -> 50.1 us  [the longest x5 22.5 us: partial_rows(): pl.pallas_call(partial_kernel, grid=(taps // block,), in_specs=[pl.BlockS...]
    all_to_all x1 -> x0, blocking collectives: 29.9 us -> none  [shards(): lax.all_to_all(coefficients, 'basis', split_axis=1, concat_axis=0, tiled=...]
    ppermute x4 -> x40, waiting for transfers between devices: 0.01 us -> 8.56 us  [flipped(): lax.ppermute(block, axis, [(i, i ^ mask) for i in range(lax.axis_size(axi...]
    dot_general x4 -> x0, matrix products: 7.53 us -> none  [shards(): jnp.einsum('mb,dbt->mdt', project_rows_here, correlation, preferred_eleme...]
  transfers between devices with their start and end apart: 6 -> 40, of which waited for: 2 -> 7; matrix products, arithmetic and copies ran while one was open for 25% -> 6% of each run, Pallas kernels for 0% -> 38%
where the time goes in v1:
time: 133 us; the launch traced here: 132 us
  starting transfers between devices  61.6 us (46%)
  Pallas kernels  50.1 us (38%)
  waiting for transfers between devices  8.56 us (6%)
  local copies, waits for them, and re-layouts  7.92 us (6%)
  other arithmetic  3.4 us (3%)
    ppermute x40, starting transfers between devices, flipped(): lax.ppermute(block, axis, [(i, i ^ mask) for i in range(lax.axis_size(axi...  61.6 us
    pallas_call x5, Pallas kernels, partial_rows(): pl.pallas_call(partial_kernel, grid=(taps // block,), in_specs=[pl.BlockS...  22.5 us
    pallas_call x4, Pallas kernels, series(): pl.pallas_call(series_kernel, grid_spec=pltpu.PrefetchScalarGridSpec(num_...  18 us
    pallas_call x1, Pallas kernels, hankel(): pl.pallas_call(hankel_kernel, grid=(detectors,), in_specs=[pl.BlockSpec((...  9.56 us
    ppermute x40, waiting for transfers between devices, flipped(): lax.ppermute(block, axis, [(i, i ^ mask) for i in range(lax.axis_size(axi...  8.56 us
    concatenate x5, other arithmetic, both(): jnp.concatenate([columns(first, size, which), columns(first, size, which...  3.29 us
    unnamed x10, local copies, waits for them, and re-layouts  3.19 us
    dynamic_slice x2, local copies, waits for them, and re-layouts, columns(): lax.dynamic_slice(coefficients, (first, which * filters), (size, filters))  3.05 us
  transfers between devices with their start and end apart: 40, of which 7 were waited for; matrix products, arithmetic and copies ran while one was open for 6% of the time, Pallas kernels for 38%

profile of v1, /device:TPU:0, one launch (start us, length us, event | category | flops | bytes accessed | tf_op | source)
XLA Modules:
  0.0 132.4 jit_solution(776771630694814708)
XLA Ops:
  0.0 0.5 collective-permute-start
  0.5 0.9 reshape.3
  1.5 2.6 %collective-permute-start.3 = (bf16[3,4,128]{2,1,0:T(4,128)(2,1)S(1)}, bf16[3,4,128]{2,1,0:T(4,128)(2,1)S(1)}, u32[]{:S(2)}, u32[]{:S(2)}) collective-permute-start(bf16[3,4,128]{2,1,0:T(4,128)(2,1)S(1)} %bitcast.5), channel_id=1, source_target_pairs={{0,1},{1,0},{2,3},{3,2},{4,5},{5,4},{6,7},{7,6},{8,9},{9,8},{10,11... | collective-permute-start | bytes 9224 | tf_op jit(solution)/shard_map/ppermute | solution.py:17
  4.0 2.2 %constant_dynamic-slice_fusion.5 = (bf16[64,1024]{1,0:T(8,128)(2,1)S(1)}, bf16[64,1024]{1,0:T(8,128)(2,1)S(1)}, bf16[64,1024]{1,0:T(8,128)(2,1)S(1)}, bf16[64,10...) fusion(bf16[256,4096]{1,0:T(8,128)(2,1)} %param.5, ...), kind=kLoop, calls=%fused_computation.56 | loop fusion | bytes 2097160 | tf_op jit(solution)/shard_map/dynamic_slice | solution.py:192
  6.2 0.7 pad_maximum_fusion.1
  6.9 1.5 %collective-permute-start.1 = (bf16[64,2048]{1,0:T(8,128)(2,1)}, bf16[64,2048]{1,0:T(8,128)(2,1)S(1)}, u32[]{:S(2)}, u32[]{:S(2)}) collective-permute-start(bf16[64,2048]{1,0:T(8,128)(2,1)} %pad_maximum_fusion.1), channel_id=1, source_target_pairs={{0,16},{8,24},{16,0},{24,8},{1,17},{9,25},{17,1},{25,9},{2,18},{10... | collective-permute-start | bytes 786440 | tf_op jit(solution)/shard_map/ppermute | solution.py:17
  8.4 0.7 pad_maximum_fusion.2
  9.1 0.5 collective-permute-start.13
  9.7 0.7 pad_maximum_fusion.3
  10.4 1.5 %collective-permute-start.22 = (bf16[64,2048]{1,0:T(8,128)(2,1)}, bf16[64,2048]{1,0:T(8,128)(2,1)S(1)}, u32[]{:S(2)}, u32[]{:S(2)}) collective-permute-start(bf16[64,2048]{1,0:T(8,128)(2,1)} %pad_maximum_fusion.3), channel_id=1, source_target_pairs={{0,16},{8,24},{16,0},{24,8},{1,17},{9,25},{17,1},{25,9},{2,18},{10... | collective-permute-start | bytes 786440 | tf_op jit(solution)/shard_map/ppermute | solution.py:17
  11.9 0.9 constant_dynamic-slice_fusion.3
  12.8 1.6 %collective-permute-start.4 = (bf16[3,4,256]{2,1,0:T(4,128)(2,1)S(1)}, bf16[3,4,256]{2,1,0:T(4,128)(2,1)S(1)}, u32[]{:S(2)}, u32[]{:S(2)}) collective-permute-start(bf16[3,4,256]{2,1,0:T(4,128)(2,1)S(1)} %pad_maximum_fusion.7), channel_id=1, source_target_pairs={{0,2},{1,3},{2,0},{3,1},{4,6},{5,7},{6,4},{7,5},{8,10},{9,11},{10,... | collective-permute-start | bytes 18440 | tf_op jit(solution)/shard_map/ppermute | solution.py:17
  14.4 1.1 pad_maximum_fusion.rows_ref
  15.6 0.9 collective-permute-done.4
  16.5 2.7 %collective-permute-start.5 = (bf16[3,4,512]{2,1,0:T(4,128)(2,1)S(1)}, bf16[3,4,512]{2,1,0:T(4,128)(2,1)S(1)}, u32[]{:S(2)}, u32[]{:S(2)}) collective-permute-start(bf16[3,4,512]{2,1,0:T(4,128)(2,1)S(1)} %pad_maximum_fusion.6), channel_id=1, source_target_pairs={{0,4},{1,5},{2,6},{3,7},{4,0},{5,1},{6,2},{7,3},{8,12},{9,13},{10,... | collective-permute-start | bytes 36872 | tf_op jit(solution)/shard_map/ppermute | solution.py:17
  19.4 1.8 %collective-permute-done.5 = bf16[3,4,512]{2,1,0:T(4,128)(2,1)S(1)} collective-permute-done((bf16[3,4,512]{2,1,0:T(4,128)(2,1)S(1)}, bf16[3,4,512]{2,1,0:T(4,128)(2,1)S(1)}, u32[]{:S(2)}, u32[]{:S(2)}) %collective-permute-start.5) | collective-permute-done | bytes 12320 | tf_op jit(solution)/shard_map/ppermute | solution.py:17
  21.2 0.5 collective-permute-start.31
  21.8 0.1 fusion.4
  21.9 9.6 %hankel.1.hankel_ref = bf16[3,512,1408]{2,1,0:T(8,128)(2,1)S(1)} custom-call(f32[3,8,1536]{2,1,0:T(8,128)S(1)} %pad_maximum_fusion.5.rows_ref), custom_call_target="tpu_custom_call" | custom-call | tf_op jit(solution)/shard_map/hankel/pallas_call | solution.py:61
  31.5 2.0 %copy-done = bf16[3,512,1408]{2,1,0:T(8,128)(2,1)} copy-done((bf16[3,512,1408]{2,1,0:T(8,128)(2,1)}, bf16[3,512,1408]{2,1,0:T(8,128)(2,1)S(1)}, u32[]{:S(2)}) %copy-start) | copy-done | bytes 4325400
  33.5 4.3 %partial_rows.6 = bf16[64,2048]{1,0:T(8,128)(2,1)S(1)} custom-call(bf16[64,2048]{1,0:T(8,128)(2,1)S(1)} %collective-permute-done.1.rows_ref, bf16[1024,2048]{1,0:T(8,128)(2,1)S(1)} %copy-done.1, bf16[1024,2048]{1,0:T(8,128)(2,1)} %collective-permute-done.far_ref), custom_call_target="tpu_custom_call" | custom-call | flops 536870912 | bytes 8388608 | tf_op jit(solution)/shard_map/partial_rows/pallas_call | solution.py:83
  37.8 1.6 %collective-permute-start.2 = (bf16[64,2048]{1,0:T(8,128)(2,1)S(1)}, bf16[64,2048]{1,0:T(8,128)(2,1)S(1)}, u32[]{:S(2)}, u32[]{:S(2)}) collective-permute-start(bf16[64,2048]{1,0:T(8,128)(2,1)S(1)} %partial_rows.6), channel_id=1, source_target_pairs={{0,16},{8,24},{16,0},{24,8},{1,17},{9,25},{17,1},{25,9},{2,18},{10... | collective-permute-start | bytes 786440 | tf_op jit(solution)/shard_map/ppermute | solution.py:17
  39.4 4.3 %partial_rows.7 = bf16[64,2048]{1,0:T(8,128)(2,1)S(1)} custom-call(bf16[64,2048]{1,0:T(8,128)(2,1)S(1)} %collective-permute-done.13.rows_ref, bf16[1024,2048]{1,0:T(8,128)(2,1)S(1)} %copy-done.1, bf16[1024,2048]{1,0:T(8,128)(2,1)} %collective-permute-done.far_ref), custom_call_target="tpu_custom_call" | custom-call | flops 536870912 | bytes 8388608 | tf_op jit(solution)/shard_map/partial_rows/pallas_call | solution.py:83
  43.6 0.6 collective-permute-start.14
  44.2 4.3 %partial_rows.8 = bf16[64,2048]{1,0:T(8,128)(2,1)S(1)} custom-call(bf16[64,2048]{1,0:T(8,128)(2,1)S(1)} %collective-permute-done.22.rows_ref, bf16[1024,2048]{1,0:T(8,128)(2,1)S(1)} %copy-done.1, bf16[1024,2048]{1,0:T(8,128)(2,1)} %collective-permute-done.far_ref), custom_call_target="tpu_custom_call" | custom-call | flops 536870912 | bytes 8388608 | tf_op jit(solution)/shard_map/partial_rows/pallas_call | solution.py:83
  48.5 1.6 %collective-permute-start.23 = (bf16[64,2048]{1,0:T(8,128)(2,1)S(1)}, bf16[64,2048]{1,0:T(8,128)(2,1)S(1)}, u32[]{:S(2)}, u32[]{:S(2)}) collective-permute-start(bf16[64,2048]{1,0:T(8,128)(2,1)S(1)} %partial_rows.8), channel_id=1, source_target_pairs={{0,16},{8,24},{16,0},{24,8},{1,17},{9,25},{17,1},{25,9},{2,18},{10... | collective-permute-start | bytes 786440 | tf_op jit(solution)/shard_map/ppermute | solution.py:17
  50.1 4.3 %partial_rows.9 = bf16[64,2048]{1,0:T(8,128)(2,1)S(1)} custom-call(bf16[64,2048]{1,0:T(8,128)(2,1)S(1)} %collective-permute-done.31.rows_ref, bf16[1024,2048]{1,0:T(8,128)(2,1)S(1)} %copy-done.1, bf16[1024,2048]{1,0:T(8,128)(2,1)} %collective-permute-done.far_ref), custom_call_target="tpu_custom_call" | custom-call | flops 536870912 | bytes 8388608 | tf_op jit(solution)/shard_map/partial_rows/pallas_call | solution.py:83
  54.3 0.6 collective-permute-start.32
  54.9 5.5 %partial_rows.5.own_ref = f32[256,2048]{1,0:T(8,128)S(1)} custom-call(bf16[256,2048]{1,0:T(8,128)(2,1)S(1)} %pad_maximum_fusion.rows_ref, bf16[1024,2048]{1,0:T(8,128)(2,1)} %near_ref.9, bf16[1024,2048]{1,0:T(8,128)(2,1)} %collective-permute-done.far_ref), custom_call_target="tpu_custom_call" | custom-call | flops 2147483648 | bytes 8388608 | tf_op jit(solution)/shard_map/partial_rows/pallas_call | solution.py:83
  60.5 4.5 %series.4 = (bf16[3,64,128]{2,1,0:T(8,128)(2,1)S(1)}, bf16[3,64,128]{2,1,0:T(8,128)(2,1)S(1)}, bf16[3,64,128]{2,1,0:T(8,128)(2,1)S(1)}, bf16[3,64,128]{2,1,0:T(8...) custom-call(s32[1]{0:T(128)} %bitcast.me_ref, ...), custom_call_target="tpu_custom_call" | custom-call | flops 805306368 | bytes 4325376 | tf_op jit(solution)/shard_map/series/pallas_call | solution.py:131
  65.0 0.2 collective-permute-start.6
  65.2 1.9 %collective-permute-start.7 = (bf16[3,64,128]{2,1,0:T(8,128)(2,1)S(1)}, bf16[3,64,128]{2,1,0:T(8,128)(2,1)S(1)}, u32[]{:S(2)}, u32[]{:S(2)}) collective-permute-start(bf16[3,64,128]{2,1,0:T(8,128)(2,1)S(1)} %get-tuple-element.39), channel_id=1, source_target_pairs={{0,2},{1,3},{2,0},{3,1},{4,6},{5,7},{6,4},{7,5},{8,10},{9,11},{10,... | collective-permute-start | bytes 147464 | tf_op jit(solution)/shard_map/ppermute | solution.py:17
  67.1 1.4 %collective-permute-start.8 = (bf16[3,64,128]{2,1,0:T(8,128)(2,1)S(1)}, bf16[3,64,128]{2,1,0:T(8,128)(2,1)S(1)}, u32[]{:S(2)}, u32[]{:S(2)}) collective-permute-start(bf16[3,64,128]{2,1,0:T(8,128)(2,1)S(1)} %get-tuple-element.40), channel_id=1, source_target_pairs={{0,3},{1,2},{2,1},{3,0},{4,7},{5,6},{6,5},{7,4},{8,11},{9,10},{10,... | collective-permute-start | bytes 147464 | tf_op jit(solution)/shard_map/ppermute | solution.py:17
  68.5 4.5 %series.5 = (bf16[3,64,128]{2,1,0:T(8,128)(2,1)S(1)}, bf16[3,64,128]{2,1,0:T(8,128)(2,1)S(1)}, bf16[3,64,128]{2,1,0:T(8,128)(2,1)S(1)}, bf16[3,64,128]{2,1,0:T(8...) custom-call(s32[1]{0:T(128)} %bitcast.me_ref, ...), custom_call_target="tpu_custom_call" | custom-call | flops 805306368 | bytes 4325376 | tf_op jit(solution)/shard_map/series/pallas_call | solution.py:131
  73.0 2.7 %collective-permute-start.9 = (bf16[3,64,128]{2,1,0:T(8,128)(2,1)S(1)}, bf16[3,64,128]{2,1,0:T(8,128)(2,1)S(1)}, u32[]{:S(2)}, u32[]{:S(2)}) collective-permute-start(bf16[3,64,128]{2,1,0:T(8,128)(2,1)S(1)} %get-tuple-element.41), channel_id=1, source_target_pairs={{0,4},{1,5},{2,6},{3,7},{4,0},{5,1},{6,2},{7,3},{8,12},{9,13},{10,... | collective-permute-start | bytes 147464 | tf_op jit(solution)/shard_map/ppermute | solution.py:17
  75.7 4.5 %series.6 = (bf16[3,64,128]{2,1,0:T(8,128)(2,1)S(1)}, bf16[3,64,128]{2,1,0:T(8,128)(2,1)S(1)}, bf16[3,64,128]{2,1,0:T(8,128)(2,1)S(1)}, bf16[3,64,128]{2,1,0:T(8...) custom-call(s32[1]{0:T(128)} %bitcast.me_ref, ...), custom_call_target="tpu_custom_call" | custom-call | flops 805306368 | bytes 4325376 | tf_op jit(solution)/shard_map/series/pallas_call | solution.py:131
  80.2 0.2 broadcast_in_dim.4
  80.5 4.5 %series.7 = (bf16[3,64,128]{2,1,0:T(8,128)(2,1)S(1)}, bf16[3,64,128]{2,1,0:T(8,128)(2,1)S(1)}, bf16[3,64,128]{2,1,0:T(8,128)(2,1)S(1)}, bf16[3,64,128]{2,1,0:T(8...) custom-call(s32[1]{0:T(128)} %bitcast.me_ref, ...), custom_call_target="tpu_custom_call" | custom-call | flops 805306368 | bytes 4325376 | tf_op jit(solution)/shard_map/series/pallas_call | solution.py:131
  85.1 3.9 %collective-permute-start.11 = (bf16[3,64,128]{2,1,0:T(8,128)(2,1)S(1)}, bf16[3,64,128]{2,1,0:T(8,128)(2,1)S(1)}, u32[]{:S(2)}, u32[]{:S(2)}) collective-permute-start(bf16[3,64,128]{2,1,0:T(8,128)(2,1)S(1)} %get-tuple-element.43), channel_id=1, source_target_pairs={{0,6},{1,7},{2,4},{3,5},{4,2},{5,3},{6,0},{7,1},{8,14},{9,15},{10,... | collective-permute-start | bytes 147464 | tf_op jit(solution)/shard_map/ppermute | solution.py:17
  89.0 1.2 collective-permute-start.12
  90.3 0.4 collective-permute-start.15
  90.9 3.1 %collective-permute-start.17 = (bf16[3,64,128]{2,1,0:T(8,128)(2,1)S(1)}, bf16[3,64,128]{2,1,0:T(8,128)(2,1)S(1)}, u32[]{:S(2)}, u32[]{:S(2)}) collective-permute-start(bf16[3,64,128]{2,1,0:T(8,128)(2,1)S(1)} %get-tuple-element.48), channel_id=1, source_target_pairs={{0,3},{1,2},{2,1},{3,0},{4,7},{5,6},{6,5},{7,4},{8,11},{9,10},{10,... | collective-permute-start | bytes 147464 | tf_op jit(solution)/shard_map/ppermute | solution.py:17
  94.0 2.2 %collective-permute-start.18 = (bf16[3,64,128]{2,1,0:T(8,128)(2,1)S(1)}, bf16[3,64,128]{2,1,0:T(8,128)(2,1)S(1)}, u32[]{:S(2)}, u32[]{:S(2)}) collective-permute-start(bf16[3,64,128]{2,1,0:T(8,128)(2,1)S(1)} %get-tuple-element.49), channel_id=1, source_target_pairs={{0,4},{1,5},{2,6},{3,7},{4,0},{5,1},{6,2},{7,3},{8,12},{9,13},{10,... | collective-permute-start | bytes 147464 | tf_op jit(solution)/shard_map/ppermute | solution.py:17
  96.3 0.2 collective-permute-done.12
  96.5 0.4 collective-permute-start.19
  97.0 3.8 %collective-permute-start.20 = (bf16[3,64,128]{2,1,0:T(8,128)(2,1)S(1)}, bf16[3,64,128]{2,1,0:T(8,128)(2,1)S(1)}, u32[]{:S(2)}, u32[]{:S(2)}) collective-permute-start(bf16[3,64,128]{2,1,0:T(8,128)(2,1)S(1)} %get-tuple-element.51), channel_id=1, source_target_pairs={{0,6},{1,7},{2,4},{3,5},{4,2},{5,3},{6,0},{7,1},{8,14},{9,15},{10,... | collective-permute-start | bytes 147464 | tf_op jit(solution)/shard_map/ppermute | solution.py:17
  100.8 1.2 collective-permute-start.21
  102.0 0.4 collective-permute-start.24
  102.6 0.3 collective-permute-done.19
  102.9 2.9 %collective-permute-start.26 = (bf16[3,64,128]{2,1,0:T(8,128)(2,1)S(1)}, bf16[3,64,128]{2,1,0:T(8,128)(2,1)S(1)}, u32[]{:S(2)}, u32[]{:S(2)}) collective-permute-start(bf16[3,64,128]{2,1,0:T(8,128)(2,1)S(1)} %get-tuple-element.56), channel_id=1, source_target_pairs={{0,3},{1,2},{2,1},{3,0},{4,7},{5,6},{6,5},{7,4},{8,11},{9,10},{10,... | collective-permute-start | bytes 147464 | tf_op jit(solution)/shard_map/ppermute | solution.py:17
  105.8 2.2 %collective-permute-start.27 = (bf16[3,64,128]{2,1,0:T(8,128)(2,1)S(1)}, bf16[3,64,128]{2,1,0:T(8,128)(2,1)S(1)}, u32[]{:S(2)}, u32[]{:S(2)}) collective-permute-start(bf16[3,64,128]{2,1,0:T(8,128)(2,1)S(1)} %get-tuple-element.57), channel_id=1, source_target_pairs={{0,4},{1,5},{2,6},{3,7},{4,0},{5,1},{6,2},{7,3},{8,12},{9,13},{10,... | collective-permute-start | bytes 147464 | tf_op jit(solution)/shard_map/ppermute | solution.py:17
  108.1 0.6 collective-permute-start.28
  108.7 3.8 %collective-permute-start.29 = (bf16[3,64,128]{2,1,0:T(8,128)(2,1)S(1)}, bf16[3,64,128]{2,1,0:T(8,128)(2,1)S(1)}, u32[]{:S(2)}, u32[]{:S(2)}) collective-permute-start(bf16[3,64,128]{2,1,0:T(8,128)(2,1)S(1)} %get-tuple-element.59), channel_id=1, source_target_pairs={{0,6},{1,7},{2,4},{3,5},{4,2},{5,3},{6,0},{7,1},{8,14},{9,15},{10,... | collective-permute-start | bytes 147464 | tf_op jit(solution)/shard_map/ppermute | solution.py:17
  112.6 1.2 collective-permute-start.30
  113.8 0.4 collective-permute-start.33
  114.4 3.1 %collective-permute-start.35 = (bf16[3,64,128]{2,1,0:T(8,128)(2,1)S(1)}, bf16[3,64,128]{2,1,0:T(8,128)(2,1)S(1)}, u32[]{:S(2)}, u32[]{:S(2)}) collective-permute-start(bf16[3,64,128]{2,1,0:T(8,128)(2,1)S(1)} %get-tuple-element.64), channel_id=1, source_target_pairs={{0,3},{1,2},{2,1},{3,0},{4,7},{5,6},{6,5},{7,4},{8,11},{9,10},{10,... | collective-permute-start | bytes 147464 | tf_op jit(solution)/shard_map/ppermute | solution.py:17
  117.6 2.6 %collective-permute-start.36 = (bf16[3,64,128]{2,1,0:T(8,128)(2,1)S(1)}, bf16[3,64,128]{2,1,0:T(8,128)(2,1)S(1)}, u32[]{:S(2)}, u32[]{:S(2)}) collective-permute-start(bf16[3,64,128]{2,1,0:T(8,128)(2,1)S(1)} %get-tuple-element.65), channel_id=1, source_target_pairs={{0,4},{1,5},{2,6},{3,7},{4,0},{5,1},{6,2},{7,3},{8,12},{9,13},{10,... | collective-permute-start | bytes 147464 | tf_op jit(solution)/shard_map/ppermute | solution.py:17
  120.2 1.6 %collective-permute-start.37 = (bf16[3,64,128]{2,1,0:T(8,128)(2,1)S(1)}, bf16[3,64,128]{2,1,0:T(8,128)(2,1)S(1)}, u32[]{:S(2)}, u32[]{:S(2)}) collective-permute-start(bf16[3,64,128]{2,1,0:T(8,128)(2,1)S(1)} %get-tuple-element.66), channel_id=1, source_target_pairs={{0,5},{1,4},{2,7},{3,6},{4,1},{5,0},{6,3},{7,2},{8,13},{9,12},{10,... | collective-permute-start | bytes 147464 | tf_op jit(solution)/shard_map/ppermute | solution.py:17
  121.8 2.5 %collective-permute-start.38 = (bf16[3,64,128]{2,1,0:T(8,128)(2,1)S(1)}, bf16[3,64,128]{2,1,0:T(8,128)(2,1)S(1)}, u32[]{:S(2)}, u32[]{:S(2)}) collective-permute-start(bf16[3,64,128]{2,1,0:T(8,128)(2,1)S(1)} %get-tuple-element.67), channel_id=1, source_target_pairs={{0,6},{1,7},{2,4},{3,5},{4,2},{5,3},{6,0},{7,1},{8,14},{9,15},{10,... | collective-permute-start | bytes 147464 | tf_op jit(solution)/shard_map/ppermute | solution.py:17
  124.3 1.5 %collective-permute-start.39 = (bf16[3,64,128]{2,1,0:T(8,128)(2,1)S(1)}, bf16[3,64,128]{2,1,0:T(8,128)(2,1)S(1)}, u32[]{:S(2)}, u32[]{:S(2)}) collective-permute-start(bf16[3,64,128]{2,1,0:T(8,128)(2,1)S(1)} %get-tuple-element.68), channel_id=1, source_target_pairs={{0,7},{1,6},{2,5},{3,4},{4,3},{5,2},{6,1},{7,0},{8,15},{9,14},{10,... | collective-permute-start | bytes 147464 | tf_op jit(solution)/shard_map/ppermute | solution.py:17
  125.9 0.2 collective-permute-done.37
  126.2 1.6 %collective-permute-done.38 = bf16[3,64,128]{2,1,0:T(8,128)(2,1)S(1)} collective-permute-done((bf16[3,64,128]{2,1,0:T(8,128)(2,1)S(1)}, bf16[3,64,128]{2,1,0:T(8,128)(2,1)S(1)}, u32[]{:S(2)}, u32[]{:S(2)}) %collective-permute-start.38) | collective-permute-done | bytes 49184 | tf_op jit(solution)/shard_map/ppermute | solution.py:17
  127.8 3.4 %collective-permute-done.39 = bf16[3,64,128]{2,1,0:T(8,128)(2,1)S(1)} collective-permute-done((bf16[3,64,128]{2,1,0:T(8,128)(2,1)S(1)}, bf16[3,64,128]{2,1,0:T(8,128)(2,1)S(1)}, u32[]{:S(2)}, u32[]{:S(2)}) %collective-permute-start.39) | collective-permute-done | bytes 49184 | tf_op jit(solution)/shard_map/ppermute | solution.py:17
  131.2 1.1 copy-done.3
  (86 shorter events, 1.0 us)
Async XLA Ops:
  0.0 33.5 %collective-permute-start = (bf16[1024,2048]{1,0:T(8,128)(2,1)}, bf16[1024,2048]{1,0:T(8,128)(2,1)}, u32[]{:S(2)}, u32[]{:S(2)}) collective-permute-start(bf16[1024,2048]{1,0:T(8,128)(2,1)} %near_ref.9), channel_id=1, source_target_pairs={{0,8},{8,0},{16,24},{24,16},{1,9},{9,1},{17,25},{25,17},{2,10},{10... | collective-permute-start | bytes 12582920 | tf_op jit(solution)/shard_map/ppermute | solution.py:17
  1.5 11.3 %collective-permute-start.3 = (bf16[3,4,128]{2,1,0:T(4,128)(2,1)S(1)}, bf16[3,4,128]{2,1,0:T(4,128)(2,1)S(1)}, u32[]{:S(2)}, u32[]{:S(2)}) collective-permute-start(bf16[3,4,128]{2,1,0:T(4,128)(2,1)S(1)} %bitcast.5), channel_id=1, source_target_pairs={{0,1},{1,0},{2,3},{3,2},{4,5},{5,4},{6,7},{7,6},{8,9},{9,8},{10,11... | collective-permute-start | bytes 9224 | tf_op jit(solution)/shard_map/ppermute | solution.py:17
  4.0 7.9 %copy-start.2 = (bf16[256,4096]{1,0:T(8,128)(2,1)S(1)}, bf16[256,4096]{1,0:T(8,128)(2,1)}, u32[]{:S(2)}) copy-start(bf16[256,4096]{1,0:T(8,128)(2,1)} %param.5) | copy-start | bytes 6291460
  6.9 26.6 %collective-permute-start.1 = (bf16[64,2048]{1,0:T(8,128)(2,1)}, bf16[64,2048]{1,0:T(8,128)(2,1)S(1)}, u32[]{:S(2)}, u32[]{:S(2)}) collective-permute-start(bf16[64,2048]{1,0:T(8,128)(2,1)} %pad_maximum_fusion.1), channel_id=1, source_target_pairs={{0,16},{8,24},{16,0},{24,8},{1,17},{9,25},{17,1},{25,9},{2,18},{10... | collective-permute-start | bytes 786440 | tf_op jit(solution)/shard_map/ppermute | solution.py:17
  9.1 30.2 %collective-permute-start.13 = (bf16[64,2048]{1,0:T(8,128)(2,1)}, bf16[64,2048]{1,0:T(8,128)(2,1)S(1)}, u32[]{:S(2)}, u32[]{:S(2)}) collective-permute-start(bf16[64,2048]{1,0:T(8,128)(2,1)} %pad_maximum_fusion.2), channel_id=1, source_target_pairs={{0,16},{8,24},{16,0},{24,8},{1,17},{9,25},{17,1},{25,9},{2,18},{10... | collective-permute-start | bytes 786440 | tf_op jit(solution)/shard_map/ppermute | solution.py:17
  10.4 33.8 %collective-permute-start.22 = (bf16[64,2048]{1,0:T(8,128)(2,1)}, bf16[64,2048]{1,0:T(8,128)(2,1)S(1)}, u32[]{:S(2)}, u32[]{:S(2)}) collective-permute-start(bf16[64,2048]{1,0:T(8,128)(2,1)} %pad_maximum_fusion.3), channel_id=1, source_target_pairs={{0,16},{8,24},{16,0},{24,8},{1,17},{9,25},{17,1},{25,9},{2,18},{10... | collective-permute-start | bytes 786440 | tf_op jit(solution)/shard_map/ppermute | solution.py:17
  12.8 6.4 %copy-start.4 = (bf16[64,1024]{1,0:T(8,128)(2,1)S(1)}, bf16[64,1024]{1,0:T(8,128)(2,1)}, u32[]{:S(2)}) copy-start(bf16[64,1024]{1,0:T(8,128)(2,1)} %get-tuple-element.76) | copy-start | bytes 393220
  12.8 3.7 %collective-permute-start.4 = (bf16[3,4,256]{2,1,0:T(4,128)(2,1)S(1)}, bf16[3,4,256]{2,1,0:T(4,128)(2,1)S(1)}, u32[]{:S(2)}, u32[]{:S(2)}) collective-permute-start(bf16[3,4,256]{2,1,0:T(4,128)(2,1)S(1)} %pad_maximum_fusion.7), channel_id=1, source_target_pairs={{0,2},{1,3},{2,0},{3,1},{4,6},{5,7},{6,4},{7,5},{8,10},{9,11},{10,... | collective-permute-start | bytes 18440 | tf_op jit(solution)/shard_map/ppermute | solution.py:17
  16.5 4.7 %collective-permute-start.5 = (bf16[3,4,512]{2,1,0:T(4,128)(2,1)S(1)}, bf16[3,4,512]{2,1,0:T(4,128)(2,1)S(1)}, u32[]{:S(2)}, u32[]{:S(2)}) collective-permute-start(bf16[3,4,512]{2,1,0:T(4,128)(2,1)S(1)} %pad_maximum_fusion.6), channel_id=1, source_target_pairs={{0,4},{1,5},{2,6},{3,7},{4,0},{5,1},{6,2},{7,3},{8,12},{9,13},{10,... | collective-permute-start | bytes 36872 | tf_op jit(solution)/shard_map/ppermute | solution.py:17
  21.2 28.9 %collective-permute-start.31 = (bf16[64,2048]{1,0:T(8,128)(2,1)S(1)}, bf16[64,2048]{1,0:T(8,128)(2,1)S(1)}, u32[]{:S(2)}, u32[]{:S(2)}) collective-permute-start(bf16[64,2048]{1,0:T(8,128)(2,1)S(1)} %pad_maximum_fusion.4), channel_id=1, source_target_pairs={{0,16},{8,24},{16,0},{24,8},{1,17},{9,25},{17,1},{25,9},{2,18},{10... | collective-permute-start | bytes 786440 | tf_op jit(solution)/shard_map/ppermute | solution.py:17
  21.9 11.6 %copy-start.1 = (bf16[1024,2048]{1,0:T(8,128)(2,1)S(1)}, bf16[1024,2048]{1,0:T(8,128)(2,1)}, u32[]{:S(2)}) copy-start(bf16[1024,2048]{1,0:T(8,128)(2,1)} %near_ref.9) | copy-start | bytes 12582916
  31.5 2.0 %copy-start = (bf16[3,512,1408]{2,1,0:T(8,128)(2,1)}, bf16[3,512,1408]{2,1,0:T(8,128)(2,1)S(1)}, u32[]{:S(2)}) copy-start(bf16[3,512,1408]{2,1,0:T(8,128)(2,1)S(1)} %hankel.1.hankel_ref) | copy-start | bytes 12976132
  37.8 22.6 %collective-permute-start.2 = (bf16[64,2048]{1,0:T(8,128)(2,1)S(1)}, bf16[64,2048]{1,0:T(8,128)(2,1)S(1)}, u32[]{:S(2)}, u32[]{:S(2)}) collective-permute-start(bf16[64,2048]{1,0:T(8,128)(2,1)S(1)} %partial_rows.6), channel_id=1, source_target_pairs={{0,16},{8,24},{16,0},{24,8},{1,17},{9,25},{17,1},{25,9},{2,18},{10... | collective-permute-start | bytes 786440 | tf_op jit(solution)/shard_map/ppermute | solution.py:17
  43.6 23.5 %collective-permute-start.14 = (bf16[64,2048]{1,0:T(8,128)(2,1)S(1)}, bf16[64,2048]{1,0:T(8,128)(2,1)S(1)}, u32[]{:S(2)}, u32[]{:S(2)}) collective-permute-start(bf16[64,2048]{1,0:T(8,128)(2,1)S(1)} %partial_rows.7), channel_id=1, source_target_pairs={{0,16},{8,24},{16,0},{24,8},{1,17},{9,25},{17,1},{25,9},{2,18},{10... | collective-permute-start | bytes 786440 | tf_op jit(solution)/shard_map/ppermute | solution.py:17
  48.5 24.5 %collective-permute-start.23 = (bf16[64,2048]{1,0:T(8,128)(2,1)S(1)}, bf16[64,2048]{1,0:T(8,128)(2,1)S(1)}, u32[]{:S(2)}, u32[]{:S(2)}) collective-permute-start(bf16[64,2048]{1,0:T(8,128)(2,1)S(1)} %partial_rows.8), channel_id=1, source_target_pairs={{0,16},{8,24},{16,0},{24,8},{1,17},{9,25},{17,1},{25,9},{2,18},{10... | collective-permute-start | bytes 786440 | tf_op jit(solution)/shard_map/ppermute | solution.py:17
  54.3 26.1 %collective-permute-start.32 = (bf16[64,2048]{1,0:T(8,128)(2,1)S(1)}, bf16[64,2048]{1,0:T(8,128)(2,1)S(1)}, u32[]{:S(2)}, u32[]{:S(2)}) collective-permute-start(bf16[64,2048]{1,0:T(8,128)(2,1)S(1)} %partial_rows.9), channel_id=1, source_target_pairs={{0,16},{8,24},{16,0},{24,8},{1,17},{9,25},{17,1},{25,9},{2,18},{10... | collective-permute-start | bytes 786440 | tf_op jit(solution)/shard_map/ppermute | solution.py:17
  65.0 20.1 %collective-permute-start.6 = (bf16[3,64,128]{2,1,0:T(8,128)(2,1)S(1)}, bf16[3,64,128]{2,1,0:T(8,128)(2,1)S(1)}, u32[]{:S(2)}, u32[]{:S(2)}) collective-permute-start(bf16[3,64,128]{2,1,0:T(8,128)(2,1)S(1)} %get-tuple-element.38), channel_id=1, source_target_pairs={{0,1},{1,0},{2,3},{3,2},{4,5},{5,4},{6,7},{7,6},{8,9},{9,8},{10,11... | collective-permute-start | bytes 147464 | tf_op jit(solution)/shard_map/ppermute | solution.py:17
  65.2 23.8 %collective-permute-start.7 = (bf16[3,64,128]{2,1,0:T(8,128)(2,1)S(1)}, bf16[3,64,128]{2,1,0:T(8,128)(2,1)S(1)}, u32[]{:S(2)}, u32[]{:S(2)}) collective-permute-start(bf16[3,64,128]{2,1,0:T(8,128)(2,1)S(1)} %get-tuple-element.39), channel_id=1, source_target_pairs={{0,2},{1,3},{2,0},{3,1},{4,6},{5,7},{6,4},{7,5},{8,10},{9,11},{10,... | collective-permute-start | bytes 147464 | tf_op jit(solution)/shard_map/ppermute | solution.py:17
  67.1 23.1 %collective-permute-start.8 = (bf16[3,64,128]{2,1,0:T(8,128)(2,1)S(1)}, bf16[3,64,128]{2,1,0:T(8,128)(2,1)S(1)}, u32[]{:S(2)}, u32[]{:S(2)}) collective-permute-start(bf16[3,64,128]{2,1,0:T(8,128)(2,1)S(1)} %get-tuple-element.40), channel_id=1, source_target_pairs={{0,3},{1,2},{2,1},{3,0},{4,7},{5,6},{6,5},{7,4},{8,11},{9,10},{10,... | collective-permute-start | bytes 147464 | tf_op jit(solution)/shard_map/ppermute | solution.py:17
  73.0 17.7 %collective-permute-start.9 = (bf16[3,64,128]{2,1,0:T(8,128)(2,1)S(1)}, bf16[3,64,128]{2,1,0:T(8,128)(2,1)S(1)}, u32[]{:S(2)}, u32[]{:S(2)}) collective-permute-start(bf16[3,64,128]{2,1,0:T(8,128)(2,1)S(1)} %get-tuple-element.41), channel_id=1, source_target_pairs={{0,4},{1,5},{2,6},{3,7},{4,0},{5,1},{6,2},{7,3},{8,12},{9,13},{10,... | collective-permute-start | bytes 147464 | tf_op jit(solution)/shard_map/ppermute | solution.py:17
  80.5 10.4 %collective-permute-start.10 = (bf16[3,64,128]{2,1,0:T(8,128)(2,1)S(1)}, bf16[3,64,128]{2,1,0:T(8,128)(2,1)S(1)}, u32[]{:S(2)}, u32[]{:S(2)}) collective-permute-start(bf16[3,64,128]{2,1,0:T(8,128)(2,1)S(1)} %get-tuple-element.42), channel_id=1, source_target_pairs={{0,5},{1,4},{2,7},{3,6},{4,1},{5,0},{6,3},{7,2},{8,13},{9,12},{10,... | collective-permute-start | bytes 147464 | tf_op jit(solution)/shard_map/ppermute | solution.py:17
  85.1 8.9 %collective-permute-start.11 = (bf16[3,64,128]{2,1,0:T(8,128)(2,1)S(1)}, bf16[3,64,128]{2,1,0:T(8,128)(2,1)S(1)}, u32[]{:S(2)}, u32[]{:S(2)}) collective-permute-start(bf16[3,64,128]{2,1,0:T(8,128)(2,1)S(1)} %get-tuple-element.43), channel_id=1, source_target_pairs={{0,6},{1,7},{2,4},{3,5},{4,2},{5,3},{6,0},{7,1},{8,14},{9,15},{10,... | collective-permute-start | bytes 147464 | tf_op jit(solution)/shard_map/ppermute | solution.py:17
  89.0 7.5 %collective-permute-start.12 = (bf16[3,64,128]{2,1,0:T(8,128)(2,1)S(1)}, bf16[3,64,128]{2,1,0:T(8,128)(2,1)S(1)}, u32[]{:S(2)}, u32[]{:S(2)}) collective-permute-start(bf16[3,64,128]{2,1,0:T(8,128)(2,1)S(1)} %get-tuple-element.44), channel_id=1, source_target_pairs={{0,7},{1,6},{2,5},{3,4},{4,3},{5,2},{6,1},{7,0},{8,15},{9,14},{10,... | collective-permute-start | bytes 147464 | tf_op jit(solution)/shard_map/ppermute | solution.py:17
  90.3 6.7 %collective-permute-start.15 = (bf16[3,64,128]{2,1,0:T(8,128)(2,1)S(1)}, bf16[3,64,128]{2,1,0:T(8,128)(2,1)S(1)}, u32[]{:S(2)}, u32[]{:S(2)}) collective-permute-start(bf16[3,64,128]{2,1,0:T(8,128)(2,1)S(1)} %get-tuple-element.46), channel_id=1, source_target_pairs={{0,1},{1,0},{2,3},{3,2},{4,5},{5,4},{6,7},{7,6},{8,9},{9,8},{10,11... | collective-permute-start | bytes 147464 | tf_op jit(solution)/shard_map/ppermute | solution.py:17
  90.7 10.0 %collective-permute-start.16 = (bf16[3,64,128]{2,1,0:T(8,128)(2,1)S(1)}, bf16[3,64,128]{2,1,0:T(8,128)(2,1)S(1)}, u32[]{:S(2)}, u32[]{:S(2)}) collective-permute-start(bf16[3,64,128]{2,1,0:T(8,128)(2,1)S(1)} %get-tuple-element.47), channel_id=1, source_target_pairs={{0,2},{1,3},{2,0},{3,1},{4,6},{5,7},{6,4},{7,5},{8,10},{9,11},{10,... | collective-permute-start | bytes 147464 | tf_op jit(solution)/shard_map/ppermute | solution.py:17
  90.9 11.2 %collective-permute-start.17 = (bf16[3,64,128]{2,1,0:T(8,128)(2,1)S(1)}, bf16[3,64,128]{2,1,0:T(8,128)(2,1)S(1)}, u32[]{:S(2)}, u32[]{:S(2)}) collective-permute-start(bf16[3,64,128]{2,1,0:T(8,128)(2,1)S(1)} %get-tuple-element.48), channel_id=1, source_target_pairs={{0,3},{1,2},{2,1},{3,0},{4,7},{5,6},{6,5},{7,4},{8,11},{9,10},{10,... | collective-permute-start | bytes 147464 | tf_op jit(solution)/shard_map/ppermute | solution.py:17
  94.0 8.5 %collective-permute-start.18 = (bf16[3,64,128]{2,1,0:T(8,128)(2,1)S(1)}, bf16[3,64,128]{2,1,0:T(8,128)(2,1)S(1)}, u32[]{:S(2)}, u32[]{:S(2)}) collective-permute-start(bf16[3,64,128]{2,1,0:T(8,128)(2,1)S(1)} %get-tuple-element.49), channel_id=1, source_target_pairs={{0,4},{1,5},{2,6},{3,7},{4,0},{5,1},{6,2},{7,3},{8,12},{9,13},{10,... | collective-permute-start | bytes 147464 | tf_op jit(solution)/shard_map/ppermute | solution.py:17
  96.5 6.4 %collective-permute-start.19 = (bf16[3,64,128]{2,1,0:T(8,128)(2,1)S(1)}, bf16[3,64,128]{2,1,0:T(8,128)(2,1)S(1)}, u32[]{:S(2)}, u32[]{:S(2)}) collective-permute-start(bf16[3,64,128]{2,1,0:T(8,128)(2,1)S(1)} %get-tuple-element.50), channel_id=1, source_target_pairs={{0,5},{1,4},{2,7},{3,6},{4,1},{5,0},{6,3},{7,2},{8,13},{9,12},{10,... | collective-permute-start | bytes 147464 | tf_op jit(solution)/shard_map/ppermute | solution.py:17
  97.0 8.8 %collective-permute-start.20 = (bf16[3,64,128]{2,1,0:T(8,128)(2,1)S(1)}, bf16[3,64,128]{2,1,0:T(8,128)(2,1)S(1)}, u32[]{:S(2)}, u32[]{:S(2)}) collective-permute-start(bf16[3,64,128]{2,1,0:T(8,128)(2,1)S(1)} %get-tuple-element.51), channel_id=1, source_target_pairs={{0,6},{1,7},{2,4},{3,5},{4,2},{5,3},{6,0},{7,1},{8,14},{9,15},{10,... | collective-permute-start | bytes 147464 | tf_op jit(solution)/shard_map/ppermute | solution.py:17
  100.8 7.3 %collective-permute-start.21 = (bf16[3,64,128]{2,1,0:T(8,128)(2,1)S(1)}, bf16[3,64,128]{2,1,0:T(8,128)(2,1)S(1)}, u32[]{:S(2)}, u32[]{:S(2)}) collective-permute-start(bf16[3,64,128]{2,1,0:T(8,128)(2,1)S(1)} %get-tuple-element.52), channel_id=1, source_target_pairs={{0,7},{1,6},{2,5},{3,4},{4,3},{5,2},{6,1},{7,0},{8,15},{9,14},{10,... | collective-permute-start | bytes 147464 | tf_op jit(solution)/shard_map/ppermute | solution.py:17
  102.0 6.7 %collective-permute-start.24 = (bf16[3,64,128]{2,1,0:T(8,128)(2,1)S(1)}, bf16[3,64,128]{2,1,0:T(8,128)(2,1)S(1)}, u32[]{:S(2)}, u32[]{:S(2)}) collective-permute-start(bf16[3,64,128]{2,1,0:T(8,128)(2,1)S(1)} %get-tuple-element.54), channel_id=1, source_target_pairs={{0,1},{1,0},{2,3},{3,2},{4,5},{5,4},{6,7},{7,6},{8,9},{9,8},{10,11... | collective-permute-start | bytes 147464 | tf_op jit(solution)/shard_map/ppermute | solution.py:17
  102.5 10.0 %collective-permute-start.25 = (bf16[3,64,128]{2,1,0:T(8,128)(2,1)S(1)}, bf16[3,64,128]{2,1,0:T(8,128)(2,1)S(1)}, u32[]{:S(2)}, u32[]{:S(2)}) collective-permute-start(bf16[3,64,128]{2,1,0:T(8,128)(2,1)S(1)} %get-tuple-element.55), channel_id=1, source_target_pairs={{0,2},{1,3},{2,0},{3,1},{4,6},{5,7},{6,4},{7,5},{8,10},{9,11},{10,... | collective-permute-start | bytes 147464 | tf_op jit(solution)/shard_map/ppermute | solution.py:17
  102.9 10.9 %collective-permute-start.26 = (bf16[3,64,128]{2,1,0:T(8,128)(2,1)S(1)}, bf16[3,64,128]{2,1,0:T(8,128)(2,1)S(1)}, u32[]{:S(2)}, u32[]{:S(2)}) collective-permute-start(bf16[3,64,128]{2,1,0:T(8,128)(2,1)S(1)} %get-tuple-element.56), channel_id=1, source_target_pairs={{0,3},{1,2},{2,1},{3,0},{4,7},{5,6},{6,5},{7,4},{8,11},{9,10},{10,... | collective-permute-start | bytes 147464 | tf_op jit(solution)/shard_map/ppermute | solution.py:17
  105.8 8.5 %collective-permute-start.27 = (bf16[3,64,128]{2,1,0:T(8,128)(2,1)S(1)}, bf16[3,64,128]{2,1,0:T(8,128)(2,1)S(1)}, u32[]{:S(2)}, u32[]{:S(2)}) collective-permute-start(bf16[3,64,128]{2,1,0:T(8,128)(2,1)S(1)} %get-tuple-element.57), channel_id=1, source_target_pairs={{0,4},{1,5},{2,6},{3,7},{4,0},{5,1},{6,2},{7,3},{8,12},{9,13},{10,... | collective-permute-start | bytes 147464 | tf_op jit(solution)/shard_map/ppermute | solution.py:17
  108.1 6.3 %collective-permute-start.28 = (bf16[3,64,128]{2,1,0:T(8,128)(2,1)S(1)}, bf16[3,64,128]{2,1,0:T(8,128)(2,1)S(1)}, u32[]{:S(2)}, u32[]{:S(2)}) collective-permute-start(bf16[3,64,128]{2,1,0:T(8,128)(2,1)S(1)} %get-tuple-element.58), channel_id=1, source_target_pairs={{0,5},{1,4},{2,7},{3,6},{4,1},{5,0},{6,3},{7,2},{8,13},{9,12},{10,... | collective-permute-start | bytes 147464 | tf_op jit(solution)/shard_map/ppermute | solution.py:17
  108.7 8.8 %collective-permute-start.29 = (bf16[3,64,128]{2,1,0:T(8,128)(2,1)S(1)}, bf16[3,64,128]{2,1,0:T(8,128)(2,1)S(1)}, u32[]{:S(2)}, u32[]{:S(2)}) collective-permute-start(bf16[3,64,128]{2,1,0:T(8,128)(2,1)S(1)} %get-tuple-element.59), channel_id=1, source_target_pairs={{0,6},{1,7},{2,4},{3,5},{4,2},{5,3},{6,0},{7,1},{8,14},{9,15},{10,... | collective-permute-start | bytes 147464 | tf_op jit(solution)/shard_map/ppermute | solution.py:17
  112.6 7.6 %collective-permute-start.30 = (bf16[3,64,128]{2,1,0:T(8,128)(2,1)S(1)}, bf16[3,64,128]{2,1,0:T(8,128)(2,1)S(1)}, u32[]{:S(2)}, u32[]{:S(2)}) collective-permute-start(bf16[3,64,128]{2,1,0:T(8,128)(2,1)S(1)} %get-tuple-element.60), channel_id=1, source_target_pairs={{0,7},{1,6},{2,5},{3,4},{4,3},{5,2},{6,1},{7,0},{8,15},{9,14},{10,... | collective-permute-start | bytes 147464 | tf_op jit(solution)/shard_map/ppermute | solution.py:17
  113.8 8.0 %collective-permute-start.33 = (bf16[3,64,128]{2,1,0:T(8,128)(2,1)S(1)}, bf16[3,64,128]{2,1,0:T(8,128)(2,1)S(1)}, u32[]{:S(2)}, u32[]{:S(2)}) collective-permute-start(bf16[3,64,128]{2,1,0:T(8,128)(2,1)S(1)} %get-tuple-element.62), channel_id=1, source_target_pairs={{0,1},{1,0},{2,3},{3,2},{4,5},{5,4},{6,7},{7,6},{8,9},{9,8},{10,11... | collective-permute-start | bytes 147464 | tf_op jit(solution)/shard_map/ppermute | solution.py:17
  114.3 10.0 %collective-permute-start.34 = (bf16[3,64,128]{2,1,0:T(8,128)(2,1)S(1)}, bf16[3,64,128]{2,1,0:T(8,128)(2,1)S(1)}, u32[]{:S(2)}, u32[]{:S(2)}) collective-permute-start(bf16[3,64,128]{2,1,0:T(8,128)(2,1)S(1)} %get-tuple-element.63), channel_id=1, source_target_pairs={{0,2},{1,3},{2,0},{3,1},{4,6},{5,7},{6,4},{7,5},{8,10},{9,11},{10,... | collective-permute-start | bytes 147464 | tf_op jit(solution)/shard_map/ppermute | solution.py:17
  114.4 11.5 %collective-permute-start.35 = (bf16[3,64,128]{2,1,0:T(8,128)(2,1)S(1)}, bf16[3,64,128]{2,1,0:T(8,128)(2,1)S(1)}, u32[]{:S(2)}, u32[]{:S(2)}) collective-permute-start(bf16[3,64,128]{2,1,0:T(8,128)(2,1)S(1)} %get-tuple-element.64), channel_id=1, source_target_pairs={{0,3},{1,2},{2,1},{3,0},{4,7},{5,6},{6,5},{7,4},{8,11},{9,10},{10,... | collective-permute-start | bytes 147464 | tf_op jit(solution)/shard_map/ppermute | solution.py:17
  117.6 8.3 %collective-permute-start.36 = (bf16[3,64,128]{2,1,0:T(8,128)(2,1)S(1)}, bf16[3,64,128]{2,1,0:T(8,128)(2,1)S(1)}, u32[]{:S(2)}, u32[]{:S(2)}) collective-permute-start(bf16[3,64,128]{2,1,0:T(8,128)(2,1)S(1)} %get-tuple-element.65), channel_id=1, source_target_pairs={{0,4},{1,5},{2,6},{3,7},{4,0},{5,1},{6,2},{7,3},{8,12},{9,13},{10,... | collective-permute-start | bytes 147464 | tf_op jit(solution)/shard_map/ppermute | solution.py:17
  120.2 6.0 %collective-permute-start.37 = (bf16[3,64,128]{2,1,0:T(8,128)(2,1)S(1)}, bf16[3,64,128]{2,1,0:T(8,128)(2,1)S(1)}, u32[]{:S(2)}, u32[]{:S(2)}) collective-permute-start(bf16[3,64,128]{2,1,0:T(8,128)(2,1)S(1)} %get-tuple-element.66), channel_id=1, source_target_pairs={{0,5},{1,4},{2,7},{3,6},{4,1},{5,0},{6,3},{7,2},{8,13},{9,12},{10,... | collective-permute-start | bytes 147464 | tf_op jit(solution)/shard_map/ppermute | solution.py:17
  121.8 6.0 %collective-permute-start.38 = (bf16[3,64,128]{2,1,0:T(8,128)(2,1)S(1)}, bf16[3,64,128]{2,1,0:T(8,128)(2,1)S(1)}, u32[]{:S(2)}, u32[]{:S(2)}) collective-permute-start(bf16[3,64,128]{2,1,0:T(8,128)(2,1)S(1)} %get-tuple-element.67), channel_id=1, source_target_pairs={{0,6},{1,7},{2,4},{3,5},{4,2},{5,3},{6,0},{7,1},{8,14},{9,15},{10,... | collective-permute-start | bytes 147464 | tf_op jit(solution)/shard_map/ppermute | solution.py:17
  124.3 6.9 %collective-permute-start.39 = (bf16[3,64,128]{2,1,0:T(8,128)(2,1)S(1)}, bf16[3,64,128]{2,1,0:T(8,128)(2,1)S(1)}, u32[]{:S(2)}, u32[]{:S(2)}) collective-permute-start(bf16[3,64,128]{2,1,0:T(8,128)(2,1)S(1)} %get-tuple-element.68), channel_id=1, source_target_pairs={{0,7},{1,6},{2,5},{3,4},{4,3},{5,2},{6,1},{7,0},{8,15},{9,14},{10,... | collective-permute-start | bytes 147464 | tf_op jit(solution)/shard_map/ppermute | solution.py:17
  131.2 1.1 copy-start.3

commit v2 on v0

v2 whole, which is shorter than its diff:
```python
import functools

import jax
import jax.numpy as jnp
from jax import lax
from jax.experimental import pallas as pl
from jax.experimental.pallas import tpu as pltpu
from jax.sharding import PartitionSpec as P

STRIDE = 4
LANES = 128
DEPTH = 4 * LANES
MIB = 1024 * 1024
GROUPS = [[128], [128]]


def flipped(block, axis, mask):
    return lax.ppermute(block, axis, [(i, i ^ mask) for i in range(lax.axis_size(axis))])


def after(value, *others):
    return lax.optimization_barrier((value, *others))[0]


def in_vmem(array):
    return pltpu.with_memory_space_constraint(array, pltpu.VMEM)


def in_hbm(array):
    return pltpu.with_memory_space_constraint(array, pltpu.HBM)


def whole_in_vmem(count):
    return [pl.BlockSpec(memory_space=pltpu.VMEM)] * count


def strain_doublings(strain):
    steps = [strain[None]]
    mask = 1
    while mask < lax.axis_size("tm"):
        steps.append(jnp.concatenate([steps[-1], flipped(steps[-1], "tm", mask)], axis=0))
        mask *= 2
    return steps


def shifted(tile, distance):
    return pltpu.roll(tile, tile.shape[1] - distance, 1) if distance else tile


def hankel_kernel(strain_ref, out_ref, split_ref, tile_ref):
    count, detectors, samples = strain_ref.shape
    here = samples // STRIDE
    width = out_ref.shape[2]
    me = lax.axis_index("tm")
    sample = lax.broadcasted_iota(jnp.int32, (samples, samples), 0)
    column = lax.broadcasted_iota(jnp.int32, (samples, samples), 1)
    wanted = STRIDE * lax.rem(column, here) + column // here
    selector = jnp.where(sample == wanted, 1.0, 0.0).astype(jnp.bfloat16)
    for k in range(count):
        split_ref[k] = jnp.dot(strain_ref[k], selector, preferred_element_type=jnp.float32)
    tile_ref[...] = jnp.zeros_like(tile_ref)
    for t in range(count):
        block = split_ref[me ^ t]
        for d in range(detectors):
            for p in range(STRIDE):
                tile_ref[d, p : p + 1, t * here : (t + 1) * here] = block[
                    d : d + 1, p * here : (p + 1) * here
                ]
    per_half = 8 // STRIDE
    row = lax.broadcasted_iota(jnp.int32, tile_ref.shape[1:], 0)
    for d in range(detectors):
        tile = tile_ref[d]
        tile = jnp.where(row < STRIDE, tile, pltpu.roll(shifted(tile, 1), STRIDE, 0))
        for i in range(out_ref.shape[1] // 16):
            first = shifted(tile, 2 * per_half * i)
            second = shifted(tile, 2 * per_half * i + per_half)
            block = jnp.concatenate([first[:, :width], second[:, :width]], axis=0)
            out_ref[d, 16 * i : 16 * (i + 1), :] = block.astype(out_ref.dtype)


def hankel(blocks, taps):
    count, detectors, samples = blocks.shape
    width = count * samples // STRIDE + (taps - DEPTH) // STRIDE
    length = -(-(width + DEPTH // STRIDE) // LANES) * LANES
    return pl.pallas_call(
        hankel_kernel,
        in_specs=whole_in_vmem(1),
        out_specs=pl.BlockSpec(memory_space=pltpu.VMEM),
        out_shape=jax.ShapeDtypeStruct((detectors, DEPTH, width), jnp.bfloat16),
        scratch_shapes=[
            pltpu.VMEM((count, detectors, samples), jnp.float32),
            pltpu.VMEM((detectors, 2 * STRIDE, length), jnp.float32),
        ],
        compiler_params=pltpu.CompilerParams(vmem_limit_bytes=16 * MIB),
        name="hankel",
    )(in_vmem(blocks))


def long_hankel_kernel(rows_ref, out_ref):
    tile = rows_ref[0]
    width = out_ref.shape[2]
    length = tile.shape[1]
    per_half = 8 // STRIDE

    def step(i, carry):
        first = pltpu.roll(tile, lax.rem(length - 2 * per_half * i, length), 1)
        second = pltpu.roll(tile, length - 2 * per_half * i - per_half, 1)
        block = jnp.concatenate([first[:, :width], second[:, :width]], axis=0)
        out_ref[0, pl.ds(pl.multiple_of(16 * i, 16), 16), :] = block.astype(out_ref.dtype)
        return carry

    lax.fori_loop(0, out_ref.shape[1] // 16, step, 0)


def long_hankel(strain, taps, times):
    detectors, here = strain.shape
    phases = strain.reshape(detectors, here // STRIDE, STRIDE).transpose(0, 2, 1)
    phases = lax.all_gather(phases, "tm", axis=2, tiled=True)
    width = times + (taps - DEPTH) // STRIDE
    length = -(-(width + DEPTH // STRIDE) // LANES) * LANES
    padded = jnp.pad(phases.astype(jnp.float32), ((0, 0), (0, 0), (0, length + 1 - times)))
    rows = jnp.concatenate([padded[:, :, :length], padded[:, :, 1:]], axis=1)
    return pl.pallas_call(
        long_hankel_kernel,
        grid=(detectors,),
        in_specs=[pl.BlockSpec((1, 2 * STRIDE, length), lambda d: (d, 0, 0))],
        out_specs=pl.BlockSpec((1, DEPTH, width), lambda d: (d, 0, 0)),
        out_shape=jax.ShapeDtypeStruct((detectors, DEPTH, width), jnp.bfloat16),
        compiler_params=pltpu.CompilerParams(vmem_limit_bytes=24 * MIB),
        name="long_hankel",
    )(rows)


def staging_kernel(coefficients_ref, near_ref, far_ref, filters_ref, own_ref, rows_ref, semaphores):
    half, taps = near_ref.shape
    block = taps // 4
    group = lax.axis_index("basis")
    copies = []
    for i, which in enumerate((group, group ^ 1)):
        columns = pl.ds(pl.multiple_of(which * half, LANES), half)
        copies.append(
            pltpu.make_async_copy(
                coefficients_ref.at[:, columns],
                rows_ref.at[:, i * half : (i + 1) * half],
                semaphores.at[i],
            )
        )
    for n in range(4):
        for i, source in enumerate((near_ref, far_ref)):
            there = filters_ref.at[i * half : (i + 1) * half, n * block : (n + 1) * block]
            copies.append(
                pltpu.make_async_copy(
                    source.at[:, n * block : (n + 1) * block], there, semaphores.at[2 + 2 * n + i]
                )
            )
    for copy in copies:
        copy.start()
    copies[0].wait()
    copies[1].wait()
    for n in range(4):
        copies[2 + 2 * n].wait()
        copies[3 + 2 * n].wait()
        own_ref[:, n * block : (n + 1) * block] = jnp.dot(
            rows_ref[...],
            filters_ref[:, n * block : (n + 1) * block],
            preferred_element_type=jnp.float32,
        )


def staged(coefficients, near, far):
    own_rows = coefficients.shape[0]
    half, taps = near.shape
    return pl.pallas_call(
        staging_kernel,
        in_specs=[pl.BlockSpec(memory_space=pl.ANY)] * 3,
        out_specs=whole_in_vmem(2),
        out_shape=[
            jax.ShapeDtypeStruct((2 * half, taps), jnp.bfloat16),
            jax.ShapeDtypeStruct((own_rows, taps), jnp.float32),
        ],
        scratch_shapes=[
            pltpu.VMEM((own_rows, 2 * half), jnp.bfloat16),
            pltpu.SemaphoreType.DMA((10,)),
        ],
        cost_estimate=pl.CostEstimate(
            flops=4 * own_rows * half * taps, bytes_accessed=8 * half * taps, transcendentals=0
        ),
        compiler_params=pltpu.CompilerParams(vmem_limit_bytes=20 * MIB),
        name="staged",
    )(in_hbm(coefficients), in_hbm(near), in_hbm(far))


def partial_kernel(rows_ref, filters_ref, out_ref):
    depth, taps = filters_ref.shape
    core = lax.rem(lax.axis_index("basis"), 2)
    near = pl.ds(pl.multiple_of(core * (depth // 2), LANES), depth // 2)
    far = pl.ds(pl.multiple_of((1 - core) * (depth // 2), LANES), depth // 2)
    rows = jnp.concatenate([rows_ref[:, near], rows_ref[:, far]], axis=1)
    for n in range(0, taps, 512):
        out_ref[:, n : n + 512] = jnp.dot(
            rows, filters_ref[:, n : n + 512], preferred_element_type=jnp.float32
        ).astype(out_ref.dtype)


def partial_rows(rows, filters):
    count = rows.shape[0]
    depth, taps = filters.shape
    return pl.pallas_call(
        partial_kernel,
        in_specs=whole_in_vmem(2),
        out_specs=pl.BlockSpec(memory_space=pltpu.VMEM),
        out_shape=jax.ShapeDtypeStruct((count, taps), jnp.bfloat16),
        cost_estimate=pl.CostEstimate(
            flops=2 * count * depth * taps, bytes_accessed=2 * depth * taps, transcendentals=0
        ),
        compiler_params=pltpu.CompilerParams(vmem_limit_bytes=16 * MIB),
        name="partial_rows",
    )(in_vmem(rows), in_vmem(filters))


def rounded_sum(own, others):
    other = jnp.concatenate([ref[...] for ref in others], axis=0)
    return (own + other.astype(jnp.float32)).astype(jnp.bfloat16)


def series_kernel(start, parts, own_ref, *refs):
    others, hankel_ref, outs, scratch = refs[:parts], refs[parts], refs[parts + 1 : -1], refs[-1]
    detectors = hankel_ref.shape[0]
    rows, times = scratch.shape
    taps = own_ref.shape[1]
    here = times // len(outs)
    me = lax.axis_index("tm")
    weights = rounded_sum(own_ref[start : start + rows], others)
    for d in range(detectors):
        total = None
        for q in range(taps // DEPTH):
            term = jnp.dot(
                weights[:, q * DEPTH : (q + 1) * DEPTH],
                hankel_ref[d, :, q * LANES : q * LANES + times],
                preferred_element_type=jnp.float32,
            )
            total = term if total is None else total + term
        scratch[...] = total.astype(jnp.bfloat16)
        for k, out in enumerate(outs):
            out[d] = scratch[:, pl.ds(pl.multiple_of((me ^ k) * here, LANES), here)]


def series(own, start, others, matrix, count, here):
    taps = own.shape[1]
    rows = sum(part.shape[0] for part in others)
    detectors, depth, width = matrix.shape
    return pl.pallas_call(
        functools.partial(series_kernel, start, len(others)),
        in_specs=whole_in_vmem(2 + len(others)),
        out_specs=whole_in_vmem(count),
        out_shape=[jax.ShapeDtypeStruct((detectors, rows, here), jnp.bfloat16)] * count,
        scratch_shapes=[pltpu.VMEM((rows, count * here), jnp.bfloat16)],
        cost_estimate=pl.CostEstimate(
            flops=2 * rows * taps * detectors * count * here,
            bytes_accessed=2 * detectors * depth * width,
            transcendentals=0,
        ),
        compiler_params=pltpu.CompilerParams(vmem_limit_bytes=16 * MIB),
        name="series",
    )(in_vmem(own), *[in_vmem(part) for part in others], in_vmem(matrix))


def assembling_kernel(starts, own_rows, *refs):
    blocks, out_ref, semaphores = refs[:-2], refs[-2], refs[-1]
    count = len(blocks) // len(starts)
    me = lax.axis_index("tm")
    copies = []
    for g, start in enumerate(starts):
        for k in range(count):
            block = blocks[g * count + k]
            at = pl.multiple_of((me ^ k) * own_rows + start, 16)
            copies.append(
                pltpu.make_async_copy(
                    block,
                    out_ref.at[:, pl.ds(at, block.shape[1]), :],
                    semaphores.at[g * count + k],
                )
            )
    for copy in copies:
        copy.start()
    for copy in copies:
        copy.wait()


def assembled(groups, own_rows):
    count = len(groups[0])
    detectors, _, here = groups[0][0].shape
    starts, start = [], 0
    for group in groups:
        starts.append(start)
        start += group[0].shape[1]
    blocks = [block for group in groups for block in group]
    return pl.pallas_call(
        functools.partial(assembling_kernel, starts, own_rows),
        in_specs=whole_in_vmem(len(blocks)),
        out_specs=pl.BlockSpec(memory_space=pl.ANY),
        out_shape=jax.ShapeDtypeStruct((detectors, count * own_rows, here), jnp.bfloat16),
        scratch_shapes=[pltpu.SemaphoreType.DMA((len(blocks),))],
        compiler_params=pltpu.CompilerParams(vmem_limit_bytes=16 * MIB),
        name="assembled",
    )(*[in_vmem(block) for block in blocks])


def long_series_kernel(weights_ref, hankel_ref, out_ref):
    here = out_ref.shape[3]
    start = pl.program_id(1) * (2 * here)
    total = None
    for q in range(weights_ref.shape[1] // DEPTH):
        columns = pl.ds(pl.multiple_of(start + q * LANES, LANES), 2 * here)
        term = jnp.dot(
            weights_ref[:, q * DEPTH : (q + 1) * DEPTH],
            hankel_ref[0, :, columns],
            preferred_element_type=jnp.float32,
        )
        total = term if total is None else total + term
    out_ref[0, 0] = total[:, :here].astype(jnp.bfloat16)
    out_ref[1, 0] = total[:, here:].astype(jnp.bfloat16)


def long_series(weights, matrix, count, here):
    rows, taps = weights.shape
    detectors, depth, width = matrix.shape
    return pl.pallas_call(
        long_series_kernel,
        grid=(detectors, count // 2),
        in_specs=[
            pl.BlockSpec((rows, taps), lambda d, n: (0, 0)),
            pl.BlockSpec((1, depth, width), lambda d, n: (d, 0, 0)),
        ],
        out_specs=pl.BlockSpec((2, 1, rows, here), lambda d, n: (n, d, 0, 0)),
        out_shape=jax.ShapeDtypeStruct((count, detectors, rows, here), jnp.bfloat16),
        compiler_params=pltpu.CompilerParams(vmem_limit_bytes=32 * MIB),
        name="long_series",
    )(weights, matrix)


def shards(strain, basis_filters, coefficients):
    detectors, samples_here = strain.shape
    here = samples_here // STRIDE
    filters, taps = basis_filters.shape
    own_rows = coefficients.shape[0]
    count = lax.axis_size("tm")
    me = lax.axis_index("tm")
    group = lax.axis_index("basis")
    short = count == 8 and here == LANES
    groups = GROUPS if short and own_rows == 256 else [[own_rows]]
    sizes = [size for part in groups for size in part]
    starts = [sum(sizes[:c]) for c in range(len(sizes))]
    chunks = range(len(sizes))

    at = (group // 2 ^ 1) * (2 * filters)
    cuts = []
    for c in chunks:
        source = after(coefficients, cuts[-1]) if cuts else coefficients
        cuts.append(lax.dynamic_slice(source, (starts[c], at), (sizes[c], 2 * filters)))
    asked = [flipped(cut, "basis", 2) for cut in cuts]
    sibling = flipped(basis_filters, "basis", 1)
    if short:
        steps = strain_doublings(after(strain, cuts[-1]))
        chip_filters, own = staged(after(coefficients, steps[1]), basis_filters, sibling)
        matrix = hankel(steps[-1], taps)
        asked[0] = after(asked[0], steps[2])
        asked[-1] = after(asked[-1], matrix)
    else:
        chip_filters, own = staged(coefficients, basis_filters, sibling)
        matrix = long_hankel(strain, taps, count * here)
    other = [flipped(partial_rows(rows, chip_filters), "basis", 2) for rows in asked]

    if not short:
        weights = (own + other[0].astype(jnp.float32)).astype(jnp.bfloat16)
        blocks = long_series(weights, matrix, count, here)
        arrived = lax.all_to_all(blocks, "tm", split_axis=0, concat_axis=0, tiled=True)
        return arrived.transpose(0, 2, 1, 3).reshape(count * own_rows, detectors, here)

    blocks = []
    c = 0
    for part in groups:
        blocks.append(series(own, starts[c], other[c : c + len(part)], matrix, count, here))
        c += len(part)
    arrived = [[flipped(b[k], "tm", k) if k else b[k] for k in range(count)] for b in blocks]
    return assembled(arrived, own_rows).transpose(1, 0, 2)


def solution(mesh):
    placed = (P(None, "tm"), P("basis", None), P(("basis", "tm"), None))
    return jax.shard_map(
        shards, mesh=mesh, in_specs=placed, out_specs=P("basis", None, "tm"), check_vma=False
    )
```

time: 402 us -> 85.1 us (0.21)
  the two profiles are of different devices: /device:TPU:0 before, /device:TPU:17 now
where the time goes in v2:
time: 85.1 us; the launch traced here: 84.9 us
  waiting for transfers between devices  44 us (52%)
  starting transfers between devices  23.8 us (28%)
  Pallas kernels  14.8 us (17%)
  local copies, waits for them, and re-layouts  2.16 us (3%)
    ppermute x22, waiting for transfers between devices, flipped(): lax.ppermute(block, axis, [(i, i ^ mask) for i in range(lax.axis_size(axi...  44 us
    ppermute x22, starting transfers between devices, flipped(): lax.ppermute(block, axis, [(i, i ^ mask) for i in range(lax.axis_size(axi...  23.8 us
    pallas_call x1, Pallas kernels, staged(): pl.pallas_call(staging_kernel, in_specs=[pl.BlockSpec(memory_space=pl.ANY...  4.8 us
    pallas_call x2, Pallas kernels, series(): pl.pallas_call(functools.partial(series_kernel, start, len(others)), in_s...  4.07 us
    pallas_call x2, Pallas kernels, partial_rows(): pl.pallas_call(partial_kernel, in_specs=whole_in_vmem(2), out_specs=pl.Bl...  2.52 us
    dynamic_slice x2, local copies, waits for them, and re-layouts, shards(): lax.dynamic_slice(source, (starts[c], at), (sizes[c], 2 * filters))  2.16 us
    pallas_call x1, Pallas kernels, hankel(): pl.pallas_call(hankel_kernel, in_specs=whole_in_vmem(1), out_specs=pl.Blo...  2.11 us
  transfers between devices with their start and end apart: 22, of which 12 were waited for; matrix products, arithmetic and copies ran while one was open for 3% of the time, Pallas kernels for 16%

profile of v2, /device:TPU:17, one launch (start us, length us, event | category | flops | bytes accessed | tf_op | source)
XLA Modules:
  0.0 84.9 jit_solution(17839761170347788953)
XLA Ops:
  0.0 0.0 copy-start
  0.0 0.7 collective-permute-start.1
  0.7 1.1 %constant_dynamic-slice_fusion.1 = bf16[128,2048]{1,0:T(8,128)(2,1)S(1)} fusion(bf16[256,4096]{1,0:T(8,128)(2,1)} %coefficients_ref, s32[]{:T(128)S(6)} %select_n.10), kind=kLoop, calls=%fused_computation.4 | loop fusion | bytes 1048580 | tf_op jit(solution)/shard_map/dynamic_slice | solution.py:360
  1.8 1.3 %collective-permute-start.2 = (bf16[128,2048]{1,0:T(8,128)(2,1)S(1)}, bf16[128,2048]{1,0:T(8,128)(2,1)S(1)}, u32[]{:S(2)}, u32[]{:S(2)}) collective-permute-start(bf16[128,2048]{1,0:T(8,128)(2,1)S(1)} %constant_dynamic-slice_fusion.1), channel_id=1, source_target_pairs={{0,16},{8,24},{16,0},{24,8},{1,17},{9,25},{17,1},{25,9},{2,18},{10... | collective-permute-start | bytes 1572872 | tf_op jit(solution)/shard_map/ppermute | solution.py:18
  3.0 1.1 %constant_dynamic-slice_fusion = bf16[128,2048]{1,0:T(8,128)(2,1)S(1)} fusion(bf16[256,4096]{1,0:T(8,128)(2,1)} %coefficients_ref, s32[]{:T(128)S(6)} %select_n.10), kind=kLoop, calls=%fused_computation.3 | loop fusion | bytes 1048580 | tf_op jit(solution)/shard_map/dynamic_slice | solution.py:360
  4.1 0.0 copy-done
  4.1 1.3 %collective-permute-start = (bf16[1,3,512]{2,1,0:T(4,128)(2,1)S(1)}, bf16[1,3,512]{2,1,0:T(4,128)(2,1)S(1)}, u32[]{:S(2)}, u32[]{:S(2)}) collective-permute-start(bf16[1,3,512]{2,1,0:T(4,128)(2,1)S(1)} %bitcast.2), channel_id=1, source_target_pairs={{0,1},{1,0},{2,3},{3,2},{4,5},{5,4},{6,7},{7,6},{8,9},{9,8},{10,11... | collective-permute-start | bytes 9224 | tf_op jit(solution)/shard_map/ppermute | solution.py:18
  5.4 1.5 %collective-permute-done = bf16[1,3,512]{2,1,0:T(4,128)(2,1)S(1)} collective-permute-done((bf16[1,3,512]{2,1,0:T(4,128)(2,1)S(1)}, bf16[1,3,512]{2,1,0:T(4,128)(2,1)S(1)}, u32[]{:S(2)}, u32[]{:S(2)}) %collective-permute-start) | collective-permute-done | bytes 3104 | tf_op jit(solution)/shard_map/ppermute | solution.py:18
  7.0 1.4 %collective-permute-start.3 = (bf16[2,3,512]{2,1,0:T(4,128)(2,1)S(1)}, bf16[2,3,512]{2,1,0:T(4,128)(2,1)S(1)}, u32[]{:S(2)}, u32[]{:S(2)}) collective-permute-start(bf16[2,3,512]{2,1,0:T(4,128)(2,1)S(1)} %pad_maximum_fusion.2), channel_id=1, source_target_pairs={{0,2},{1,3},{2,0},{3,1},{4,6},{5,7},{6,4},{7,5},{8,10},{9,11},{10,... | collective-permute-start | bytes 18440 | tf_op jit(solution)/shard_map/ppermute | solution.py:18
  8.3 0.3 collective-permute-start.13
  8.6 1.2 %collective-permute-done.3 = bf16[2,3,512]{2,1,0:T(4,128)(2,1)S(1)} collective-permute-done((bf16[2,3,512]{2,1,0:T(4,128)(2,1)S(1)}, bf16[2,3,512]{2,1,0:T(4,128)(2,1)S(1)}, u32[]{:S(2)}, u32[]{:S(2)}) %collective-permute-start.3) | collective-permute-done | bytes 6176 | tf_op jit(solution)/shard_map/ppermute | solution.py:18
  9.9 0.1 collective-permute-start.5
  10.0 5.4 %collective-permute-done.2.rows_ref = bf16[128,2048]{1,0:T(8,128)(2,1)S(1)} collective-permute-done((bf16[128,2048]{1,0:T(8,128)(2,1)S(1)}, bf16[128,2048]{1,0:T(8,128)(2,1)S(1)}, u32[]{:S(2)}, u32[]{:S(2)}) %collective-permute-start.2) | collective-permute-done | bytes 524320 | tf_op jit(solution)/shard_map/ppermute | solution.py:18
  15.4 0.0 collective-permute-done.1.far_ref
  15.4 4.8 %staged.1 = (bf16[2048,2048]{1,0:T(8,128)(2,1)S(1)}, f32[256,2048]{1,0:T(8,128)S(1)}) custom-call(bf16[256,4096]{1,0:T(8,128)(2,1)} %coefficients_ref, bf16[1024,2048]{1,0:T(8,128)(2,1)} %near_ref.1, bf16[1024,2048]{1,0:T(8,128)(2,1)} %collective-permute-done.1.far_ref), custom_call_target="tpu_custom_call" | custom-call | flops 2147483648 | bytes 16777216 | tf_op jit(solution)/shard_map/staged/pallas_call | solution.py:173
  20.2 1.3 %partial_rows.2 = bf16[128,2048]{1,0:T(8,128)(2,1)S(1)} custom-call(bf16[128,2048]{1,0:T(8,128)(2,1)S(1)} %collective-permute-done.2.rows_ref, bf16[2048,2048]{1,0:T(8,128)(2,1)S(1)} %get-tuple-element.33.filters_ref), custom_call_target="tpu_custom_call" | custom-call | flops 1073741824 | bytes 8388608 | tf_op jit(solution)/shard_map/partial_rows/pallas_call | solution.py:208
  21.5 1.3 %collective-permute-start.4 = (bf16[128,2048]{1,0:T(8,128)(2,1)S(1)}, bf16[128,2048]{1,0:T(8,128)(2,1)S(1)}, u32[]{:S(2)}, u32[]{:S(2)}) collective-permute-start(bf16[128,2048]{1,0:T(8,128)(2,1)S(1)} %partial_rows.2), channel_id=1, source_target_pairs={{0,16},{8,24},{16,0},{24,8},{1,17},{9,25},{17,1},{25,9},{2,18},{10... | collective-permute-start | bytes 1572872 | tf_op jit(solution)/shard_map/ppermute | solution.py:18
  22.7 0.0 collective-permute-done.5
  22.8 2.1 %hankel.1.refs_1_ = bf16[3,512,1408]{2,1,0:T(8,128)(2,1)S(1)} custom-call(bf16[8,3,512]{2,1,0:T(4,128)(2,1)S(1)} %pad_maximum_fusion.strain_ref), custom_call_target="tpu_custom_call" | custom-call | tf_op jit(solution)/shard_map/hankel/pallas_call | solution.py:85
  24.9 1.7 %collective-permute-done.13.rows_ref = bf16[128,2048]{1,0:T(8,128)(2,1)S(1)} collective-permute-done((bf16[128,2048]{1,0:T(8,128)(2,1)S(1)}, bf16[128,2048]{1,0:T(8,128)(2,1)S(1)}, u32[]{:S(2)}, u32[]{:S(2)}) %collective-permute-start.13) | collective-permute-done | bytes 524320 | tf_op jit(solution)/shard_map/ppermute | solution.py:18
  26.6 1.3 %partial_rows.3 = bf16[128,2048]{1,0:T(8,128)(2,1)S(1)} custom-call(bf16[128,2048]{1,0:T(8,128)(2,1)S(1)} %collective-permute-done.13.rows_ref, bf16[2048,2048]{1,0:T(8,128)(2,1)S(1)} %get-tuple-element.33.filters_ref), custom_call_target="tpu_custom_call" | custom-call | flops 1073741824 | bytes 8388608 | tf_op jit(solution)/shard_map/partial_rows/pallas_call | solution.py:208
  27.9 1.3 %collective-permute-start.14 = (bf16[128,2048]{1,0:T(8,128)(2,1)S(1)}, bf16[128,2048]{1,0:T(8,128)(2,1)S(1)}, u32[]{:S(2)}, u32[]{:S(2)}) collective-permute-start(bf16[128,2048]{1,0:T(8,128)(2,1)S(1)} %partial_rows.3), channel_id=1, source_target_pairs={{0,16},{8,24},{16,0},{24,8},{1,17},{9,25},{17,1},{25,9},{2,18},{10... | collective-permute-start | bytes 1572872 | tf_op jit(solution)/shard_map/ppermute | solution.py:18
  29.2 8.7 %collective-permute-done.4.refs_0_ = bf16[128,2048]{1,0:T(8,128)(2,1)S(1)} collective-permute-done((bf16[128,2048]{1,0:T(8,128)(2,1)S(1)}, bf16[128,2048]{1,0:T(8,128)(2,1)S(1)}, u32[]{:S(2)}, u32[]{:S(2)}) %collective-permute-start.4) | collective-permute-done | bytes 524320 | tf_op jit(solution)/shard_map/ppermute | solution.py:18
  37.8 2.0 %series.2 = (bf16[3,128,128]{2,1,0:T(8,128)(2,1)S(1)}, bf16[3,128,128]{2,1,0:T(8,128)(2,1)S(1)}, bf16[3,128,128]{2,1,0:T(8,128)(2,1)S(1)}, bf16[3,128,128]{2,1,0...) custom-call(f32[256,2048]{1,0:T(8,128)S(1)} %get-tuple-element.31.ow, ...), custom_call_target="tpu_custom_call" | custom-call | flops 1610612736 | bytes 4325376 | tf_op jit(solution)/shard_map/series/pallas_call | solution.py:252
  39.9 1.3 %collective-permute-start.6 = (bf16[3,128,128]{2,1,0:T(8,128)(2,1)S(1)}, bf16[3,128,128]{2,1,0:T(8,128)(2,1)S(1)}, u32[]{:S(2)}, u32[]{:S(2)}) collective-permute-start(bf16[3,128,128]{2,1,0:T(8,128)(2,1)S(1)} %get-tuple-element.35), channel_id=1, source_target_pairs={{0,1},{1,0},{2,3},{3,2},{4,5},{5,4},{6,7},{7,6},{8,9},{9,8},{10,11... | collective-permute-start | bytes 294920 | tf_op jit(solution)/shard_map/ppermute | solution.py:18
  41.2 1.3 %collective-permute-start.7 = (bf16[3,128,128]{2,1,0:T(8,128)(2,1)S(1)}, bf16[3,128,128]{2,1,0:T(8,128)(2,1)S(1)}, u32[]{:S(2)}, u32[]{:S(2)}) collective-permute-start(bf16[3,128,128]{2,1,0:T(8,128)(2,1)S(1)} %get-tuple-element.36), channel_id=1, source_target_pairs={{0,2},{1,3},{2,0},{3,1},{4,6},{5,7},{6,4},{7,5},{8,10},{9,11},{10,... | collective-permute-start | bytes 294920 | tf_op jit(solution)/shard_map/ppermute | solution.py:18
  42.5 0.1 collective-permute-start.8
  42.6 0.0 collective-permute-start.9
  42.6 6.5 %collective-permute-done.14.refs_0_ = bf16[128,2048]{1,0:T(8,128)(2,1)S(1)} collective-permute-done((bf16[128,2048]{1,0:T(8,128)(2,1)S(1)}, bf16[128,2048]{1,0:T(8,128)(2,1)S(1)}, u32[]{:S(2)}, u32[]{:S(2)}) %collective-permute-start.14) | collective-permute-done | bytes 524320 | tf_op jit(solution)/shard_map/ppermute | solution.py:18
  49.1 1.0 %collective-permute-start.10 = (bf16[3,128,128]{2,1,0:T(8,128)(2,1)S(1)}, bf16[3,128,128]{2,1,0:T(8,128)(2,1)S(1)}, u32[]{:S(2)}, u32[]{:S(2)}) collective-permute-start(bf16[3,128,128]{2,1,0:T(8,128)(2,1)S(1)} %get-tuple-element.39), channel_id=1, source_target_pairs={{0,5},{1,4},{2,7},{3,6},{4,1},{5,0},{6,3},{7,2},{8,13},{9,12},{10,... | collective-permute-start | bytes 294920 | tf_op jit(solution)/shard_map/ppermute | solution.py:18
  50.1 2.0 %series.3 = (bf16[3,128,128]{2,1,0:T(8,128)(2,1)S(1)}, bf16[3,128,128]{2,1,0:T(8,128)(2,1)S(1)}, bf16[3,128,128]{2,1,0:T(8,128)(2,1)S(1)}, bf16[3,128,128]{2,1,0...) custom-call(f32[256,2048]{1,0:T(8,128)S(1)} %get-tuple-element.31.ow, ...), custom_call_target="tpu_custom_call" | custom-call | flops 1610612736 | bytes 4325376 | tf_op jit(solution)/shard_map/series/pallas_call | solution.py:252
  52.1 0.0 collective-permute-done.6.refs_1_
  52.2 2.5 %collective-permute-start.11 = (bf16[3,128,128]{2,1,0:T(8,128)(2,1)S(1)}, bf16[3,128,128]{2,1,0:T(8,128)(2,1)S(1)}, u32[]{:S(2)}, u32[]{:S(2)}) collective-permute-start(bf16[3,128,128]{2,1,0:T(8,128)(2,1)S(1)} %get-tuple-element.40), channel_id=1, source_target_pairs={{0,6},{1,7},{2,4},{3,5},{4,2},{5,3},{6,0},{7,1},{8,14},{9,15},{10,... | collective-permute-start | bytes 294920 | tf_op jit(solution)/shard_map/ppermute | solution.py:18
  54.6 0.0 collective-permute-done.7.refs_2_
  54.6 0.0 collective-permute-start.12
  54.7 0.0 collective-permute-done.8.refs_3_
  54.7 1.2 %collective-permute-start.15 = (bf16[3,128,128]{2,1,0:T(8,128)(2,1)S(1)}, bf16[3,128,128]{2,1,0:T(8,128)(2,1)S(1)}, u32[]{:S(2)}, u32[]{:S(2)}) collective-permute-start(bf16[3,128,128]{2,1,0:T(8,128)(2,1)S(1)} %get-tuple-element.44), channel_id=1, source_target_pairs={{0,1},{1,0},{2,3},{3,2},{4,5},{5,4},{6,7},{7,6},{8,9},{9,8},{10,11... | collective-permute-start | bytes 294920 | tf_op jit(solution)/shard_map/ppermute | solution.py:18
  55.9 0.0 collective-permute-done.9.refs_4_
  55.9 2.1 %collective-permute-start.16 = (bf16[3,128,128]{2,1,0:T(8,128)(2,1)S(1)}, bf16[3,128,128]{2,1,0:T(8,128)(2,1)S(1)}, u32[]{:S(2)}, u32[]{:S(2)}) collective-permute-start(bf16[3,128,128]{2,1,0:T(8,128)(2,1)S(1)} %get-tuple-element.45), channel_id=1, source_target_pairs={{0,2},{1,3},{2,0},{3,1},{4,6},{5,7},{6,4},{7,5},{8,10},{9,11},{10,... | collective-permute-start | bytes 294920 | tf_op jit(solution)/shard_map/ppermute | solution.py:18
  58.0 0.0 collective-permute-done.10.refs_5_
  58.0 4.9 %collective-permute-start.17 = (bf16[3,128,128]{2,1,0:T(8,128)(2,1)S(1)}, bf16[3,128,128]{2,1,0:T(8,128)(2,1)S(1)}, u32[]{:S(2)}, u32[]{:S(2)}) collective-permute-start(bf16[3,128,128]{2,1,0:T(8,128)(2,1)S(1)} %get-tuple-element.46), channel_id=1, source_target_pairs={{0,3},{1,2},{2,1},{3,0},{4,7},{5,6},{6,5},{7,4},{8,11},{9,10},{10,... | collective-permute-start | bytes 294920 | tf_op jit(solution)/shard_map/ppermute | solution.py:18
  62.9 1.1 %collective-permute-done.11.refs_6_ = bf16[3,128,128]{2,1,0:T(8,128)(2,1)S(1)} collective-permute-done((bf16[3,128,128]{2,1,0:T(8,128)(2,1)S(1)}, bf16[3,128,128]{2,1,0:T(8,128)(2,1)S(1)}, u32[]{:S(2)}, u32[]{:S(2)}) %collective-permute-start.11) | collective-permute-done | bytes 98336 | tf_op jit(solution)/shard_map/ppermute | solution.py:18
  64.0 0.0 collective-permute-start.18
  64.0 3.4 %collective-permute-done.12.refs_7_ = bf16[3,128,128]{2,1,0:T(8,128)(2,1)S(1)} collective-permute-done((bf16[3,128,128]{2,1,0:T(8,128)(2,1)S(1)}, bf16[3,128,128]{2,1,0:T(8,128)(2,1)S(1)}, u32[]{:S(2)}, u32[]{:S(2)}) %collective-permute-start.12) | collective-permute-done | bytes 98336 | tf_op jit(solution)/shard_map/ppermute | solution.py:18
  67.4 0.0 collective-permute-start.19
  67.4 0.0 collective-permute-done.15.refs_9_
  67.4 0.0 collective-permute-start.20
  67.4 0.0 collective-permute-done.16.refs_10_
  67.4 1.8 %collective-permute-start.21 = (bf16[3,128,128]{2,1,0:T(8,128)(2,1)S(1)}, bf16[3,128,128]{2,1,0:T(8,128)(2,1)S(1)}, u32[]{:S(2)}, u32[]{:S(2)}) collective-permute-start(bf16[3,128,128]{2,1,0:T(8,128)(2,1)S(1)} %get-tuple-element.50), channel_id=1, source_target_pairs={{0,7},{1,6},{2,5},{3,4},{4,3},{5,2},{6,1},{7,0},{8,15},{9,14},{10,... | collective-permute-start | bytes 294920 | tf_op jit(solution)/shard_map/ppermute | solution.py:18
  69.2 0.0 collective-permute-done.17.refs_11_
  69.2 0.1 collective-permute-done.18.refs_12_
  69.3 7.5 %collective-permute-done.19.refs_13_ = bf16[3,128,128]{2,1,0:T(8,128)(2,1)S(1)} collective-permute-done((bf16[3,128,128]{2,1,0:T(8,128)(2,1)S(1)}, bf16[3,128,128]{2,1,0:T(8,128)(2,1)S(1)}, u32[]{:S(2)}, u32[]{:S(2)}) %collective-permute-start.19) | collective-permute-done | bytes 98336 | tf_op jit(solution)/shard_map/ppermute | solution.py:18
  76.9 4.7 %collective-permute-done.20.refs_14_ = bf16[3,128,128]{2,1,0:T(8,128)(2,1)S(1)} collective-permute-done((bf16[3,128,128]{2,1,0:T(8,128)(2,1)S(1)}, bf16[3,128,128]{2,1,0:T(8,128)(2,1)S(1)}, u32[]{:S(2)}, u32[]{:S(2)}) %collective-permute-start.20) | collective-permute-done | bytes 98336 | tf_op jit(solution)/shard_map/ppermute | solution.py:18
  81.5 2.1 %collective-permute-done.21.refs_15_ = bf16[3,128,128]{2,1,0:T(8,128)(2,1)S(1)} collective-permute-done((bf16[3,128,128]{2,1,0:T(8,128)(2,1)S(1)}, bf16[3,128,128]{2,1,0:T(8,128)(2,1)S(1)}, u32[]{:S(2)}, u32[]{:S(2)}) %collective-permute-start.21) | collective-permute-done | bytes 98336 | tf_op jit(solution)/shard_map/ppermute | solution.py:18
  83.7 1.3 %assembled.1 = bf16[3,2048,128]{2,1,0:T(8,128)(2,1)} custom-call(bf16[3,128,128]{2,1,0:T(8,128)(2,1)S(1)} %get-tuple-element.34.refs_0_, bf16[3,128,128]{2,1,0:T(8,128)(2,1)S(1)} %collective-permute-done.6.refs_1_, bf16[3,128,128]{2,1,0:T(8,128)(2,1)S(1)} %collective-permute-done.7.refs_2_, bf16[3,128,128]{2,1,0:T(8,128)(2,1)S(1)} %collective-permute-done.8.refs_3_, ...), custom_call_target="tpu_custom_call" | custom-call | tf_op jit(solution)/shard_map/assembled/pallas_call | solution.py:298
  (3 shorter events, 0.1 us)
Async XLA Ops:
  0.0 4.1 %copy-start = (bf16[3,512]{1,0:T(4,128)(2,1)S(1)}, bf16[3,512]{1,0:T(4,128)(2,1)}, u32[]{:S(2)}) copy-start(bf16[3,512]{1,0:T(4,128)(2,1)} %param.3) | copy-start | bytes 9220
  0.0 15.4 %collective-permute-start.1 = (bf16[1024,2048]{1,0:T(8,128)(2,1)}, bf16[1024,2048]{1,0:T(8,128)(2,1)}, u32[]{:S(2)}, u32[]{:S(2)}) collective-permute-start(bf16[1024,2048]{1,0:T(8,128)(2,1)} %near_ref.1), channel_id=1, source_target_pairs={{0,8},{8,0},{16,24},{24,16},{1,9},{9,1},{17,25},{25,17},{2,10},{10... | collective-permute-start | bytes 12582920 | tf_op jit(solution)/shard_map/ppermute | solution.py:18
  1.8 13.6 %collective-permute-start.2 = (bf16[128,2048]{1,0:T(8,128)(2,1)S(1)}, bf16[128,2048]{1,0:T(8,128)(2,1)S(1)}, u32[]{:S(2)}, u32[]{:S(2)}) collective-permute-start(bf16[128,2048]{1,0:T(8,128)(2,1)S(1)} %constant_dynamic-slice_fusion.1), channel_id=1, source_target_pairs={{0,16},{8,24},{16,0},{24,8},{1,17},{9,25},{17,1},{25,9},{2,18},{10... | collective-permute-start | bytes 1572872 | tf_op jit(solution)/shard_map/ppermute | solution.py:18
  4.1 2.8 %collective-permute-start = (bf16[1,3,512]{2,1,0:T(4,128)(2,1)S(1)}, bf16[1,3,512]{2,1,0:T(4,128)(2,1)S(1)}, u32[]{:S(2)}, u32[]{:S(2)}) collective-permute-start(bf16[1,3,512]{2,1,0:T(4,128)(2,1)S(1)} %bitcast.2), channel_id=1, source_target_pairs={{0,1},{1,0},{2,3},{3,2},{4,5},{5,4},{6,7},{7,6},{8,9},{9,8},{10,11... | collective-permute-start | bytes 9224 | tf_op jit(solution)/shard_map/ppermute | solution.py:18
  7.0 2.9 %collective-permute-start.3 = (bf16[2,3,512]{2,1,0:T(4,128)(2,1)S(1)}, bf16[2,3,512]{2,1,0:T(4,128)(2,1)S(1)}, u32[]{:S(2)}, u32[]{:S(2)}) collective-permute-start(bf16[2,3,512]{2,1,0:T(4,128)(2,1)S(1)} %pad_maximum_fusion.2), channel_id=1, source_target_pairs={{0,2},{1,3},{2,0},{3,1},{4,6},{5,7},{6,4},{7,5},{8,10},{9,11},{10,... | collective-permute-start | bytes 18440 | tf_op jit(solution)/shard_map/ppermute | solution.py:18
  8.3 18.3 %collective-permute-start.13 = (bf16[128,2048]{1,0:T(8,128)(2,1)S(1)}, bf16[128,2048]{1,0:T(8,128)(2,1)S(1)}, u32[]{:S(2)}, u32[]{:S(2)}) collective-permute-start(bf16[128,2048]{1,0:T(8,128)(2,1)S(1)} %constant_dynamic-slice_fusion), channel_id=1, source_target_pairs={{0,16},{8,24},{16,0},{24,8},{1,17},{9,25},{17,1},{25,9},{2,18},{10... | collective-permute-start | bytes 1572872 | tf_op jit(solution)/shard_map/ppermute | solution.py:18
  9.9 12.9 %collective-permute-start.5 = (bf16[4,3,512]{2,1,0:T(4,128)(2,1)S(1)}, bf16[4,3,512]{2,1,0:T(4,128)(2,1)S(1)}, u32[]{:S(2)}, u32[]{:S(2)}) collective-permute-start(bf16[4,3,512]{2,1,0:T(4,128)(2,1)S(1)} %pad_maximum_fusion.1), channel_id=1, source_target_pairs={{0,4},{1,5},{2,6},{3,7},{4,0},{5,1},{6,2},{7,3},{8,12},{9,13},{10,... | collective-permute-start | bytes 36872 | tf_op jit(solution)/shard_map/ppermute | solution.py:18
  21.5 16.4 %collective-permute-start.4 = (bf16[128,2048]{1,0:T(8,128)(2,1)S(1)}, bf16[128,2048]{1,0:T(8,128)(2,1)S(1)}, u32[]{:S(2)}, u32[]{:S(2)}) collective-permute-start(bf16[128,2048]{1,0:T(8,128)(2,1)S(1)} %partial_rows.2), channel_id=1, source_target_pairs={{0,16},{8,24},{16,0},{24,8},{1,17},{9,25},{17,1},{25,9},{2,18},{10... | collective-permute-start | bytes 1572872 | tf_op jit(solution)/shard_map/ppermute | solution.py:18
  27.9 21.2 %collective-permute-start.14 = (bf16[128,2048]{1,0:T(8,128)(2,1)S(1)}, bf16[128,2048]{1,0:T(8,128)(2,1)S(1)}, u32[]{:S(2)}, u32[]{:S(2)}) collective-permute-start(bf16[128,2048]{1,0:T(8,128)(2,1)S(1)} %partial_rows.3), channel_id=1, source_target_pairs={{0,16},{8,24},{16,0},{24,8},{1,17},{9,25},{17,1},{25,9},{2,18},{10... | collective-permute-start | bytes 1572872 | tf_op jit(solution)/shard_map/ppermute | solution.py:18
  39.9 12.3 %collective-permute-start.6 = (bf16[3,128,128]{2,1,0:T(8,128)(2,1)S(1)}, bf16[3,128,128]{2,1,0:T(8,128)(2,1)S(1)}, u32[]{:S(2)}, u32[]{:S(2)}) collective-permute-start(bf16[3,128,128]{2,1,0:T(8,128)(2,1)S(1)} %get-tuple-element.35), channel_id=1, source_target_pairs={{0,1},{1,0},{2,3},{3,2},{4,5},{5,4},{6,7},{7,6},{8,9},{9,8},{10,11... | collective-permute-start | bytes 294920 | tf_op jit(solution)/shard_map/ppermute | solution.py:18
  41.2 13.4 %collective-permute-start.7 = (bf16[3,128,128]{2,1,0:T(8,128)(2,1)S(1)}, bf16[3,128,128]{2,1,0:T(8,128)(2,1)S(1)}, u32[]{:S(2)}, u32[]{:S(2)}) collective-permute-start(bf16[3,128,128]{2,1,0:T(8,128)(2,1)S(1)} %get-tuple-element.36), channel_id=1, source_target_pairs={{0,2},{1,3},{2,0},{3,1},{4,6},{5,7},{6,4},{7,5},{8,10},{9,11},{10,... | collective-permute-start | bytes 294920 | tf_op jit(solution)/shard_map/ppermute | solution.py:18
  42.5 12.2 %collective-permute-start.8 = (bf16[3,128,128]{2,1,0:T(8,128)(2,1)S(1)}, bf16[3,128,128]{2,1,0:T(8,128)(2,1)S(1)}, u32[]{:S(2)}, u32[]{:S(2)}) collective-permute-start(bf16[3,128,128]{2,1,0:T(8,128)(2,1)S(1)} %get-tuple-element.37), channel_id=1, source_target_pairs={{0,3},{1,2},{2,1},{3,0},{4,7},{5,6},{6,5},{7,4},{8,11},{9,10},{10,... | collective-permute-start | bytes 294920 | tf_op jit(solution)/shard_map/ppermute | solution.py:18
  42.6 13.3 %collective-permute-start.9 = (bf16[3,128,128]{2,1,0:T(8,128)(2,1)S(1)}, bf16[3,128,128]{2,1,0:T(8,128)(2,1)S(1)}, u32[]{:S(2)}, u32[]{:S(2)}) collective-permute-start(bf16[3,128,128]{2,1,0:T(8,128)(2,1)S(1)} %get-tuple-element.38), channel_id=1, source_target_pairs={{0,4},{1,5},{2,6},{3,7},{4,0},{5,1},{6,2},{7,3},{8,12},{9,13},{10,... | collective-permute-start | bytes 294920 | tf_op jit(solution)/shard_map/ppermute | solution.py:18
  49.1 8.9 %collective-permute-start.10 = (bf16[3,128,128]{2,1,0:T(8,128)(2,1)S(1)}, bf16[3,128,128]{2,1,0:T(8,128)(2,1)S(1)}, u32[]{:S(2)}, u32[]{:S(2)}) collective-permute-start(bf16[3,128,128]{2,1,0:T(8,128)(2,1)S(1)} %get-tuple-element.39), channel_id=1, source_target_pairs={{0,5},{1,4},{2,7},{3,6},{4,1},{5,0},{6,3},{7,2},{8,13},{9,12},{10,... | collective-permute-start | bytes 294920 | tf_op jit(solution)/shard_map/ppermute | solution.py:18
  52.2 11.8 %collective-permute-start.11 = (bf16[3,128,128]{2,1,0:T(8,128)(2,1)S(1)}, bf16[3,128,128]{2,1,0:T(8,128)(2,1)S(1)}, u32[]{:S(2)}, u32[]{:S(2)}) collective-permute-start(bf16[3,128,128]{2,1,0:T(8,128)(2,1)S(1)} %get-tuple-element.40), channel_id=1, source_target_pairs={{0,6},{1,7},{2,4},{3,5},{4,2},{5,3},{6,0},{7,1},{8,14},{9,15},{10,... | collective-permute-start | bytes 294920 | tf_op jit(solution)/shard_map/ppermute | solution.py:18
  54.6 12.7 %collective-permute-start.12 = (bf16[3,128,128]{2,1,0:T(8,128)(2,1)S(1)}, bf16[3,128,128]{2,1,0:T(8,128)(2,1)S(1)}, u32[]{:S(2)}, u32[]{:S(2)}) collective-permute-start(bf16[3,128,128]{2,1,0:T(8,128)(2,1)S(1)} %get-tuple-element.41), channel_id=1, source_target_pairs={{0,7},{1,6},{2,5},{3,4},{4,3},{5,2},{6,1},{7,0},{8,15},{9,14},{10,... | collective-permute-start | bytes 294920 | tf_op jit(solution)/shard_map/ppermute | solution.py:18
  54.7 12.7 %collective-permute-start.15 = (bf16[3,128,128]{2,1,0:T(8,128)(2,1)S(1)}, bf16[3,128,128]{2,1,0:T(8,128)(2,1)S(1)}, u32[]{:S(2)}, u32[]{:S(2)}) collective-permute-start(bf16[3,128,128]{2,1,0:T(8,128)(2,1)S(1)} %get-tuple-element.44), channel_id=1, source_target_pairs={{0,1},{1,0},{2,3},{3,2},{4,5},{5,4},{6,7},{7,6},{8,9},{9,8},{10,11... | collective-permute-start | bytes 294920 | tf_op jit(solution)/shard_map/ppermute | solution.py:18
  55.9 11.5 %collective-permute-start.16 = (bf16[3,128,128]{2,1,0:T(8,128)(2,1)S(1)}, bf16[3,128,128]{2,1,0:T(8,128)(2,1)S(1)}, u32[]{:S(2)}, u32[]{:S(2)}) collective-permute-start(bf16[3,128,128]{2,1,0:T(8,128)(2,1)S(1)} %get-tuple-element.45), channel_id=1, source_target_pairs={{0,2},{1,3},{2,0},{3,1},{4,6},{5,7},{6,4},{7,5},{8,10},{9,11},{10,... | collective-permute-start | bytes 294920 | tf_op jit(solution)/shard_map/ppermute | solution.py:18
  58.0 11.2 %collective-permute-start.17 = (bf16[3,128,128]{2,1,0:T(8,128)(2,1)S(1)}, bf16[3,128,128]{2,1,0:T(8,128)(2,1)S(1)}, u32[]{:S(2)}, u32[]{:S(2)}) collective-permute-start(bf16[3,128,128]{2,1,0:T(8,128)(2,1)S(1)} %get-tuple-element.46), channel_id=1, source_target_pairs={{0,3},{1,2},{2,1},{3,0},{4,7},{5,6},{6,5},{7,4},{8,11},{9,10},{10,... | collective-permute-start | bytes 294920 | tf_op jit(solution)/shard_map/ppermute | solution.py:18
  64.0 5.4 %collective-permute-start.18 = (bf16[3,128,128]{2,1,0:T(8,128)(2,1)S(1)}, bf16[3,128,128]{2,1,0:T(8,128)(2,1)S(1)}, u32[]{:S(2)}, u32[]{:S(2)}) collective-permute-start(bf16[3,128,128]{2,1,0:T(8,128)(2,1)S(1)} %get-tuple-element.47), channel_id=1, source_target_pairs={{0,4},{1,5},{2,6},{3,7},{4,0},{5,1},{6,2},{7,3},{8,12},{9,13},{10,... | collective-permute-start | bytes 294920 | tf_op jit(solution)/shard_map/ppermute | solution.py:18
  67.4 9.5 %collective-permute-start.19 = (bf16[3,128,128]{2,1,0:T(8,128)(2,1)S(1)}, bf16[3,128,128]{2,1,0:T(8,128)(2,1)S(1)}, u32[]{:S(2)}, u32[]{:S(2)}) collective-permute-start(bf16[3,128,128]{2,1,0:T(8,128)(2,1)S(1)} %get-tuple-element.48), channel_id=1, source_target_pairs={{0,5},{1,4},{2,7},{3,6},{4,1},{5,0},{6,3},{7,2},{8,13},{9,12},{10,... | collective-permute-start | bytes 294920 | tf_op jit(solution)/shard_map/ppermute | solution.py:18
  67.4 14.2 %collective-permute-start.20 = (bf16[3,128,128]{2,1,0:T(8,128)(2,1)S(1)}, bf16[3,128,128]{2,1,0:T(8,128)(2,1)S(1)}, u32[]{:S(2)}, u32[]{:S(2)}) collective-permute-start(bf16[3,128,128]{2,1,0:T(8,128)(2,1)S(1)} %get-tuple-element.49), channel_id=1, source_target_pairs={{0,6},{1,7},{2,4},{3,5},{4,2},{5,3},{6,0},{7,1},{8,14},{9,15},{10,... | collective-permute-start | bytes 294920 | tf_op jit(solution)/shard_map/ppermute | solution.py:18
  67.4 16.3 %collective-permute-start.21 = (bf16[3,128,128]{2,1,0:T(8,128)(2,1)S(1)}, bf16[3,128,128]{2,1,0:T(8,128)(2,1)S(1)}, u32[]{:S(2)}, u32[]{:S(2)}) collective-permute-start(bf16[3,128,128]{2,1,0:T(8,128)(2,1)S(1)} %get-tuple-element.50), channel_id=1, source_target_pairs={{0,7},{1,6},{2,5},{3,4},{4,3},{5,2},{6,1},{7,0},{8,15},{9,14},{10,... | collective-permute-start | bytes 294920 | tf_op jit(solution)/shard_map/ppermute | solution.py:18

commit v3 on v2

--- a/solution.py
+++ b/solution.py
@@ -11,7 +11,8 @@
 LANES = 128
 DEPTH = 4 * LANES
 MIB = 1024 * 1024
-GROUPS = [[128], [128]]
+COST = pl.CostEstimate(flops=1, bytes_accessed=1, transcendentals=0)
+SIZES = [64, 64, 64, 64]
 
 
 def flipped(block, axis, mask):
@@ -34,13 +35,8 @@
     return [pl.BlockSpec(memory_space=pltpu.VMEM)] * count
 
 
-def strain_doublings(strain):
-    steps = [strain[None]]
-    mask = 1
-    while mask < lax.axis_size("tm"):
-        steps.append(jnp.concatenate([steps[-1], flipped(steps[-1], "tm", mask)], axis=0))
-        mask *= 2
-    return steps
+def doubled(blocks):
+    return jnp.concatenate([blocks, flipped(blocks, "tm", blocks.shape[0])], axis=0)
 
 
 def shifted(tile, distance):
@@ -91,6 +87,7 @@
             pltpu.VMEM((count, detectors, samples), jnp.float32),
             pltpu.VMEM((detectors, 2 * STRIDE, length), jnp.float32),
         ],
+        cost_estimate=COST,
         compiler_params=pltpu.CompilerParams(vmem_limit_bytes=16 * MIB),
         name="hankel",
     )(in_vmem(blocks))
@@ -126,6 +123,7 @@
         in_specs=[pl.BlockSpec((1, 2 * STRIDE, length), lambda d: (d, 0, 0))],
         out_specs=pl.BlockSpec((1, DEPTH, width), lambda d: (d, 0, 0)),
         out_shape=jax.ShapeDtypeStruct((detectors, DEPTH, width), jnp.bfloat16),
+        cost_estimate=COST,
         compiler_params=pltpu.CompilerParams(vmem_limit_bytes=24 * MIB),
         name="long_hankel",
     )(rows)
@@ -182,9 +180,7 @@
             pltpu.VMEM((own_rows, 2 * half), jnp.bfloat16),
             pltpu.SemaphoreType.DMA((10,)),
         ],
-        cost_estimate=pl.CostEstimate(
-            flops=4 * own_rows * half * taps, bytes_accessed=8 * half * taps, transcendentals=0
-        ),
+        cost_estimate=COST,
         compiler_params=pltpu.CompilerParams(vmem_limit_bytes=20 * MIB),
         name="staged",
     )(in_hbm(coefficients), in_hbm(near), in_hbm(far))
@@ -210,100 +206,117 @@
         in_specs=whole_in_vmem(2),
         out_specs=pl.BlockSpec(memory_space=pltpu.VMEM),
         out_shape=jax.ShapeDtypeStruct((count, taps), jnp.bfloat16),
-        cost_estimate=pl.CostEstimate(
-            flops=2 * count * depth * taps, bytes_accessed=2 * depth * taps, transcendentals=0
-        ),
+        cost_estimate=COST,
         compiler_params=pltpu.CompilerParams(vmem_limit_bytes=16 * MIB),
         name="partial_rows",
     )(in_vmem(rows), in_vmem(filters))
 
 
-def rounded_sum(own, others):
-    other = jnp.concatenate([ref[...] for ref in others], axis=0)
-    return (own + other.astype(jnp.float32)).astype(jnp.bfloat16)
-
-
-def series_kernel(start, parts, own_ref, *refs):
+def series_kernel(start, parts, far, targets, own_ref, *refs):
     others, hankel_ref, outs, scratch = refs[:parts], refs[parts], refs[parts + 1 : -1], refs[-1]
     detectors = hankel_ref.shape[0]
     rows, times = scratch.shape
     taps = own_ref.shape[1]
-    here = times // len(outs)
+    here = outs[0].shape[-1]
+    near = times // here
     me = lax.axis_index("tm")
-    weights = rounded_sum(own_ref[start : start + rows], others)
+    half = me // near
+    first = (1 - half if far else half) * times
+    other = jnp.concatenate([ref[...] for ref in others], axis=0)
+    weights = (own_ref[start : start + rows] + other.astype(jnp.float32)).astype(jnp.bfloat16)
     for d in range(detectors):
         total = None
         for q in range(taps // DEPTH):
+            columns = pl.ds(pl.multiple_of(first + q * LANES, LANES), times)
             term = jnp.dot(
                 weights[:, q * DEPTH : (q + 1) * DEPTH],
-                hankel_ref[d, :, q * LANES : q * LANES + times],
+                hankel_ref[d, :, columns],
                 preferred_element_type=jnp.float32,
             )
             total = term if total is None else total + term
         scratch[...] = total.astype(jnp.bfloat16)
-        for k, out in enumerate(outs):
-            out[d] = scratch[:, pl.ds(pl.multiple_of((me ^ k) * here, LANES), here)]
-
-
-def series(own, start, others, matrix, count, here):
+        for out, target in zip(outs, targets):
+            for s, k in enumerate(target):
+                at = pl.multiple_of(lax.rem(me ^ k, near) * here, LANES)
+                out[s, d] = scratch[:, pl.ds(at, here)]
+
+
+def series(own, start, others, matrix, here, targets):
     taps = own.shape[1]
     rows = sum(part.shape[0] for part in others)
-    detectors, depth, width = matrix.shape
-    return pl.pallas_call(
-        functools.partial(series_kernel, start, len(others)),
+    detectors = matrix.shape[0]
+    near = 4
+    far = targets[0][0] >= near
+    shapes = [(len(target), detectors, rows, here) for target in targets]
+    return pl.pallas_call(
+        functools.partial(series_kernel, start, len(others), far, targets),
         in_specs=whole_in_vmem(2 + len(others)),
-        out_specs=whole_in_vmem(count),
-        out_shape=[jax.ShapeDtypeStruct((detectors, rows, here), jnp.bfloat16)] * count,
-        scratch_shapes=[pltpu.VMEM((rows, count * here), jnp.bfloat16)],
-        cost_estimate=pl.CostEstimate(
-            flops=2 * rows * taps * detectors * count * here,
-            bytes_accessed=2 * detectors * depth * width,
-            transcendentals=0,
-        ),
+        out_specs=whole_in_vmem(len(targets)),
+        out_shape=[jax.ShapeDtypeStruct(shape, jnp.bfloat16) for shape in shapes],
+        scratch_shapes=[pltpu.VMEM((rows, near * here), jnp.bfloat16)],
+        cost_estimate=COST,
         compiler_params=pltpu.CompilerParams(vmem_limit_bytes=16 * MIB),
         name="series",
     )(in_vmem(own), *[in_vmem(part) for part in others], in_vmem(matrix))
 
 
-def assembling_kernel(starts, own_rows, *refs):
+def second_halves_kernel(counts, *refs):
+    ins, out_ref = list(refs[:-1]), refs[-1]
+    for k, count in enumerate(counts):
+        start = 0
+        for ref in ins[:count]:
+            rows = ref.shape[2]
+            out_ref[k, :, start : start + rows] = ref[1]
+            start += rows
+        ins = ins[count:]
+
+
+def second_halves(columns):
+    detectors, _, here = columns[0][0].shape[1:]
+    rows = sum(pair.shape[2] for pair in columns[0])
+    pairs = [pair for column in columns for pair in column]
+    return pl.pallas_call(
+        functools.partial(second_halves_kernel, [len(column) for column in columns]),
+        in_specs=whole_in_vmem(len(pairs)),
+        out_specs=pl.BlockSpec(memory_space=pltpu.VMEM),
+        out_shape=jax.ShapeDtypeStruct((len(columns), detectors, rows, here), jnp.bfloat16),
+        cost_estimate=COST,
+        compiler_params=pltpu.CompilerParams(vmem_limit_bytes=16 * MIB),
+        name="second_halves",
+    )(*[in_vmem(pair) for pair in pairs])
+
+
+def assembling_kernel(places, own_rows, *refs):
     blocks, out_ref, semaphores = refs[:-2], refs[-2], refs[-1]
-    count = len(blocks) // len(starts)
     me = lax.axis_index("tm")
     copies = []
-    for g, start in enumerate(starts):
-        for k in range(count):
-            block = blocks[g * count + k]
-            at = pl.multiple_of((me ^ k) * own_rows + start, 16)
-            copies.append(
-                pltpu.make_async_copy(
-                    block,
-                    out_ref.at[:, pl.ds(at, block.shape[1]), :],
-                    semaphores.at[g * count + k],
-                )
+    for i, (operand, index, k, start) in enumerate(places):
+        block = blocks[operand].at[index]
+        rows = block.shape[1]
+        at = pl.multiple_of((me ^ k) * own_rows + start, 16)
+        copies.append(
+            pltpu.make_async_copy(
+                block, out_ref.at[:, pl.ds(at, rows), :], semaphores.at[i]
             )
+        )
     for copy in copies:
         copy.start()
     for copy in copies:
         copy.wait()
 
 
-def assembled(groups, own_rows):
-    count = len(groups[0])
-    detectors, _, here = groups[0][0].shape
-    starts, start = [], 0
-    for group in groups:
-        starts.append(start)
-        start += group[0].shape[1]
-    blocks = [block for group in groups for block in group]
-    return pl.pallas_call(
-        functools.partial(assembling_kernel, starts, own_rows),
-        in_specs=whole_in_vmem(len(blocks)),
+def assembled(operands, places, count, own_rows):
+    detectors, _, here = operands[0].shape[-3:]
+    return pl.pallas_call(
+        functools.partial(assembling_kernel, places, own_rows),
+        in_specs=whole_in_vmem(len(operands)),
         out_specs=pl.BlockSpec(memory_space=pl.ANY),
         out_shape=jax.ShapeDtypeStruct((detectors, count * own_rows, here), jnp.bfloat16),
-        scratch_shapes=[pltpu.SemaphoreType.DMA((len(blocks),))],
+        scratch_shapes=[pltpu.SemaphoreType.DMA((len(places),))],
+        cost_estimate=COST,
         compiler_params=pltpu.CompilerParams(vmem_limit_bytes=16 * MIB),
         name="assembled",
-    )(*[in_vmem(block) for block in blocks])
+    )(*[in_vmem(operand) for operand in operands])
 
 
 def long_series_kernel(weights_ref, hankel_ref, out_ref):
@@ -334,6 +347,7 @@
         ],
         out_specs=pl.BlockSpec((2, 1, rows, here), lambda d, n: (n, d, 0, 0)),
         out_shape=jax.ShapeDtypeStruct((count, detectors, rows, here), jnp.bfloat16),
+        cost_estimate=COST,
         compiler_params=pltpu.CompilerParams(vmem_limit_bytes=32 * MIB),
         name="long_series",
     )(weights, matrix)
@@ -348,42 +362,75 @@
     me = lax.axis_index("tm")
     group = lax.axis_index("basis")
     short = count == 8 and here == LANES
-    groups = GROUPS if short and own_rows == 256 else [[own_rows]]
-    sizes = [size for part in groups for size in part]
-    starts = [sum(sizes[:c]) for c in range(len(sizes))]
-    chunks = range(len(sizes))
-
-    at = (group // 2 ^ 1) * (2 * filters)
-    cuts = []
-    for c in chunks:
-        source = after(coefficients, cuts[-1]) if cuts else coefficients
-        cuts.append(lax.dynamic_slice(source, (starts[c], at), (sizes[c], 2 * filters)))
-    asked = [flipped(cut, "basis", 2) for cut in cuts]
+
+    def theirs(start, rows, *earlier):
+        source = after(coefficients, *earlier) if earlier else coefficients
+        at = (group // 2 ^ 1) * (2 * filters)
+        return lax.dynamic_slice(source, (start, at), (rows, 2 * filters))
+
     sibling = flipped(basis_filters, "basis", 1)
-    if short:
-        steps = strain_doublings(after(strain, cuts[-1]))
-        chip_filters, own = staged(after(coefficients, steps[1]), basis_filters, sibling)
-        matrix = hankel(steps[-1], taps)
-        asked[0] = after(asked[0], steps[2])
-        asked[-1] = after(asked[-1], matrix)
-    else:
+    if not (short and own_rows == 256):
         chip_filters, own = staged(coefficients, basis_filters, sibling)
+        answer = partial_rows(flipped(theirs(0, own_rows), "basis", 2), chip_filters)
+        other = flipped(answer, "basis", 2).astype(jnp.float32)
         matrix = long_hankel(strain, taps, count * here)
-    other = [flipped(partial_rows(rows, chip_filters), "basis", 2) for rows in asked]
-
-    if not short:
-        weights = (own + other[0].astype(jnp.float32)).astype(jnp.bfloat16)
-        blocks = long_series(weights, matrix, count, here)
+        blocks = long_series((own + other).astype(jnp.bfloat16), matrix, count, here)
         arrived = lax.all_to_all(blocks, "tm", split_axis=0, concat_axis=0, tiled=True)
         return arrived.transpose(0, 2, 1, 3).reshape(count * own_rows, detectors, here)
 
-    blocks = []
-    c = 0
-    for part in groups:
-        blocks.append(series(own, starts[c], other[c : c + len(part)], matrix, count, here))
-        c += len(part)
-    arrived = [[flipped(b[k], "tm", k) if k else b[k] for k in range(count)] for b in blocks]
-    return assembled(arrived, own_rows).transpose(1, 0, 2)
+    starts = [sum(SIZES[:g]) for g in range(len(SIZES))]
+    cuts = [theirs(0, SIZES[0])]
+    two = doubled(after(strain, cuts[0])[None])
+    cuts.append(theirs(starts[1], SIZES[1], two))
+    chip_filters, own = staged(after(coefficients, cuts[1]), basis_filters, sibling)
+    cuts.append(theirs(starts[2], SIZES[2], own))
+    waiting = [flipped(cut, "basis", 2) for cut in cuts]
+
+    def answered(c, *earlier):
+        answer = partial_rows(after(waiting[c], *earlier), chip_filters)
+        return answer, flipped(answer, "basis", 2)
+
+    four = doubled(after(two, own))
+    answer_0, other_0 = answered(0, waiting[1], four)
+    eight = doubled(after(four, answer_0))
+    waiting.append(flipped(theirs(starts[3], SIZES[3], answer_0), "basis", 2))
+    answer_1, other_1 = answered(1, waiting[2], answer_0)
+    matrix = hankel(after(eight, answer_1), taps)
+    answer_2, other_2 = answered(2, matrix)
+
+    def along_z(pair, k):
+        return flipped(pair, "tm", 2 * k)
+
+    operands, places = [], []
+
+    def place(operand, sources, start):
+        places.extend((len(operands), i, k, start) for i, k in enumerate(sources))
+        operands.append(operand)
+
+    far_a = series(own, starts[0], [other_0], matrix, here, [(6, 7), (4, 5)])
+    sent_a = [along_z(far_a[0], 3), along_z(far_a[1], 2)]
+    _, other_3 = answered(3, answer_2, *sent_a)
+    far_b = series(own, starts[1], [other_1], matrix, here, [(6, 7), (4, 5)])
+    sent_b = [along_z(far_b[0], 3), along_z(far_b[1], 2)]
+    rest = [after(other_2, sent_b[0], *sent_a), other_3]
+    far_c = series(own, starts[2], rest, matrix, here, [(6,), (7,), (4,), (5,)])
+    sent_c = [flipped(block, "tm", k) for block, k in zip(far_c, (6, 7, 4, 5))]
+    rest = [after(other_0, far_c[0]), other_1, other_2, other_3]
+    near = series(own, starts[0], rest, matrix, here, [(2,), (3,), (1,), (0,)])
+    near = list(near)
+    near[1], near[2] = after(near[1], sent_c[1]), after(near[2], sent_c[1])
+    near = [flipped(block, "tm", k) if k else block for block, k in zip(near, (2, 3, 1, 0))]
+    held = after(sent_a[0], near[3])
+    halves = second_halves([[sent_a[1], sent_b[1]], [held, sent_b[0]]])
+    for i, k in enumerate((6, 4)):
+        place(sent_a[i], [k], starts[0])
+        place(sent_b[i], [k], starts[1])
+    for block, k in zip(sent_c, (6, 7, 4, 5)):
+        place(block, [k], starts[2])
+    place(flipped(halves, "tm", 1), [5, 7], starts[0])
+    for block, k in zip(near, (2, 3, 1, 0)):
+        place(block, [k], starts[0])
+    return assembled(operands, places, count, own_rows).transpose(1, 0, 2)
 
 
 def solution(mesh):

time: 85.1 us -> 78.5 us (0.922)
  the two profiles are of different devices: /device:TPU:17 before, /device:TPU:0 now
where the time goes in v3:
time: 78.5 us; the launch traced here: 78.3 us
  starting transfers between devices  38.4 us (49%)
  Pallas kernels  20.3 us (26%)
  waiting for transfers between devices  14.9 us (19%)
  local copies, waits for them, and re-layouts  3.89 us (5%)
    ppermute x24, starting transfers between devices, flipped(): lax.ppermute(block, axis, [(i, i ^ mask) for i in range(lax.axis_size(axi...  38.4 us
    ppermute x24, waiting for transfers between devices, flipped(): lax.ppermute(block, axis, [(i, i ^ mask) for i in range(lax.axis_size(axi...  14.9 us
    pallas_call x4, Pallas kernels, partial_rows(): pl.pallas_call(partial_kernel, in_specs=whole_in_vmem(2), out_specs=pl.Bl...  6.25 us
    pallas_call x4, Pallas kernels, series(): pl.pallas_call(functools.partial(series_kernel, start, len(others), far,...  5.78 us
    pallas_call x1, Pallas kernels, staged(): pl.pallas_call(staging_kernel, in_specs=[pl.BlockSpec(memory_space=pl.ANY...  4.83 us
    dynamic_slice x4, local copies, waits for them, and re-layouts, theirs(): return lax.dynamic_slice(source, (start, at), (rows, 2 * filters))  3.88 us
    pallas_call x1, Pallas kernels, hankel(): pl.pallas_call(hankel_kernel, in_specs=whole_in_vmem(1), out_specs=pl.Blo...  2.11 us
  transfers between devices with their start and end apart: 24, of which 9 were waited for; matrix products, arithmetic and copies ran while one was open for 6% of the time, Pallas kernels for 24%

profile of v3, /device:TPU:0, one launch (start us, length us, event | category | flops | bytes accessed | tf_op | source)
XLA Modules:
  0.0 78.3 jit_solution(12495678405489418591)
XLA Ops:
  0.0 0.5 collective-permute-start.1
  0.5 1.0 %constant_dynamic-slice_fusion.3 = bf16[64,2048]{1,0:T(8,128)(2,1)S(1)} fusion(bf16[256,4096]{1,0:T(8,128)(2,1)} %coefficients_ref, s32[]{:T(128)S(6)} %select_n.15), kind=kLoop, calls=%fused_computation.7 | loop fusion | bytes 524292 | tf_op jit(solution)/shard_map/dynamic_slice | solution.py:369
  1.4 2.6 %collective-permute-start = (bf16[1,3,512]{2,1,0:T(4,128)(2,1)}, bf16[1,3,512]{2,1,0:T(4,128)(2,1)S(1)}, u32[]{:S(2)}, u32[]{:S(2)}) collective-permute-start(bf16[1,3,512]{2,1,0:T(4,128)(2,1)} %bitcast.2), channel_id=1, source_target_pairs={{0,1},{1,0},{2,3},{3,2},{4,5},{5,4},{6,7},{7,6},{8,9},{9,8},{10,11... | collective-permute-start | bytes 9224 | tf_op jit(solution)/shard_map/ppermute | solution.py:19
  4.0 1.5 %collective-permute-start.2 = (bf16[64,2048]{1,0:T(8,128)(2,1)S(1)}, bf16[64,2048]{1,0:T(8,128)(2,1)S(1)}, u32[]{:S(2)}, u32[]{:S(2)}) collective-permute-start(bf16[64,2048]{1,0:T(8,128)(2,1)S(1)} %constant_dynamic-slice_fusion.3), channel_id=1, source_target_pairs={{0,16},{8,24},{16,0},{24,8},{1,17},{9,25},{17,1},{25,9},{2,18},{10... | collective-permute-start | bytes 786440 | tf_op jit(solution)/shard_map/ppermute | solution.py:19
  5.5 0.3 collective-permute-done
  5.8 0.7 pad_maximum_fusion.1
  6.5 1.0 %constant_dynamic-slice_fusion.2 = bf16[64,2048]{1,0:T(8,128)(2,1)S(1)} fusion(bf16[256,4096]{1,0:T(8,128)(2,1)} %coefficients_ref, s32[]{:T(128)S(6)} %select_n.15), kind=kLoop, calls=%fused_computation.6 | loop fusion | bytes 524292 | tf_op jit(solution)/shard_map/dynamic_slice | solution.py:369
  7.5 2.1 %collective-permute-start.3 = (bf16[64,2048]{1,0:T(8,128)(2,1)S(1)}, bf16[64,2048]{1,0:T(8,128)(2,1)S(1)}, u32[]{:S(2)}, u32[]{:S(2)}) collective-permute-start(bf16[64,2048]{1,0:T(8,128)(2,1)S(1)} %constant_dynamic-slice_fusion.2), channel_id=1, source_target_pairs={{0,16},{8,24},{16,0},{24,8},{1,17},{9,25},{17,1},{25,9},{2,18},{10... | collective-permute-start | bytes 786440 | tf_op jit(solution)/shard_map/ppermute | solution.py:19
  9.5 0.0 collective-permute-done.1.far_ref
  9.5 4.8 %staged.1 = (bf16[2048,2048]{1,0:T(8,128)(2,1)S(1)}, f32[256,2048]{1,0:T(8,128)S(1)}) custom-call(bf16[256,4096]{1,0:T(8,128)(2,1)} %coefficients_ref, bf16[1024,2048]{1,0:T(8,128)(2,1)} %near_ref.1, bf16[1024,2048]{1,0:T(8,128)(2,1)} %collective-permute-done.1.far_ref), custom_call_target="tpu_custom_call" | custom-call | flops 1 | bytes 1 | tf_op jit(solution)/shard_map/staged/pallas_call | solution.py:171
  14.4 1.6 %collective-permute-start.4 = (bf16[2,3,512]{2,1,0:T(4,128)(2,1)S(1)}, bf16[2,3,512]{2,1,0:T(4,128)(2,1)S(1)}, u32[]{:S(2)}, u32[]{:S(2)}) collective-permute-start(bf16[2,3,512]{2,1,0:T(4,128)(2,1)S(1)} %pad_maximum_fusion.1), channel_id=1, source_target_pairs={{0,2},{1,3},{2,0},{3,1},{4,6},{5,7},{6,4},{7,5},{8,10},{9,11},{10,... | collective-permute-start | bytes 18440 | tf_op jit(solution)/shard_map/ppermute | solution.py:19
  16.0 1.0 %constant_dynamic-slice_fusion.1 = bf16[64,2048]{1,0:T(8,128)(2,1)S(1)} fusion(bf16[256,4096]{1,0:T(8,128)(2,1)} %coefficients_ref, s32[]{:T(128)S(6)} %select_n.15), kind=kLoop, calls=%fused_computation.5 | loop fusion | bytes 524292 | tf_op jit(solution)/shard_map/dynamic_slice | solution.py:369
  17.0 0.9 %collective-permute-start.7 = (bf16[64,2048]{1,0:T(8,128)(2,1)S(1)}, bf16[64,2048]{1,0:T(8,128)(2,1)S(1)}, u32[]{:S(2)}, u32[]{:S(2)}) collective-permute-start(bf16[64,2048]{1,0:T(8,128)(2,1)S(1)} %constant_dynamic-slice_fusion.1), channel_id=1, source_target_pairs={{0,16},{8,24},{16,0},{24,8},{1,17},{9,25},{17,1},{25,9},{2,18},{10... | collective-permute-start | bytes 786440 | tf_op jit(solution)/shard_map/ppermute | solution.py:19
  17.9 0.2 collective-permute-done.4
  18.1 0.0 collective-permute-done.2.rows_ref
  18.1 0.0 collective-permute-done.3.rows_ref
  18.1 1.6 %partial_rows.4 = bf16[64,2048]{1,0:T(8,128)(2,1)S(1)} custom-call(bf16[64,2048]{1,0:T(8,128)(2,1)S(1)} %collective-permute-done.2.rows_ref, bf16[2048,2048]{1,0:T(8,128)(2,1)S(1)} %get-tuple-element.42.filters_ref), custom_call_target="tpu_custom_call" | custom-call | flops 1 | bytes 1 | tf_op jit(solution)/shard_map/partial_rows/pallas_call | solution.py:204
  19.7 1.5 %collective-permute-start.5 = (bf16[64,2048]{1,0:T(8,128)(2,1)S(1)}, bf16[64,2048]{1,0:T(8,128)(2,1)S(1)}, u32[]{:S(2)}, u32[]{:S(2)}) collective-permute-start(bf16[64,2048]{1,0:T(8,128)(2,1)S(1)} %partial_rows.4), channel_id=1, source_target_pairs={{0,16},{8,24},{16,0},{24,8},{1,17},{9,25},{17,1},{25,9},{2,18},{10... | collective-permute-start | bytes 786440 | tf_op jit(solution)/shard_map/ppermute | solution.py:19
  21.2 1.0 %constant_dynamic-slice_fusion = bf16[64,2048]{1,0:T(8,128)(2,1)S(1)} fusion(bf16[256,4096]{1,0:T(8,128)(2,1)} %coefficients_ref, s32[]{:T(128)S(6)} %select_n.15), kind=kLoop, calls=%fused_computation.4 | loop fusion | bytes 524292 | tf_op jit(solution)/shard_map/dynamic_slice | solution.py:369
  22.2 0.7 collective-permute-start.14
  22.8 2.6 %collective-permute-start.6 = (bf16[4,3,512]{2,1,0:T(4,128)(2,1)S(1)}, bf16[4,3,512]{2,1,0:T(4,128)(2,1)S(1)}, u32[]{:S(2)}, u32[]{:S(2)}) collective-permute-start(bf16[4,3,512]{2,1,0:T(4,128)(2,1)S(1)} %constant_dynamic-update-slice_fusion), channel_id=1, source_target_pairs={{0,4},{1,5},{2,6},{3,7},{4,0},{5,1},{6,2},{7,3},{8,12},{9,13},{10,... | collective-permute-start | bytes 36872 | tf_op jit(solution)/shard_map/ppermute | solution.py:19
  25.4 2.1 %collective-permute-done.6 = bf16[4,3,512]{2,1,0:T(4,128)(2,1)S(1)} collective-permute-done((bf16[4,3,512]{2,1,0:T(4,128)(2,1)S(1)}, bf16[4,3,512]{2,1,0:T(4,128)(2,1)S(1)}, u32[]{:S(2)}, u32[]{:S(2)}) %collective-permute-start.6) | collective-permute-done | bytes 12320 | tf_op jit(solution)/shard_map/ppermute | solution.py:19
  27.5 0.0 collective-permute-done.7.rows_ref
  27.5 1.6 %partial_rows.5 = bf16[64,2048]{1,0:T(8,128)(2,1)S(1)} custom-call(bf16[64,2048]{1,0:T(8,128)(2,1)S(1)} %collective-permute-done.3.rows_ref, bf16[2048,2048]{1,0:T(8,128)(2,1)S(1)} %get-tuple-element.42.filters_ref), custom_call_target="tpu_custom_call" | custom-call | flops 1 | bytes 1 | tf_op jit(solution)/shard_map/partial_rows/pallas_call | solution.py:204
  29.1 1.5 %collective-permute-start.9 = (bf16[64,2048]{1,0:T(8,128)(2,1)S(1)}, bf16[64,2048]{1,0:T(8,128)(2,1)S(1)}, u32[]{:S(2)}, u32[]{:S(2)}) collective-permute-start(bf16[64,2048]{1,0:T(8,128)(2,1)S(1)} %partial_rows.5), channel_id=1, source_target_pairs={{0,16},{8,24},{16,0},{24,8},{1,17},{9,25},{17,1},{25,9},{2,18},{10... | collective-permute-start | bytes 786440 | tf_op jit(solution)/shard_map/ppermute | solution.py:19
  30.6 2.1 %hankel.1.refs_1_.refs_2_.refs_4_ = bf16[3,512,1408]{2,1,0:T(8,128)(2,1)S(1)} custom-call(bf16[8,3,512]{2,1,0:T(4,128)(2,1)S(1)} %pad_maximum_fusion.strain_ref), custom_call_target="tpu_custom_call" | custom-call | flops 1 | bytes 1 | tf_op jit(solution)/shard_map/hankel/pallas_call | solution.py:81
  32.7 0.0 collective-permute-done.5.refs_0_
  32.7 1.3 %series.4 = (bf16[2,3,64,128]{3,2,1,0:T(8,128)(2,1)S(1)}, bf16[2,3,64,128]{3,2,1,0:T(8,128)(2,1)S(1)}) custom-call(f32[256,2048]{1,0:T(8,128)S(1)} %get-tuple-element.39.own_ref, bf16[64,2048]{1,0:T(8,128)(2,1)S(1)} %collective-permute-done.5.refs_0_, bf16[3,512,1408]{2,1,0:T(8,128)(2,1)S(1)} %hankel.1.refs_1_.refs_2_.refs_4_), custom_call_target="tpu_custom_call" | custom-call | flops 1 | bytes 1 | tf_op jit(solution)/shard_map/series/pallas_call | solution.py:251
  34.0 2.7 %collective-permute-start.11 = (bf16[2,3,64,128]{3,2,1,0:T(8,128)(2,1)S(1)}, bf16[2,3,64,128]{3,2,1,0:T(8,128)(2,1)S(1)}, u32[]{:S(2)}, u32[]{:S(2)}) collective-permute-start(bf16[2,3,64,128]{3,2,1,0:T(8,128)(2,1)S(1)} %get-tuple-element.49), channel_id=1, source_target_pairs={{0,4},{1,5},{2,6},{3,7},{4,0},{5,1},{6,2},{7,3},{8,12},{9,13},{10,... | collective-permute-start | bytes 294920 | tf_op jit(solution)/shard_map/ppermute | solution.py:19
  36.6 1.6 %collective-permute-start.8 = (bf16[2,3,64,128]{3,2,1,0:T(8,128)(2,1)S(1)}, bf16[2,3,64,128]{3,2,1,0:T(8,128)(2,1)S(1)}, u32[]{:S(2)}, u32[]{:S(2)}) collective-permute-start(bf16[2,3,64,128]{3,2,1,0:T(8,128)(2,1)S(1)} %get-tuple-element.47), channel_id=1, source_target_pairs={{0,6},{1,7},{2,4},{3,5},{4,2},{5,3},{6,0},{7,1},{8,14},{9,15},{10,... | collective-permute-start | bytes 294920 | tf_op jit(solution)/shard_map/ppermute | solution.py:19
  38.2 1.6 %partial_rows.6 = bf16[64,2048]{1,0:T(8,128)(2,1)S(1)} custom-call(bf16[64,2048]{1,0:T(8,128)(2,1)S(1)} %collective-permute-done.7.rows_ref, bf16[2048,2048]{1,0:T(8,128)(2,1)S(1)} %get-tuple-element.42.filters_ref), custom_call_target="tpu_custom_call" | custom-call | flops 1 | bytes 1 | tf_op jit(solution)/shard_map/partial_rows/pallas_call | solution.py:204
  39.8 0.7 collective-permute-start.13
  40.5 0.0 collective-permute-done.14.rows_ref
  40.5 1.2 %collective-permute-done.11.refs_0_.refs_2_ = bf16[2,3,64,128]{3,2,1,0:T(8,128)(2,1)S(1)} collective-permute-done((bf16[2,3,64,128]{3,2,1,0:T(8,128)(2,1)S(1)}, bf16[2,3,64,128]{3,2,1,0:T(8,128)(2,1)S(1)}, u32[]{:S(2)}, u32[]{:S(2)}) %collective-permute-start.11) | collective-permute-done | bytes 98336 | tf_op jit(solution)/shard_map/ppermute | solution.py:19
  41.7 1.5 %collective-permute-done.8.refs_2_.refs_0_ = bf16[2,3,64,128]{3,2,1,0:T(8,128)(2,1)S(1)} collective-permute-done((bf16[2,3,64,128]{3,2,1,0:T(8,128)(2,1)S(1)}, bf16[2,3,64,128]{3,2,1,0:T(8,128)(2,1)S(1)}, u32[]{:S(2)}, u32[]{:S(2)}) %collective-permute-start.8) | collective-permute-done | bytes 98336 | tf_op jit(solution)/shard_map/ppermute | solution.py:19
  43.2 1.6 %partial_rows.7 = bf16[64,2048]{1,0:T(8,128)(2,1)S(1)} custom-call(bf16[64,2048]{1,0:T(8,128)(2,1)S(1)} %collective-permute-done.14.rows_ref, bf16[2048,2048]{1,0:T(8,128)(2,1)S(1)} %get-tuple-element.42.filters_ref), custom_call_target="tpu_custom_call" | custom-call | flops 1 | bytes 1 | tf_op jit(solution)/shard_map/partial_rows/pallas_call | solution.py:204
  44.7 0.7 collective-permute-start.15
  45.4 0.0 collective-permute-done.9.refs_0_.refs_1_
  45.4 1.3 %series.5 = (bf16[2,3,64,128]{3,2,1,0:T(8,128)(2,1)S(1)}, bf16[2,3,64,128]{3,2,1,0:T(8,128)(2,1)S(1)}) custom-call(f32[256,2048]{1,0:T(8,128)S(1)} %get-tuple-element.39.own_ref, bf16[64,2048]{1,0:T(8,128)(2,1)S(1)} %collective-permute-done.9.refs_0_.refs_1_, bf16[3,512,1408]{2,1,0:T(8,128)(2,1)S(1)} %hankel.1.refs_1_.refs_2_.refs_4_), custom_call_target="tpu_custom_call" | custom-call | flops 1 | bytes 1 | tf_op jit(solution)/shard_map/series/pallas_call | solution.py:251
  46.7 2.8 %collective-permute-start.10 = (bf16[2,3,64,128]{3,2,1,0:T(8,128)(2,1)S(1)}, bf16[2,3,64,128]{3,2,1,0:T(8,128)(2,1)S(1)}, u32[]{:S(2)}, u32[]{:S(2)}) collective-permute-start(bf16[2,3,64,128]{3,2,1,0:T(8,128)(2,1)S(1)} %get-tuple-element.48), channel_id=1, source_target_pairs={{0,6},{1,7},{2,4},{3,5},{4,2},{5,3},{6,0},{7,1},{8,14},{9,15},{10,... | collective-permute-start | bytes 294920 | tf_op jit(solution)/shard_map/ppermute | solution.py:19
  49.4 0.2 collective-permute-start.12
  49.7 0.0 collective-permute-done.13.refs_0_.refs_2_
  49.7 3.6 %collective-permute-done.10.refs_3_.refs_1_ = bf16[2,3,64,128]{3,2,1,0:T(8,128)(2,1)S(1)} collective-permute-done((bf16[2,3,64,128]{3,2,1,0:T(8,128)(2,1)S(1)}, bf16[2,3,64,128]{3,2,1,0:T(8,128)(2,1)S(1)}, u32[]{:S(2)}, u32[]{:S(2)}) %collective-permute-start.10) | collective-permute-done | bytes 98336 | tf_op jit(solution)/shard_map/ppermute | solution.py:19
  53.3 0.0 collective-permute-done.15.refs_1_.refs_3_
  53.3 1.2 %series.6 = (bf16[1,3,128,128]{3,2,1,0:T(8,128)(2,1)S(1)}, bf16[1,3,128,128]{3,2,1,0:T(8,128)(2,1)S(1)}, bf16[1,3,128,128]{3,2,1,0:T(8,128)(2,1)S(1)}, bf16[1,3,128,128]{3,2,1,0:T(8,128)(2,1)S(1)}) custom-call(f32[256,2048]{1,0:T(8,128)S(1)} %get-tuple-element.39.own_ref, bf16[64,2048]{1,0:T(8,128)(2,1)S(1)} %collective-permute-done.13.refs_0_.refs_2_, ...), custom_call_target="tpu_custom_call" | custom-call | flops 1 | bytes 1 | tf_op jit(solution)/shard_map/series/pallas_call | solution.py:251
  54.5 3.1 %collective-permute-start.17 = (bf16[1,3,128,128]{3,2,1,0:T(8,128)(2,1)S(1)}, bf16[1,3,128,128]{3,2,1,0:T(8,128)(2,1)S(1)}, u32[]{:S(2)}, u32[]{:S(2)}) collective-permute-start(bf16[1,3,128,128]{3,2,1,0:T(8,128)(2,1)S(1)} %get-tuple-element.56), channel_id=1, source_target_pairs={{0,7},{1,6},{2,5},{3,4},{4,3},{5,2},{6,1},{7,0},{8,15},{9,14},{10,... | collective-permute-start | bytes 294920 | tf_op jit(solution)/shard_map/ppermute | solution.py:19
  57.5 1.7 %collective-permute-start.16 = (bf16[1,3,128,128]{3,2,1,0:T(8,128)(2,1)S(1)}, bf16[1,3,128,128]{3,2,1,0:T(8,128)(2,1)S(1)}, u32[]{:S(2)}, u32[]{:S(2)}) collective-permute-start(bf16[1,3,128,128]{3,2,1,0:T(8,128)(2,1)S(1)} %get-tuple-element.55), channel_id=1, source_target_pairs={{0,6},{1,7},{2,4},{3,5},{4,2},{5,3},{6,0},{7,1},{8,14},{9,15},{10,... | collective-permute-start | bytes 294920 | tf_op jit(solution)/shard_map/ppermute | solution.py:19
  59.2 2.0 %series.7 = (bf16[1,3,256,128]{3,2,1,0:T(8,128)(2,1)S(1)}, bf16[1,3,256,128]{3,2,1,0:T(8,128)(2,1)S(1)}, bf16[1,3,256,128]{3,2,1,0:T(8,128)(2,1)S(1)}, bf16[1,3,256,128]{3,2,1,0:T(8,128)(2,1)S(1)}) custom-call(f32[256,2048]{1,0:T(8,128)S(1)} %get-tuple-element.39.own_ref, bf16[64,2048]{1,0:T(8,128)(2,1)S(1)} %collective-permute-done.5.refs_0_, ...), custom_call_target="tpu_custom_call" | custom-call | flops 1 | bytes 1 | tf_op jit(solution)/shard_map/series/pallas_call | solution.py:251
  61.2 0.0 collective-permute-done.12.refs_1_.refs_3_
  61.3 0.7 collective-permute-start.20
  62.0 0.8 %collective-permute-start.21 = (bf16[1,3,256,128]{3,2,1,0:T(8,128)(2,1)S(1)}, bf16[1,3,256,128]{3,2,1,0:T(8,128)(2,1)S(1)}, u32[]{:S(2)}, u32[]{:S(2)}) collective-permute-start(bf16[1,3,256,128]{3,2,1,0:T(8,128)(2,1)S(1)} %get-tuple-element.62), channel_id=1, source_target_pairs={{0,2},{1,3},{2,0},{3,1},{4,6},{5,7},{6,4},{7,5},{8,10},{9,11},{10,... | collective-permute-start | bytes 589832 | tf_op jit(solution)/shard_map/ppermute | solution.py:19
  62.8 2.4 %collective-permute-start.18 = (bf16[1,3,128,128]{3,2,1,0:T(8,128)(2,1)S(1)}, bf16[1,3,128,128]{3,2,1,0:T(8,128)(2,1)S(1)}, u32[]{:S(2)}, u32[]{:S(2)}) collective-permute-start(bf16[1,3,128,128]{3,2,1,0:T(8,128)(2,1)S(1)} %get-tuple-element.57), channel_id=1, source_target_pairs={{0,4},{1,5},{2,6},{3,7},{4,0},{5,1},{6,2},{7,3},{8,12},{9,13},{10,... | collective-permute-start | bytes 294920 | tf_op jit(solution)/shard_map/ppermute | solution.py:19
  65.2 0.0 collective-permute-done.17.refs_5_
  65.2 0.9 %collective-permute-start.23 = (bf16[1,3,256,128]{3,2,1,0:T(8,128)(2,1)S(1)}, bf16[1,3,256,128]{3,2,1,0:T(8,128)(2,1)S(1)}, u32[]{:S(2)}, u32[]{:S(2)}) collective-permute-start(bf16[1,3,256,128]{3,2,1,0:T(8,128)(2,1)S(1)} %get-tuple-element.66), channel_id=1, source_target_pairs={{0,1},{1,0},{2,3},{3,2},{4,5},{5,4},{6,7},{7,6},{8,9},{9,8},{10,11... | collective-permute-start | bytes 589832 | tf_op jit(solution)/shard_map/ppermute | solution.py:19
  66.1 0.0 collective-permute-done.16.refs_4_
  66.1 1.0 %collective-permute-start.22 = (bf16[1,3,256,128]{3,2,1,0:T(8,128)(2,1)S(1)}, bf16[1,3,256,128]{3,2,1,0:T(8,128)(2,1)S(1)}, u32[]{:S(2)}, u32[]{:S(2)}) collective-permute-start(bf16[1,3,256,128]{3,2,1,0:T(8,128)(2,1)S(1)} %get-tuple-element.64), channel_id=1, source_target_pairs={{0,3},{1,2},{2,1},{3,0},{4,7},{5,6},{6,5},{7,4},{8,11},{9,10},{10,... | collective-permute-start | bytes 589832 | tf_op jit(solution)/shard_map/ppermute | solution.py:19
  67.1 2.7 %collective-permute-done.18.refs_6_ = bf16[1,3,128,128]{3,2,1,0:T(8,128)(2,1)S(1)} collective-permute-done((bf16[1,3,128,128]{3,2,1,0:T(8,128)(2,1)S(1)}, bf16[1,3,128,128]{3,2,1,0:T(8,128)(2,1)S(1)}, u32[]{:S(2)}, u32[]{:S(2)}) %collective-permute-start.18) | collective-permute-done | bytes 98336 | tf_op jit(solution)/shard_map/ppermute | solution.py:19
  69.9 3.8 %collective-permute-start.19 = (bf16[1,3,128,128]{3,2,1,0:T(8,128)(2,1)S(1)}, bf16[1,3,128,128]{3,2,1,0:T(8,128)(2,1)S(1)}, u32[]{:S(2)}, u32[]{:S(2)}) collective-permute-start(bf16[1,3,128,128]{3,2,1,0:T(8,128)(2,1)S(1)} %get-tuple-element.58), channel_id=1, source_target_pairs={{0,5},{1,4},{2,7},{3,6},{4,1},{5,0},{6,3},{7,2},{8,13},{9,12},{10,... | collective-permute-start | bytes 294920 | tf_op jit(solution)/shard_map/ppermute | solution.py:19
  73.7 2.7 %collective-permute-done.19.refs_7_ = bf16[1,3,128,128]{3,2,1,0:T(8,128)(2,1)S(1)} collective-permute-done((bf16[1,3,128,128]{3,2,1,0:T(8,128)(2,1)S(1)}, bf16[1,3,128,128]{3,2,1,0:T(8,128)(2,1)S(1)}, u32[]{:S(2)}, u32[]{:S(2)}) %collective-permute-start.19) | collective-permute-done | bytes 98336 | tf_op jit(solution)/shard_map/ppermute | solution.py:19
  76.3 0.0 collective-permute-done.20.refs_8_
  76.3 0.0 collective-permute-done.21.refs_9_
  76.3 0.7 collective-permute-done.23.refs_11_
  77.0 0.0 collective-permute-done.22.refs_10_
  77.0 1.2 %assembled.1 = bf16[3,2048,128]{2,1,0:T(8,128)(2,1)} custom-call(bf16[2,3,64,128]{3,2,1,0:T(8,128)(2,1)S(1)} %collective-permute-done.8.refs_2_.refs_0_, bf16[2,3,64,128]{3,2,1,0:T(8,128)(2,1)S(1)} %collective-permute-done.10.refs_3_.refs_1_, bf16[2,3,64,128]{3,2,1,0:T(8,128)(2,1)S(1)} %collective-permute-done.11.refs_0_.refs_2_, ...), custom_call_target="tpu_custom_call" | custom-call | flops 1 | bytes 1 | tf_op jit(solution)/shard_map/assembled/pallas_call | solution.py:310
  (4 shorter events, 0.1 us)
Async XLA Ops:
  0.0 9.5 %collective-permute-start.1 = (bf16[1024,2048]{1,0:T(8,128)(2,1)}, bf16[1024,2048]{1,0:T(8,128)(2,1)}, u32[]{:S(2)}, u32[]{:S(2)}) collective-permute-start(bf16[1024,2048]{1,0:T(8,128)(2,1)} %near_ref.1), channel_id=1, source_target_pairs={{0,8},{8,0},{16,24},{24,16},{1,9},{9,1},{17,25},{25,17},{2,10},{10... | collective-permute-start | bytes 12582920 | tf_op jit(solution)/shard_map/ppermute | solution.py:19
  1.4 4.4 %collective-permute-start = (bf16[1,3,512]{2,1,0:T(4,128)(2,1)}, bf16[1,3,512]{2,1,0:T(4,128)(2,1)S(1)}, u32[]{:S(2)}, u32[]{:S(2)}) collective-permute-start(bf16[1,3,512]{2,1,0:T(4,128)(2,1)} %bitcast.2), channel_id=1, source_target_pairs={{0,1},{1,0},{2,3},{3,2},{4,5},{5,4},{6,7},{7,6},{8,9},{9,8},{10,11... | collective-permute-start | bytes 9224 | tf_op jit(solution)/shard_map/ppermute | solution.py:19
  4.0 14.1 %collective-permute-start.2 = (bf16[64,2048]{1,0:T(8,128)(2,1)S(1)}, bf16[64,2048]{1,0:T(8,128)(2,1)S(1)}, u32[]{:S(2)}, u32[]{:S(2)}) collective-permute-start(bf16[64,2048]{1,0:T(8,128)(2,1)S(1)} %constant_dynamic-slice_fusion.3), channel_id=1, source_target_pairs={{0,16},{8,24},{16,0},{24,8},{1,17},{9,25},{17,1},{25,9},{2,18},{10... | collective-permute-start | bytes 786440 | tf_op jit(solution)/shard_map/ppermute | solution.py:19
  7.5 10.6 %collective-permute-start.3 = (bf16[64,2048]{1,0:T(8,128)(2,1)S(1)}, bf16[64,2048]{1,0:T(8,128)(2,1)S(1)}, u32[]{:S(2)}, u32[]{:S(2)}) collective-permute-start(bf16[64,2048]{1,0:T(8,128)(2,1)S(1)} %constant_dynamic-slice_fusion.2), channel_id=1, source_target_pairs={{0,16},{8,24},{16,0},{24,8},{1,17},{9,25},{17,1},{25,9},{2,18},{10... | collective-permute-start | bytes 786440 | tf_op jit(solution)/shard_map/ppermute | solution.py:19
  14.4 3.7 %collective-permute-start.4 = (bf16[2,3,512]{2,1,0:T(4,128)(2,1)S(1)}, bf16[2,3,512]{2,1,0:T(4,128)(2,1)S(1)}, u32[]{:S(2)}, u32[]{:S(2)}) collective-permute-start(bf16[2,3,512]{2,1,0:T(4,128)(2,1)S(1)} %pad_maximum_fusion.1), channel_id=1, source_target_pairs={{0,2},{1,3},{2,0},{3,1},{4,6},{5,7},{6,4},{7,5},{8,10},{9,11},{10,... | collective-permute-start | bytes 18440 | tf_op jit(solution)/shard_map/ppermute | solution.py:19
  17.0 10.5 %collective-permute-start.7 = (bf16[64,2048]{1,0:T(8,128)(2,1)S(1)}, bf16[64,2048]{1,0:T(8,128)(2,1)S(1)}, u32[]{:S(2)}, u32[]{:S(2)}) collective-permute-start(bf16[64,2048]{1,0:T(8,128)(2,1)S(1)} %constant_dynamic-slice_fusion.1), channel_id=1, source_target_pairs={{0,16},{8,24},{16,0},{24,8},{1,17},{9,25},{17,1},{25,9},{2,18},{10... | collective-permute-start | bytes 786440 | tf_op jit(solution)/shard_map/ppermute | solution.py:19
  19.7 13.0 %collective-permute-start.5 = (bf16[64,2048]{1,0:T(8,128)(2,1)S(1)}, bf16[64,2048]{1,0:T(8,128)(2,1)S(1)}, u32[]{:S(2)}, u32[]{:S(2)}) collective-permute-start(bf16[64,2048]{1,0:T(8,128)(2,1)S(1)} %partial_rows.4), channel_id=1, source_target_pairs={{0,16},{8,24},{16,0},{24,8},{1,17},{9,25},{17,1},{25,9},{2,18},{10... | collective-permute-start | bytes 786440 | tf_op jit(solution)/shard_map/ppermute | solution.py:19
  22.2 18.3 %collective-permute-start.14 = (bf16[64,2048]{1,0:T(8,128)(2,1)S(1)}, bf16[64,2048]{1,0:T(8,128)(2,1)S(1)}, u32[]{:S(2)}, u32[]{:S(2)}) collective-permute-start(bf16[64,2048]{1,0:T(8,128)(2,1)S(1)} %constant_dynamic-slice_fusion), channel_id=1, source_target_pairs={{0,16},{8,24},{16,0},{24,8},{1,17},{9,25},{17,1},{25,9},{2,18},{10... | collective-permute-start | bytes 786440 | tf_op jit(solution)/shard_map/ppermute | solution.py:19
  22.8 4.6 %collective-permute-start.6 = (bf16[4,3,512]{2,1,0:T(4,128)(2,1)S(1)}, bf16[4,3,512]{2,1,0:T(4,128)(2,1)S(1)}, u32[]{:S(2)}, u32[]{:S(2)}) collective-permute-start(bf16[4,3,512]{2,1,0:T(4,128)(2,1)S(1)} %constant_dynamic-update-slice_fusion), channel_id=1, source_target_pairs={{0,4},{1,5},{2,6},{3,7},{4,0},{5,1},{6,2},{7,3},{8,12},{9,13},{10,... | collective-permute-start | bytes 36872 | tf_op jit(solution)/shard_map/ppermute | solution.py:19
  29.1 16.3 %collective-permute-start.9 = (bf16[64,2048]{1,0:T(8,128)(2,1)S(1)}, bf16[64,2048]{1,0:T(8,128)(2,1)S(1)}, u32[]{:S(2)}, u32[]{:S(2)}) collective-permute-start(bf16[64,2048]{1,0:T(8,128)(2,1)S(1)} %partial_rows.5), channel_id=1, source_target_pairs={{0,16},{8,24},{16,0},{24,8},{1,17},{9,25},{17,1},{25,9},{2,18},{10... | collective-permute-start | bytes 786440 | tf_op jit(solution)/shard_map/ppermute | solution.py:19
  34.0 7.7 %collective-permute-start.11 = (bf16[2,3,64,128]{3,2,1,0:T(8,128)(2,1)S(1)}, bf16[2,3,64,128]{3,2,1,0:T(8,128)(2,1)S(1)}, u32[]{:S(2)}, u32[]{:S(2)}) collective-permute-start(bf16[2,3,64,128]{3,2,1,0:T(8,128)(2,1)S(1)} %get-tuple-element.49), channel_id=1, source_target_pairs={{0,4},{1,5},{2,6},{3,7},{4,0},{5,1},{6,2},{7,3},{8,12},{9,13},{10,... | collective-permute-start | bytes 294920 | tf_op jit(solution)/shard_map/ppermute | solution.py:19
  36.6 6.5 %collective-permute-start.8 = (bf16[2,3,64,128]{3,2,1,0:T(8,128)(2,1)S(1)}, bf16[2,3,64,128]{3,2,1,0:T(8,128)(2,1)S(1)}, u32[]{:S(2)}, u32[]{:S(2)}) collective-permute-start(bf16[2,3,64,128]{3,2,1,0:T(8,128)(2,1)S(1)} %get-tuple-element.47), channel_id=1, source_target_pairs={{0,6},{1,7},{2,4},{3,5},{4,2},{5,3},{6,0},{7,1},{8,14},{9,15},{10,... | collective-permute-start | bytes 294920 | tf_op jit(solution)/shard_map/ppermute | solution.py:19
  39.8 9.9 %collective-permute-start.13 = (bf16[64,2048]{1,0:T(8,128)(2,1)S(1)}, bf16[64,2048]{1,0:T(8,128)(2,1)S(1)}, u32[]{:S(2)}, u32[]{:S(2)}) collective-permute-start(bf16[64,2048]{1,0:T(8,128)(2,1)S(1)} %partial_rows.6), channel_id=1, source_target_pairs={{0,16},{8,24},{16,0},{24,8},{1,17},{9,25},{17,1},{25,9},{2,18},{10... | collective-permute-start | bytes 786440 | tf_op jit(solution)/shard_map/ppermute | solution.py:19
  44.7 8.5 %collective-permute-start.15 = (bf16[64,2048]{1,0:T(8,128)(2,1)S(1)}, bf16[64,2048]{1,0:T(8,128)(2,1)S(1)}, u32[]{:S(2)}, u32[]{:S(2)}) collective-permute-start(bf16[64,2048]{1,0:T(8,128)(2,1)S(1)} %partial_rows.7), channel_id=1, source_target_pairs={{0,16},{8,24},{16,0},{24,8},{1,17},{9,25},{17,1},{25,9},{2,18},{10... | collective-permute-start | bytes 786440 | tf_op jit(solution)/shard_map/ppermute | solution.py:19
  46.7 6.6 %collective-permute-start.10 = (bf16[2,3,64,128]{3,2,1,0:T(8,128)(2,1)S(1)}, bf16[2,3,64,128]{3,2,1,0:T(8,128)(2,1)S(1)}, u32[]{:S(2)}, u32[]{:S(2)}) collective-permute-start(bf16[2,3,64,128]{3,2,1,0:T(8,128)(2,1)S(1)} %get-tuple-element.48), channel_id=1, source_target_pairs={{0,6},{1,7},{2,4},{3,5},{4,2},{5,3},{6,0},{7,1},{8,14},{9,15},{10,... | collective-permute-start | bytes 294920 | tf_op jit(solution)/shard_map/ppermute | solution.py:19
  49.4 11.8 %collective-permute-start.12 = (bf16[2,3,64,128]{3,2,1,0:T(8,128)(2,1)S(1)}, bf16[2,3,64,128]{3,2,1,0:T(8,128)(2,1)S(1)}, u32[]{:S(2)}, u32[]{:S(2)}) collective-permute-start(bf16[2,3,64,128]{3,2,1,0:T(8,128)(2,1)S(1)} %get-tuple-element.50), channel_id=1, source_target_pairs={{0,4},{1,5},{2,6},{3,7},{4,0},{5,1},{6,2},{7,3},{8,12},{9,13},{10,... | collective-permute-start | bytes 294920 | tf_op jit(solution)/shard_map/ppermute | solution.py:19
  54.5 10.8 %collective-permute-start.17 = (bf16[1,3,128,128]{3,2,1,0:T(8,128)(2,1)S(1)}, bf16[1,3,128,128]{3,2,1,0:T(8,128)(2,1)S(1)}, u32[]{:S(2)}, u32[]{:S(2)}) collective-permute-start(bf16[1,3,128,128]{3,2,1,0:T(8,128)(2,1)S(1)} %get-tuple-element.56), channel_id=1, source_target_pairs={{0,7},{1,6},{2,5},{3,4},{4,3},{5,2},{6,1},{7,0},{8,15},{9,14},{10,... | collective-permute-start | bytes 294920 | tf_op jit(solution)/shard_map/ppermute | solution.py:19
  57.5 8.6 %collective-permute-start.16 = (bf16[1,3,128,128]{3,2,1,0:T(8,128)(2,1)S(1)}, bf16[1,3,128,128]{3,2,1,0:T(8,128)(2,1)S(1)}, u32[]{:S(2)}, u32[]{:S(2)}) collective-permute-start(bf16[1,3,128,128]{3,2,1,0:T(8,128)(2,1)S(1)} %get-tuple-element.55), channel_id=1, source_target_pairs={{0,6},{1,7},{2,4},{3,5},{4,2},{5,3},{6,0},{7,1},{8,14},{9,15},{10,... | collective-permute-start | bytes 294920 | tf_op jit(solution)/shard_map/ppermute | solution.py:19
  61.3 15.1 %collective-permute-start.20 = (bf16[2,3,128,128]{3,2,1,0:T(8,128)(2,1)S(1)}, bf16[2,3,128,128]{3,2,1,0:T(8,128)(2,1)S(1)}, u32[]{:S(2)}, u32[]{:S(2)}) collective-permute-start(bf16[2,3,128,128]{3,2,1,0:T(8,128)(2,1)S(1)} %second_halves.1), channel_id=1, source_target_pairs={{0,1},{1,0},{2,3},{3,2},{4,5},{5,4},{6,7},{7,6},{8,9},{9,8},{10,11... | collective-permute-start | bytes 589832 | tf_op jit(solution)/shard_map/ppermute | solution.py:19
  62.0 14.4 %collective-permute-start.21 = (bf16[1,3,256,128]{3,2,1,0:T(8,128)(2,1)S(1)}, bf16[1,3,256,128]{3,2,1,0:T(8,128)(2,1)S(1)}, u32[]{:S(2)}, u32[]{:S(2)}) collective-permute-start(bf16[1,3,256,128]{3,2,1,0:T(8,128)(2,1)S(1)} %get-tuple-element.62), channel_id=1, source_target_pairs={{0,2},{1,3},{2,0},{3,1},{4,6},{5,7},{6,4},{7,5},{8,10},{9,11},{10,... | collective-permute-start | bytes 589832 | tf_op jit(solution)/shard_map/ppermute | solution.py:19
  62.8 7.1 %collective-permute-start.18 = (bf16[1,3,128,128]{3,2,1,0:T(8,128)(2,1)S(1)}, bf16[1,3,128,128]{3,2,1,0:T(8,128)(2,1)S(1)}, u32[]{:S(2)}, u32[]{:S(2)}) collective-permute-start(bf16[1,3,128,128]{3,2,1,0:T(8,128)(2,1)S(1)} %get-tuple-element.57), channel_id=1, source_target_pairs={{0,4},{1,5},{2,6},{3,7},{4,0},{5,1},{6,2},{7,3},{8,12},{9,13},{10,... | collective-permute-start | bytes 294920 | tf_op jit(solution)/shard_map/ppermute | solution.py:19
  65.2 11.8 %collective-permute-start.23 = (bf16[1,3,256,128]{3,2,1,0:T(8,128)(2,1)S(1)}, bf16[1,3,256,128]{3,2,1,0:T(8,128)(2,1)S(1)}, u32[]{:S(2)}, u32[]{:S(2)}) collective-permute-start(bf16[1,3,256,128]{3,2,1,0:T(8,128)(2,1)S(1)} %get-tuple-element.66), channel_id=1, source_target_pairs={{0,1},{1,0},{2,3},{3,2},{4,5},{5,4},{6,7},{7,6},{8,9},{9,8},{10,11... | collective-permute-start | bytes 589832 | tf_op jit(solution)/shard_map/ppermute | solution.py:19
  66.1 10.9 %collective-permute-start.22 = (bf16[1,3,256,128]{3,2,1,0:T(8,128)(2,1)S(1)}, bf16[1,3,256,128]{3,2,1,0:T(8,128)(2,1)S(1)}, u32[]{:S(2)}, u32[]{:S(2)}) collective-permute-start(bf16[1,3,256,128]{3,2,1,0:T(8,128)(2,1)S(1)} %get-tuple-element.64), channel_id=1, source_target_pairs={{0,3},{1,2},{2,1},{3,0},{4,7},{5,6},{6,5},{7,4},{8,11},{9,10},{10,... | collective-permute-start | bytes 589832 | tf_op jit(solution)/shard_map/ppermute | solution.py:19
  69.9 6.5 %collective-permute-start.19 = (bf16[1,3,128,128]{3,2,1,0:T(8,128)(2,1)S(1)}, bf16[1,3,128,128]{3,2,1,0:T(8,128)(2,1)S(1)}, u32[]{:S(2)}, u32[]{:S(2)}) collective-permute-start(bf16[1,3,128,128]{3,2,1,0:T(8,128)(2,1)S(1)} %get-tuple-element.58), channel_id=1, source_target_pairs={{0,5},{1,4},{2,7},{3,6},{4,1},{5,0},{6,3},{7,2},{8,13},{9,12},{10,... | collective-permute-start | bytes 294920 | tf_op jit(solution)/shard_map/ppermute | solution.py:19

commit v4 on v3

--- a/solution.py
+++ b/solution.py
@@ -44,9 +44,9 @@
 
 
 def hankel_kernel(strain_ref, out_ref, split_ref, tile_ref):
-    count, detectors, samples = strain_ref.shape
+    count, _, samples = strain_ref.shape
     here = samples // STRIDE
-    width = out_ref.shape[2]
+    detectors, _, width = out_ref.shape
     me = lax.axis_index("tm")
     sample = lax.broadcasted_iota(jnp.int32, (samples, samples), 0)
     column = lax.broadcasted_iota(jnp.int32, (samples, samples), 1)
@@ -76,6 +76,7 @@
 
 def hankel(blocks, taps):
     count, detectors, samples = blocks.shape
+    filled = jnp.pad(blocks, ((0, 0), (0, 16 - detectors), (0, 0)))
     width = count * samples // STRIDE + (taps - DEPTH) // STRIDE
     length = -(-(width + DEPTH // STRIDE) // LANES) * LANES
     return pl.pallas_call(
@@ -84,13 +85,13 @@
         out_specs=pl.BlockSpec(memory_space=pltpu.VMEM),
         out_shape=jax.ShapeDtypeStruct((detectors, DEPTH, width), jnp.bfloat16),
         scratch_shapes=[
-            pltpu.VMEM((count, detectors, samples), jnp.float32),
+            pltpu.VMEM(filled.shape, jnp.float32),
             pltpu.VMEM((detectors, 2 * STRIDE, length), jnp.float32),
         ],
         cost_estimate=COST,
         compiler_params=pltpu.CompilerParams(vmem_limit_bytes=16 * MIB),
         name="hankel",
-    )(in_vmem(blocks))
+    )(in_vmem(filled))
 
 
 def long_hankel_kernel(rows_ref, out_ref):

time: 78.5 us -> 78.5 us (level)
  no operation moved by 1% of the time
where the time goes in v4:
time: 78.5 us; the launch traced here: 78.2 us
  starting transfers between devices  38.4 us (49%)
  Pallas kernels  20.2 us (26%)
  waiting for transfers between devices  14.8 us (19%)
  local copies, waits for them, and re-layouts  3.91 us (5%)
    ppermute x24, starting transfers between devices, flipped(): lax.ppermute(block, axis, [(i, i ^ mask) for i in range(lax.axis_size(axi...  38.4 us
    ppermute x24, waiting for transfers between devices, flipped(): lax.ppermute(block, axis, [(i, i ^ mask) for i in range(lax.axis_size(axi...  14.8 us
    pallas_call x4, Pallas kernels, partial_rows(): pl.pallas_call(partial_kernel, in_specs=whole_in_vmem(2), out_specs=pl.Bl...  6.25 us
    pallas_call x4, Pallas kernels, series(): pl.pallas_call(functools.partial(series_kernel, start, len(others), far,...  5.78 us
    pallas_call x1, Pallas kernels, staged(): pl.pallas_call(staging_kernel, in_specs=[pl.BlockSpec(memory_space=pl.ANY...  4.83 us
    dynamic_slice x4, local copies, waits for them, and re-layouts, theirs(): return lax.dynamic_slice(source, (start, at), (rows, 2 * filters))  3.88 us
    pallas_call x1, Pallas kernels, hankel(): pl.pallas_call(hankel_kernel, in_specs=whole_in_vmem(1), out_specs=pl.Blo...  2.1 us
  transfers between devices with their start and end apart: 24, of which 9 were waited for; matrix products, arithmetic and copies ran while one was open for 6% of the time, Pallas kernels for 24%

profile of v4, /device:TPU:0, one launch (start us, length us, event | category | flops | bytes accessed | tf_op | source)
XLA Modules:
  0.0 78.2 jit_solution(1170224839530635713)
XLA Ops:
  0.0 0.5 collective-permute-start.1
  0.5 1.0 %constant_dynamic-slice_fusion.3 = bf16[64,2048]{1,0:T(8,128)(2,1)S(1)} fusion(bf16[256,4096]{1,0:T(8,128)(2,1)} %coefficients_ref, s32[]{:T(128)S(6)} %select_n.15), kind=kLoop, calls=%fused_computation.7 | loop fusion | bytes 524292 | tf_op jit(solution)/shard_map/dynamic_slice | solution.py:370
  1.4 2.6 %collective-permute-start = (bf16[1,3,512]{2,1,0:T(4,128)(2,1)}, bf16[1,3,512]{2,1,0:T(4,128)(2,1)S(1)}, u32[]{:S(2)}, u32[]{:S(2)}) collective-permute-start(bf16[1,3,512]{2,1,0:T(4,128)(2,1)} %bitcast.2), channel_id=1, source_target_pairs={{0,1},{1,0},{2,3},{3,2},{4,5},{5,4},{6,7},{7,6},{8,9},{9,8},{10,11... | collective-permute-start | bytes 9224 | tf_op jit(solution)/shard_map/ppermute | solution.py:19
  4.0 1.5 %collective-permute-start.2 = (bf16[64,2048]{1,0:T(8,128)(2,1)S(1)}, bf16[64,2048]{1,0:T(8,128)(2,1)S(1)}, u32[]{:S(2)}, u32[]{:S(2)}) collective-permute-start(bf16[64,2048]{1,0:T(8,128)(2,1)S(1)} %constant_dynamic-slice_fusion.3), channel_id=1, source_target_pairs={{0,16},{8,24},{16,0},{24,8},{1,17},{9,25},{17,1},{25,9},{2,18},{10... | collective-permute-start | bytes 786440 | tf_op jit(solution)/shard_map/ppermute | solution.py:19
  5.5 0.3 collective-permute-done
  5.8 0.7 pad_maximum_fusion.1
  6.5 1.0 %constant_dynamic-slice_fusion.2 = bf16[64,2048]{1,0:T(8,128)(2,1)S(1)} fusion(bf16[256,4096]{1,0:T(8,128)(2,1)} %coefficients_ref, s32[]{:T(128)S(6)} %select_n.15), kind=kLoop, calls=%fused_computation.6 | loop fusion | bytes 524292 | tf_op jit(solution)/shard_map/dynamic_slice | solution.py:370
  7.5 2.1 %collective-permute-start.3 = (bf16[64,2048]{1,0:T(8,128)(2,1)S(1)}, bf16[64,2048]{1,0:T(8,128)(2,1)S(1)}, u32[]{:S(2)}, u32[]{:S(2)}) collective-permute-start(bf16[64,2048]{1,0:T(8,128)(2,1)S(1)} %constant_dynamic-slice_fusion.2), channel_id=1, source_target_pairs={{0,16},{8,24},{16,0},{24,8},{1,17},{9,25},{17,1},{25,9},{2,18},{10... | collective-permute-start | bytes 786440 | tf_op jit(solution)/shard_map/ppermute | solution.py:19
  9.5 0.0 collective-permute-done.1.far_ref
  9.5 4.8 %staged.1 = (bf16[2048,2048]{1,0:T(8,128)(2,1)S(1)}, f32[256,2048]{1,0:T(8,128)S(1)}) custom-call(bf16[256,4096]{1,0:T(8,128)(2,1)} %coefficients_ref, bf16[1024,2048]{1,0:T(8,128)(2,1)} %near_ref.1, bf16[1024,2048]{1,0:T(8,128)(2,1)} %collective-permute-done.1.far_ref), custom_call_target="tpu_custom_call" | custom-call | flops 1 | bytes 1 | tf_op jit(solution)/shard_map/staged/pallas_call | solution.py:172
  14.4 1.6 %collective-permute-start.4 = (bf16[2,3,512]{2,1,0:T(4,128)(2,1)S(1)}, bf16[2,3,512]{2,1,0:T(4,128)(2,1)S(1)}, u32[]{:S(2)}, u32[]{:S(2)}) collective-permute-start(bf16[2,3,512]{2,1,0:T(4,128)(2,1)S(1)} %pad_maximum_fusion.1), channel_id=1, source_target_pairs={{0,2},{1,3},{2,0},{3,1},{4,6},{5,7},{6,4},{7,5},{8,10},{9,11},{10,... | collective-permute-start | bytes 18440 | tf_op jit(solution)/shard_map/ppermute | solution.py:19
  16.0 1.0 %constant_dynamic-slice_fusion.1 = bf16[64,2048]{1,0:T(8,128)(2,1)S(1)} fusion(bf16[256,4096]{1,0:T(8,128)(2,1)} %coefficients_ref, s32[]{:T(128)S(6)} %select_n.15), kind=kLoop, calls=%fused_computation.5 | loop fusion | bytes 524292 | tf_op jit(solution)/shard_map/dynamic_slice | solution.py:370
  17.0 0.9 %collective-permute-start.7 = (bf16[64,2048]{1,0:T(8,128)(2,1)S(1)}, bf16[64,2048]{1,0:T(8,128)(2,1)S(1)}, u32[]{:S(2)}, u32[]{:S(2)}) collective-permute-start(bf16[64,2048]{1,0:T(8,128)(2,1)S(1)} %constant_dynamic-slice_fusion.1), channel_id=1, source_target_pairs={{0,16},{8,24},{16,0},{24,8},{1,17},{9,25},{17,1},{25,9},{2,18},{10... | collective-permute-start | bytes 786440 | tf_op jit(solution)/shard_map/ppermute | solution.py:19
  17.9 0.2 collective-permute-done.4
  18.1 0.0 collective-permute-done.2.rows_ref
  18.1 0.0 collective-permute-done.3.rows_ref
  18.1 1.6 %partial_rows.4 = bf16[64,2048]{1,0:T(8,128)(2,1)S(1)} custom-call(bf16[64,2048]{1,0:T(8,128)(2,1)S(1)} %collective-permute-done.2.rows_ref, bf16[2048,2048]{1,0:T(8,128)(2,1)S(1)} %get-tuple-element.42.filters_ref), custom_call_target="tpu_custom_call" | custom-call | flops 1 | bytes 1 | tf_op jit(solution)/shard_map/partial_rows/pallas_call | solution.py:205
  19.7 1.5 %collective-permute-start.5 = (bf16[64,2048]{1,0:T(8,128)(2,1)S(1)}, bf16[64,2048]{1,0:T(8,128)(2,1)S(1)}, u32[]{:S(2)}, u32[]{:S(2)}) collective-permute-start(bf16[64,2048]{1,0:T(8,128)(2,1)S(1)} %partial_rows.4), channel_id=1, source_target_pairs={{0,16},{8,24},{16,0},{24,8},{1,17},{9,25},{17,1},{25,9},{2,18},{10... | collective-permute-start | bytes 786440 | tf_op jit(solution)/shard_map/ppermute | solution.py:19
  21.2 1.0 %constant_dynamic-slice_fusion = bf16[64,2048]{1,0:T(8,128)(2,1)S(1)} fusion(bf16[256,4096]{1,0:T(8,128)(2,1)} %coefficients_ref, s32[]{:T(128)S(6)} %select_n.15), kind=kLoop, calls=%fused_computation.4 | loop fusion | bytes 524292 | tf_op jit(solution)/shard_map/dynamic_slice | solution.py:370
  22.2 0.7 collective-permute-start.14
  22.8 2.6 %collective-permute-start.6 = (bf16[4,3,512]{2,1,0:T(4,128)(2,1)S(1)}, bf16[4,3,512]{2,1,0:T(4,128)(2,1)S(1)}, u32[]{:S(2)}, u32[]{:S(2)}) collective-permute-start(bf16[4,3,512]{2,1,0:T(4,128)(2,1)S(1)} %constant_dynamic-update-slice_fusion), channel_id=1, source_target_pairs={{0,4},{1,5},{2,6},{3,7},{4,0},{5,1},{6,2},{7,3},{8,12},{9,13},{10,... | collective-permute-start | bytes 36872 | tf_op jit(solution)/shard_map/ppermute | solution.py:19
  25.4 2.1 %collective-permute-done.6 = bf16[4,3,512]{2,1,0:T(4,128)(2,1)S(1)} collective-permute-done((bf16[4,3,512]{2,1,0:T(4,128)(2,1)S(1)}, bf16[4,3,512]{2,1,0:T(4,128)(2,1)S(1)}, u32[]{:S(2)}, u32[]{:S(2)}) %collective-permute-start.6) | collective-permute-done | bytes 12320 | tf_op jit(solution)/shard_map/ppermute | solution.py:19
  27.5 0.0 collective-permute-done.7.rows_ref
  27.5 1.6 %partial_rows.5 = bf16[64,2048]{1,0:T(8,128)(2,1)S(1)} custom-call(bf16[64,2048]{1,0:T(8,128)(2,1)S(1)} %collective-permute-done.3.rows_ref, bf16[2048,2048]{1,0:T(8,128)(2,1)S(1)} %get-tuple-element.42.filters_ref), custom_call_target="tpu_custom_call" | custom-call | flops 1 | bytes 1 | tf_op jit(solution)/shard_map/partial_rows/pallas_call | solution.py:205
  29.1 1.5 %collective-permute-start.9 = (bf16[64,2048]{1,0:T(8,128)(2,1)S(1)}, bf16[64,2048]{1,0:T(8,128)(2,1)S(1)}, u32[]{:S(2)}, u32[]{:S(2)}) collective-permute-start(bf16[64,2048]{1,0:T(8,128)(2,1)S(1)} %partial_rows.5), channel_id=1, source_target_pairs={{0,16},{8,24},{16,0},{24,8},{1,17},{9,25},{17,1},{25,9},{2,18},{10... | collective-permute-start | bytes 786440 | tf_op jit(solution)/shard_map/ppermute | solution.py:19
  30.6 2.1 %hankel.1.refs_1_.refs_2_.refs_4_ = bf16[3,512,1408]{2,1,0:T(8,128)(2,1)S(1)} custom-call(bf16[8,16,512]{2,1,0:T(8,128)(2,1)S(1)} %pad.4.strain_ref), custom_call_target="tpu_custom_call" | custom-call | flops 1 | bytes 1 | tf_op jit(solution)/shard_map/hankel/pallas_call | solution.py:82
  32.7 0.0 collective-permute-done.5.refs_0_
  32.7 1.3 %series.4 = (bf16[2,3,64,128]{3,2,1,0:T(8,128)(2,1)S(1)}, bf16[2,3,64,128]{3,2,1,0:T(8,128)(2,1)S(1)}) custom-call(f32[256,2048]{1,0:T(8,128)S(1)} %get-tuple-element.39.own_ref, bf16[64,2048]{1,0:T(8,128)(2,1)S(1)} %collective-permute-done.5.refs_0_, bf16[3,512,1408]{2,1,0:T(8,128)(2,1)S(1)} %hankel.1.refs_1_.refs_2_.refs_4_), custom_call_target="tpu_custom_call" | custom-call | flops 1 | bytes 1 | tf_op jit(solution)/shard_map/series/pallas_call | solution.py:252
  34.0 2.7 %collective-permute-start.11 = (bf16[2,3,64,128]{3,2,1,0:T(8,128)(2,1)S(1)}, bf16[2,3,64,128]{3,2,1,0:T(8,128)(2,1)S(1)}, u32[]{:S(2)}, u32[]{:S(2)}) collective-permute-start(bf16[2,3,64,128]{3,2,1,0:T(8,128)(2,1)S(1)} %get-tuple-element.49), channel_id=1, source_target_pairs={{0,4},{1,5},{2,6},{3,7},{4,0},{5,1},{6,2},{7,3},{8,12},{9,13},{10,... | collective-permute-start | bytes 294920 | tf_op jit(solution)/shard_map/ppermute | solution.py:19
  36.7 1.6 %collective-permute-start.8 = (bf16[2,3,64,128]{3,2,1,0:T(8,128)(2,1)S(1)}, bf16[2,3,64,128]{3,2,1,0:T(8,128)(2,1)S(1)}, u32[]{:S(2)}, u32[]{:S(2)}) collective-permute-start(bf16[2,3,64,128]{3,2,1,0:T(8,128)(2,1)S(1)} %get-tuple-element.47), channel_id=1, source_target_pairs={{0,6},{1,7},{2,4},{3,5},{4,2},{5,3},{6,0},{7,1},{8,14},{9,15},{10,... | collective-permute-start | bytes 294920 | tf_op jit(solution)/shard_map/ppermute | solution.py:19
  38.2 1.6 %partial_rows.6 = bf16[64,2048]{1,0:T(8,128)(2,1)S(1)} custom-call(bf16[64,2048]{1,0:T(8,128)(2,1)S(1)} %collective-permute-done.7.rows_ref, bf16[2048,2048]{1,0:T(8,128)(2,1)S(1)} %get-tuple-element.42.filters_ref), custom_call_target="tpu_custom_call" | custom-call | flops 1 | bytes 1 | tf_op jit(solution)/shard_map/partial_rows/pallas_call | solution.py:205
  39.8 0.7 collective-permute-start.13
  40.5 0.0 collective-permute-done.14.rows_ref
  40.5 1.2 %collective-permute-done.11.refs_0_.refs_2_ = bf16[2,3,64,128]{3,2,1,0:T(8,128)(2,1)S(1)} collective-permute-done((bf16[2,3,64,128]{3,2,1,0:T(8,128)(2,1)S(1)}, bf16[2,3,64,128]{3,2,1,0:T(8,128)(2,1)S(1)}, u32[]{:S(2)}, u32[]{:S(2)}) %collective-permute-start.11) | collective-permute-done | bytes 98336 | tf_op jit(solution)/shard_map/ppermute | solution.py:19
  41.7 1.5 %collective-permute-done.8.refs_2_.refs_0_ = bf16[2,3,64,128]{3,2,1,0:T(8,128)(2,1)S(1)} collective-permute-done((bf16[2,3,64,128]{3,2,1,0:T(8,128)(2,1)S(1)}, bf16[2,3,64,128]{3,2,1,0:T(8,128)(2,1)S(1)}, u32[]{:S(2)}, u32[]{:S(2)}) %collective-permute-start.8) | collective-permute-done | bytes 98336 | tf_op jit(solution)/shard_map/ppermute | solution.py:19
  43.2 1.6 %partial_rows.7 = bf16[64,2048]{1,0:T(8,128)(2,1)S(1)} custom-call(bf16[64,2048]{1,0:T(8,128)(2,1)S(1)} %collective-permute-done.14.rows_ref, bf16[2048,2048]{1,0:T(8,128)(2,1)S(1)} %get-tuple-element.42.filters_ref), custom_call_target="tpu_custom_call" | custom-call | flops 1 | bytes 1 | tf_op jit(solution)/shard_map/partial_rows/pallas_call | solution.py:205
  44.7 0.7 collective-permute-start.15
  45.4 0.0 collective-permute-done.9.refs_0_.refs_1_
  45.4 1.3 %series.5 = (bf16[2,3,64,128]{3,2,1,0:T(8,128)(2,1)S(1)}, bf16[2,3,64,128]{3,2,1,0:T(8,128)(2,1)S(1)}) custom-call(f32[256,2048]{1,0:T(8,128)S(1)} %get-tuple-element.39.own_ref, bf16[64,2048]{1,0:T(8,128)(2,1)S(1)} %collective-permute-done.9.refs_0_.refs_1_, bf16[3,512,1408]{2,1,0:T(8,128)(2,1)S(1)} %hankel.1.refs_1_.refs_2_.refs_4_), custom_call_target="tpu_custom_call" | custom-call | flops 1 | bytes 1 | tf_op jit(solution)/shard_map/series/pallas_call | solution.py:252
  46.7 2.8 %collective-permute-start.10 = (bf16[2,3,64,128]{3,2,1,0:T(8,128)(2,1)S(1)}, bf16[2,3,64,128]{3,2,1,0:T(8,128)(2,1)S(1)}, u32[]{:S(2)}, u32[]{:S(2)}) collective-permute-start(bf16[2,3,64,128]{3,2,1,0:T(8,128)(2,1)S(1)} %get-tuple-element.48), channel_id=1, source_target_pairs={{0,6},{1,7},{2,4},{3,5},{4,2},{5,3},{6,0},{7,1},{8,14},{9,15},{10,... | collective-permute-start | bytes 294920 | tf_op jit(solution)/shard_map/ppermute | solution.py:19
  49.4 0.2 collective-permute-start.12
  49.7 0.0 collective-permute-done.13.refs_0_.refs_2_
  49.7 3.6 %collective-permute-done.10.refs_3_.refs_1_ = bf16[2,3,64,128]{3,2,1,0:T(8,128)(2,1)S(1)} collective-permute-done((bf16[2,3,64,128]{3,2,1,0:T(8,128)(2,1)S(1)}, bf16[2,3,64,128]{3,2,1,0:T(8,128)(2,1)S(1)}, u32[]{:S(2)}, u32[]{:S(2)}) %collective-permute-start.10) | collective-permute-done | bytes 98336 | tf_op jit(solution)/shard_map/ppermute | solution.py:19
  53.3 0.0 collective-permute-done.15.refs_1_.refs_3_
  53.3 1.2 %series.6 = (bf16[1,3,128,128]{3,2,1,0:T(8,128)(2,1)S(1)}, bf16[1,3,128,128]{3,2,1,0:T(8,128)(2,1)S(1)}, bf16[1,3,128,128]{3,2,1,0:T(8,128)(2,1)S(1)}, bf16[1,3,128,128]{3,2,1,0:T(8,128)(2,1)S(1)}) custom-call(f32[256,2048]{1,0:T(8,128)S(1)} %get-tuple-element.39.own_ref, bf16[64,2048]{1,0:T(8,128)(2,1)S(1)} %collective-permute-done.13.refs_0_.refs_2_, ...), custom_call_target="tpu_custom_call" | custom-call | flops 1 | bytes 1 | tf_op jit(solution)/shard_map/series/pallas_call | solution.py:252
  54.5 3.0 %collective-permute-start.17 = (bf16[1,3,128,128]{3,2,1,0:T(8,128)(2,1)S(1)}, bf16[1,3,128,128]{3,2,1,0:T(8,128)(2,1)S(1)}, u32[]{:S(2)}, u32[]{:S(2)}) collective-permute-start(bf16[1,3,128,128]{3,2,1,0:T(8,128)(2,1)S(1)} %get-tuple-element.56), channel_id=1, source_target_pairs={{0,7},{1,6},{2,5},{3,4},{4,3},{5,2},{6,1},{7,0},{8,15},{9,14},{10,... | collective-permute-start | bytes 294920 | tf_op jit(solution)/shard_map/ppermute | solution.py:19
  57.5 1.7 %collective-permute-start.16 = (bf16[1,3,128,128]{3,2,1,0:T(8,128)(2,1)S(1)}, bf16[1,3,128,128]{3,2,1,0:T(8,128)(2,1)S(1)}, u32[]{:S(2)}, u32[]{:S(2)}) collective-permute-start(bf16[1,3,128,128]{3,2,1,0:T(8,128)(2,1)S(1)} %get-tuple-element.55), channel_id=1, source_target_pairs={{0,6},{1,7},{2,4},{3,5},{4,2},{5,3},{6,0},{7,1},{8,14},{9,15},{10,... | collective-permute-start | bytes 294920 | tf_op jit(solution)/shard_map/ppermute | solution.py:19
  59.2 2.0 %series.7 = (bf16[1,3,256,128]{3,2,1,0:T(8,128)(2,1)S(1)}, bf16[1,3,256,128]{3,2,1,0:T(8,128)(2,1)S(1)}, bf16[1,3,256,128]{3,2,1,0:T(8,128)(2,1)S(1)}, bf16[1,3,256,128]{3,2,1,0:T(8,128)(2,1)S(1)}) custom-call(f32[256,2048]{1,0:T(8,128)S(1)} %get-tuple-element.39.own_ref, bf16[64,2048]{1,0:T(8,128)(2,1)S(1)} %collective-permute-done.5.refs_0_, ...), custom_call_target="tpu_custom_call" | custom-call | flops 1 | bytes 1 | tf_op jit(solution)/shard_map/series/pallas_call | solution.py:252
  61.3 0.0 collective-permute-done.12.refs_1_.refs_3_
  61.3 0.7 collective-permute-start.20
  62.0 0.8 %collective-permute-start.21 = (bf16[1,3,256,128]{3,2,1,0:T(8,128)(2,1)S(1)}, bf16[1,3,256,128]{3,2,1,0:T(8,128)(2,1)S(1)}, u32[]{:S(2)}, u32[]{:S(2)}) collective-permute-start(bf16[1,3,256,128]{3,2,1,0:T(8,128)(2,1)S(1)} %get-tuple-element.62), channel_id=1, source_target_pairs={{0,2},{1,3},{2,0},{3,1},{4,6},{5,7},{6,4},{7,5},{8,10},{9,11},{10,... | collective-permute-start | bytes 589832 | tf_op jit(solution)/shard_map/ppermute | solution.py:19
  62.8 2.5 %collective-permute-start.18 = (bf16[1,3,128,128]{3,2,1,0:T(8,128)(2,1)S(1)}, bf16[1,3,128,128]{3,2,1,0:T(8,128)(2,1)S(1)}, u32[]{:S(2)}, u32[]{:S(2)}) collective-permute-start(bf16[1,3,128,128]{3,2,1,0:T(8,128)(2,1)S(1)} %get-tuple-element.57), channel_id=1, source_target_pairs={{0,4},{1,5},{2,6},{3,7},{4,0},{5,1},{6,2},{7,3},{8,12},{9,13},{10,... | collective-permute-start | bytes 294920 | tf_op jit(solution)/shard_map/ppermute | solution.py:19
  65.2 0.0 collective-permute-done.17.refs_5_
  65.2 0.9 %collective-permute-start.23 = (bf16[1,3,256,128]{3,2,1,0:T(8,128)(2,1)S(1)}, bf16[1,3,256,128]{3,2,1,0:T(8,128)(2,1)S(1)}, u32[]{:S(2)}, u32[]{:S(2)}) collective-permute-start(bf16[1,3,256,128]{3,2,1,0:T(8,128)(2,1)S(1)} %get-tuple-element.66), channel_id=1, source_target_pairs={{0,1},{1,0},{2,3},{3,2},{4,5},{5,4},{6,7},{7,6},{8,9},{9,8},{10,11... | collective-permute-start | bytes 589832 | tf_op jit(solution)/shard_map/ppermute | solution.py:19
  66.1 0.0 collective-permute-done.16.refs_4_
  66.1 1.0 %collective-permute-start.22 = (bf16[1,3,256,128]{3,2,1,0:T(8,128)(2,1)S(1)}, bf16[1,3,256,128]{3,2,1,0:T(8,128)(2,1)S(1)}, u32[]{:S(2)}, u32[]{:S(2)}) collective-permute-start(bf16[1,3,256,128]{3,2,1,0:T(8,128)(2,1)S(1)} %get-tuple-element.64), channel_id=1, source_target_pairs={{0,3},{1,2},{2,1},{3,0},{4,7},{5,6},{6,5},{7,4},{8,11},{9,10},{10,... | collective-permute-start | bytes 589832 | tf_op jit(solution)/shard_map/ppermute | solution.py:19
  67.2 2.7 %collective-permute-done.18.refs_6_ = bf16[1,3,128,128]{3,2,1,0:T(8,128)(2,1)S(1)} collective-permute-done((bf16[1,3,128,128]{3,2,1,0:T(8,128)(2,1)S(1)}, bf16[1,3,128,128]{3,2,1,0:T(8,128)(2,1)S(1)}, u32[]{:S(2)}, u32[]{:S(2)}) %collective-permute-start.18) | collective-permute-done | bytes 98336 | tf_op jit(solution)/shard_map/ppermute | solution.py:19
  69.9 3.9 %collective-permute-start.19 = (bf16[1,3,128,128]{3,2,1,0:T(8,128)(2,1)S(1)}, bf16[1,3,128,128]{3,2,1,0:T(8,128)(2,1)S(1)}, u32[]{:S(2)}, u32[]{:S(2)}) collective-permute-start(bf16[1,3,128,128]{3,2,1,0:T(8,128)(2,1)S(1)} %get-tuple-element.58), channel_id=1, source_target_pairs={{0,5},{1,4},{2,7},{3,6},{4,1},{5,0},{6,3},{7,2},{8,13},{9,12},{10,... | collective-permute-start | bytes 294920 | tf_op jit(solution)/shard_map/ppermute | solution.py:19
  73.7 2.6 %collective-permute-done.19.refs_7_ = bf16[1,3,128,128]{3,2,1,0:T(8,128)(2,1)S(1)} collective-permute-done((bf16[1,3,128,128]{3,2,1,0:T(8,128)(2,1)S(1)}, bf16[1,3,128,128]{3,2,1,0:T(8,128)(2,1)S(1)}, u32[]{:S(2)}, u32[]{:S(2)}) %collective-permute-start.19) | collective-permute-done | bytes 98336 | tf_op jit(solution)/shard_map/ppermute | solution.py:19
  76.4 0.0 collective-permute-done.20.refs_8_
  76.4 0.0 collective-permute-done.21.refs_9_
  76.4 0.6 collective-permute-done.23.refs_11_
  77.0 0.0 collective-permute-done.22.refs_10_
  77.0 1.2 %assembled.1 = bf16[3,2048,128]{2,1,0:T(8,128)(2,1)} custom-call(bf16[2,3,64,128]{3,2,1,0:T(8,128)(2,1)S(1)} %collective-permute-done.8.refs_2_.refs_0_, bf16[2,3,64,128]{3,2,1,0:T(8,128)(2,1)S(1)} %collective-permute-done.10.refs_3_.refs_1_, bf16[2,3,64,128]{3,2,1,0:T(8,128)(2,1)S(1)} %collective-permute-done.11.refs_0_.refs_2_, ...), custom_call_target="tpu_custom_call" | custom-call | flops 1 | bytes 1 | tf_op jit(solution)/shard_map/assembled/pallas_call | solution.py:311
  (5 shorter events, 0.1 us)
Async XLA Ops:
  0.0 9.5 %collective-permute-start.1 = (bf16[1024,2048]{1,0:T(8,128)(2,1)}, bf16[1024,2048]{1,0:T(8,128)(2,1)}, u32[]{:S(2)}, u32[]{:S(2)}) collective-permute-start(bf16[1024,2048]{1,0:T(8,128)(2,1)} %near_ref.1), channel_id=1, source_target_pairs={{0,8},{8,0},{16,24},{24,16},{1,9},{9,1},{17,25},{25,17},{2,10},{10... | collective-permute-start | bytes 12582920 | tf_op jit(solution)/shard_map/ppermute | solution.py:19
  1.4 4.4 %collective-permute-start = (bf16[1,3,512]{2,1,0:T(4,128)(2,1)}, bf16[1,3,512]{2,1,0:T(4,128)(2,1)S(1)}, u32[]{:S(2)}, u32[]{:S(2)}) collective-permute-start(bf16[1,3,512]{2,1,0:T(4,128)(2,1)} %bitcast.2), channel_id=1, source_target_pairs={{0,1},{1,0},{2,3},{3,2},{4,5},{5,4},{6,7},{7,6},{8,9},{9,8},{10,11... | collective-permute-start | bytes 9224 | tf_op jit(solution)/shard_map/ppermute | solution.py:19
  4.0 14.1 %collective-permute-start.2 = (bf16[64,2048]{1,0:T(8,128)(2,1)S(1)}, bf16[64,2048]{1,0:T(8,128)(2,1)S(1)}, u32[]{:S(2)}, u32[]{:S(2)}) collective-permute-start(bf16[64,2048]{1,0:T(8,128)(2,1)S(1)} %constant_dynamic-slice_fusion.3), channel_id=1, source_target_pairs={{0,16},{8,24},{16,0},{24,8},{1,17},{9,25},{17,1},{25,9},{2,18},{10... | collective-permute-start | bytes 786440 | tf_op jit(solution)/shard_map/ppermute | solution.py:19
  7.5 10.6 %collective-permute-start.3 = (bf16[64,2048]{1,0:T(8,128)(2,1)S(1)}, bf16[64,2048]{1,0:T(8,128)(2,1)S(1)}, u32[]{:S(2)}, u32[]{:S(2)}) collective-permute-start(bf16[64,2048]{1,0:T(8,128)(2,1)S(1)} %constant_dynamic-slice_fusion.2), channel_id=1, source_target_pairs={{0,16},{8,24},{16,0},{24,8},{1,17},{9,25},{17,1},{25,9},{2,18},{10... | collective-permute-start | bytes 786440 | tf_op jit(solution)/shard_map/ppermute | solution.py:19
  14.4 3.7 %collective-permute-start.4 = (bf16[2,3,512]{2,1,0:T(4,128)(2,1)S(1)}, bf16[2,3,512]{2,1,0:T(4,128)(2,1)S(1)}, u32[]{:S(2)}, u32[]{:S(2)}) collective-permute-start(bf16[2,3,512]{2,1,0:T(4,128)(2,1)S(1)} %pad_maximum_fusion.1), channel_id=1, source_target_pairs={{0,2},{1,3},{2,0},{3,1},{4,6},{5,7},{6,4},{7,5},{8,10},{9,11},{10,... | collective-permute-start | bytes 18440 | tf_op jit(solution)/shard_map/ppermute | solution.py:19
  17.0 10.5 %collective-permute-start.7 = (bf16[64,2048]{1,0:T(8,128)(2,1)S(1)}, bf16[64,2048]{1,0:T(8,128)(2,1)S(1)}, u32[]{:S(2)}, u32[]{:S(2)}) collective-permute-start(bf16[64,2048]{1,0:T(8,128)(2,1)S(1)} %constant_dynamic-slice_fusion.1), channel_id=1, source_target_pairs={{0,16},{8,24},{16,0},{24,8},{1,17},{9,25},{17,1},{25,9},{2,18},{10... | collective-permute-start | bytes 786440 | tf_op jit(solution)/shard_map/ppermute | solution.py:19
  19.7 13.0 %collective-permute-start.5 = (bf16[64,2048]{1,0:T(8,128)(2,1)S(1)}, bf16[64,2048]{1,0:T(8,128)(2,1)S(1)}, u32[]{:S(2)}, u32[]{:S(2)}) collective-permute-start(bf16[64,2048]{1,0:T(8,128)(2,1)S(1)} %partial_rows.4), channel_id=1, source_target_pairs={{0,16},{8,24},{16,0},{24,8},{1,17},{9,25},{17,1},{25,9},{2,18},{10... | collective-permute-start | bytes 786440 | tf_op jit(solution)/shard_map/ppermute | solution.py:19
  22.2 18.4 %collective-permute-start.14 = (bf16[64,2048]{1,0:T(8,128)(2,1)S(1)}, bf16[64,2048]{1,0:T(8,128)(2,1)S(1)}, u32[]{:S(2)}, u32[]{:S(2)}) collective-permute-start(bf16[64,2048]{1,0:T(8,128)(2,1)S(1)} %constant_dynamic-slice_fusion), channel_id=1, source_target_pairs={{0,16},{8,24},{16,0},{24,8},{1,17},{9,25},{17,1},{25,9},{2,18},{10... | collective-permute-start | bytes 786440 | tf_op jit(solution)/shard_map/ppermute | solution.py:19
  22.8 4.6 %collective-permute-start.6 = (bf16[4,3,512]{2,1,0:T(4,128)(2,1)S(1)}, bf16[4,3,512]{2,1,0:T(4,128)(2,1)S(1)}, u32[]{:S(2)}, u32[]{:S(2)}) collective-permute-start(bf16[4,3,512]{2,1,0:T(4,128)(2,1)S(1)} %constant_dynamic-update-slice_fusion), channel_id=1, source_target_pairs={{0,4},{1,5},{2,6},{3,7},{4,0},{5,1},{6,2},{7,3},{8,12},{9,13},{10,... | collective-permute-start | bytes 36872 | tf_op jit(solution)/shard_map/ppermute | solution.py:19
  29.1 16.3 %collective-permute-start.9 = (bf16[64,2048]{1,0:T(8,128)(2,1)S(1)}, bf16[64,2048]{1,0:T(8,128)(2,1)S(1)}, u32[]{:S(2)}, u32[]{:S(2)}) collective-permute-start(bf16[64,2048]{1,0:T(8,128)(2,1)S(1)} %partial_rows.5), channel_id=1, source_target_pairs={{0,16},{8,24},{16,0},{24,8},{1,17},{9,25},{17,1},{25,9},{2,18},{10... | collective-permute-start | bytes 786440 | tf_op jit(solution)/shard_map/ppermute | solution.py:19
  34.0 7.7 %collective-permute-start.11 = (bf16[2,3,64,128]{3,2,1,0:T(8,128)(2,1)S(1)}, bf16[2,3,64,128]{3,2,1,0:T(8,128)(2,1)S(1)}, u32[]{:S(2)}, u32[]{:S(2)}) collective-permute-start(bf16[2,3,64,128]{3,2,1,0:T(8,128)(2,1)S(1)} %get-tuple-element.49), channel_id=1, source_target_pairs={{0,4},{1,5},{2,6},{3,7},{4,0},{5,1},{6,2},{7,3},{8,12},{9,13},{10,... | collective-permute-start | bytes 294920 | tf_op jit(solution)/shard_map/ppermute | solution.py:19
  36.7 6.5 %collective-permute-start.8 = (bf16[2,3,64,128]{3,2,1,0:T(8,128)(2,1)S(1)}, bf16[2,3,64,128]{3,2,1,0:T(8,128)(2,1)S(1)}, u32[]{:S(2)}, u32[]{:S(2)}) collective-permute-start(bf16[2,3,64,128]{3,2,1,0:T(8,128)(2,1)S(1)} %get-tuple-element.47), channel_id=1, source_target_pairs={{0,6},{1,7},{2,4},{3,5},{4,2},{5,3},{6,0},{7,1},{8,14},{9,15},{10,... | collective-permute-start | bytes 294920 | tf_op jit(solution)/shard_map/ppermute | solution.py:19
  39.8 9.9 %collective-permute-start.13 = (bf16[64,2048]{1,0:T(8,128)(2,1)S(1)}, bf16[64,2048]{1,0:T(8,128)(2,1)S(1)}, u32[]{:S(2)}, u32[]{:S(2)}) collective-permute-start(bf16[64,2048]{1,0:T(8,128)(2,1)S(1)} %partial_rows.6), channel_id=1, source_target_pairs={{0,16},{8,24},{16,0},{24,8},{1,17},{9,25},{17,1},{25,9},{2,18},{10... | collective-permute-start | bytes 786440 | tf_op jit(solution)/shard_map/ppermute | solution.py:19
  44.7 8.5 %collective-permute-start.15 = (bf16[64,2048]{1,0:T(8,128)(2,1)S(1)}, bf16[64,2048]{1,0:T(8,128)(2,1)S(1)}, u32[]{:S(2)}, u32[]{:S(2)}) collective-permute-start(bf16[64,2048]{1,0:T(8,128)(2,1)S(1)} %partial_rows.7), channel_id=1, source_target_pairs={{0,16},{8,24},{16,0},{24,8},{1,17},{9,25},{17,1},{25,9},{2,18},{10... | collective-permute-start | bytes 786440 | tf_op jit(solution)/shard_map/ppermute | solution.py:19
  46.7 6.6 %collective-permute-start.10 = (bf16[2,3,64,128]{3,2,1,0:T(8,128)(2,1)S(1)}, bf16[2,3,64,128]{3,2,1,0:T(8,128)(2,1)S(1)}, u32[]{:S(2)}, u32[]{:S(2)}) collective-permute-start(bf16[2,3,64,128]{3,2,1,0:T(8,128)(2,1)S(1)} %get-tuple-element.48), channel_id=1, source_target_pairs={{0,6},{1,7},{2,4},{3,5},{4,2},{5,3},{6,0},{7,1},{8,14},{9,15},{10,... | collective-permute-start | bytes 294920 | tf_op jit(solution)/shard_map/ppermute | solution.py:19
  49.4 11.8 %collective-permute-start.12 = (bf16[2,3,64,128]{3,2,1,0:T(8,128)(2,1)S(1)}, bf16[2,3,64,128]{3,2,1,0:T(8,128)(2,1)S(1)}, u32[]{:S(2)}, u32[]{:S(2)}) collective-permute-start(bf16[2,3,64,128]{3,2,1,0:T(8,128)(2,1)S(1)} %get-tuple-element.50), channel_id=1, source_target_pairs={{0,4},{1,5},{2,6},{3,7},{4,0},{5,1},{6,2},{7,3},{8,12},{9,13},{10,... | collective-permute-start | bytes 294920 | tf_op jit(solution)/shard_map/ppermute | solution.py:19
  54.5 10.8 %collective-permute-start.17 = (bf16[1,3,128,128]{3,2,1,0:T(8,128)(2,1)S(1)}, bf16[1,3,128,128]{3,2,1,0:T(8,128)(2,1)S(1)}, u32[]{:S(2)}, u32[]{:S(2)}) collective-permute-start(bf16[1,3,128,128]{3,2,1,0:T(8,128)(2,1)S(1)} %get-tuple-element.56), channel_id=1, source_target_pairs={{0,7},{1,6},{2,5},{3,4},{4,3},{5,2},{6,1},{7,0},{8,15},{9,14},{10,... | collective-permute-start | bytes 294920 | tf_op jit(solution)/shard_map/ppermute | solution.py:19
  57.5 8.6 %collective-permute-start.16 = (bf16[1,3,128,128]{3,2,1,0:T(8,128)(2,1)S(1)}, bf16[1,3,128,128]{3,2,1,0:T(8,128)(2,1)S(1)}, u32[]{:S(2)}, u32[]{:S(2)}) collective-permute-start(bf16[1,3,128,128]{3,2,1,0:T(8,128)(2,1)S(1)} %get-tuple-element.55), channel_id=1, source_target_pairs={{0,6},{1,7},{2,4},{3,5},{4,2},{5,3},{6,0},{7,1},{8,14},{9,15},{10,... | collective-permute-start | bytes 294920 | tf_op jit(solution)/shard_map/ppermute | solution.py:19
  61.3 15.1 %collective-permute-start.20 = (bf16[2,3,128,128]{3,2,1,0:T(8,128)(2,1)S(1)}, bf16[2,3,128,128]{3,2,1,0:T(8,128)(2,1)S(1)}, u32[]{:S(2)}, u32[]{:S(2)}) collective-permute-start(bf16[2,3,128,128]{3,2,1,0:T(8,128)(2,1)S(1)} %second_halves.1), channel_id=1, source_target_pairs={{0,1},{1,0},{2,3},{3,2},{4,5},{5,4},{6,7},{7,6},{8,9},{9,8},{10,11... | collective-permute-start | bytes 589832 | tf_op jit(solution)/shard_map/ppermute | solution.py:19
  62.0 14.4 %collective-permute-start.21 = (bf16[1,3,256,128]{3,2,1,0:T(8,128)(2,1)S(1)}, bf16[1,3,256,128]{3,2,1,0:T(8,128)(2,1)S(1)}, u32[]{:S(2)}, u32[]{:S(2)}) collective-permute-start(bf16[1,3,256,128]{3,2,1,0:T(8,128)(2,1)S(1)} %get-tuple-element.62), channel_id=1, source_target_pairs={{0,2},{1,3},{2,0},{3,1},{4,6},{5,7},{6,4},{7,5},{8,10},{9,11},{10,... | collective-permute-start | bytes 589832 | tf_op jit(solution)/shard_map/ppermute | solution.py:19
  62.8 7.1 %collective-permute-start.18 = (bf16[1,3,128,128]{3,2,1,0:T(8,128)(2,1)S(1)}, bf16[1,3,128,128]{3,2,1,0:T(8,128)(2,1)S(1)}, u32[]{:S(2)}, u32[]{:S(2)}) collective-permute-start(bf16[1,3,128,128]{3,2,1,0:T(8,128)(2,1)S(1)} %get-tuple-element.57), channel_id=1, source_target_pairs={{0,4},{1,5},{2,6},{3,7},{4,0},{5,1},{6,2},{7,3},{8,12},{9,13},{10,... | collective-permute-start | bytes 294920 | tf_op jit(solution)/shard_map/ppermute | solution.py:19
  65.2 11.7 %collective-permute-start.23 = (bf16[1,3,256,128]{3,2,1,0:T(8,128)(2,1)S(1)}, bf16[1,3,256,128]{3,2,1,0:T(8,128)(2,1)S(1)}, u32[]{:S(2)}, u32[]{:S(2)}) collective-permute-start(bf16[1,3,256,128]{3,2,1,0:T(8,128)(2,1)S(1)} %get-tuple-element.66), channel_id=1, source_target_pairs={{0,1},{1,0},{2,3},{3,2},{4,5},{5,4},{6,7},{7,6},{8,9},{9,8},{10,11... | collective-permute-start | bytes 589832 | tf_op jit(solution)/shard_map/ppermute | solution.py:19
  66.1 10.9 %collective-permute-start.22 = (bf16[1,3,256,128]{3,2,1,0:T(8,128)(2,1)S(1)}, bf16[1,3,256,128]{3,2,1,0:T(8,128)(2,1)S(1)}, u32[]{:S(2)}, u32[]{:S(2)}) collective-permute-start(bf16[1,3,256,128]{3,2,1,0:T(8,128)(2,1)S(1)} %get-tuple-element.64), channel_id=1, source_target_pairs={{0,3},{1,2},{2,1},{3,0},{4,7},{5,6},{6,5},{7,4},{8,11},{9,10},{10,... | collective-permute-start | bytes 589832 | tf_op jit(solution)/shard_map/ppermute | solution.py:19
  69.9 6.5 %collective-permute-start.19 = (bf16[1,3,128,128]{3,2,1,0:T(8,128)(2,1)S(1)}, bf16[1,3,128,128]{3,2,1,0:T(8,128)(2,1)S(1)}, u32[]{:S(2)}, u32[]{:S(2)}) collective-permute-start(bf16[1,3,128,128]{3,2,1,0:T(8,128)(2,1)S(1)} %get-tuple-element.58), channel_id=1, source_target_pairs={{0,5},{1,4},{2,7},{3,6},{4,1},{5,0},{6,3},{7,2},{8,13},{9,12},{10,... | collective-permute-start | bytes 294920 | tf_op jit(solution)/shard_map/ppermute | solution.py:19
